TPU v7x, 512 devices: a whole 4x8x8 slice. The times are simulated.
512 devices in a mesh: ep: 32 (over x, y), dp: 16 (over z, core).
Axes of the slice: x: 4, y: 8, z: 8, core: 2. Of those that a mesh axis runs over, the one named last changes fastest.
Arguments:
- tokens: bfloat16 [4096, 7168], P('ep', 'dp'), may hold values from -6 to 6
- routes: int32 [4096, 8], P('ep'), may hold values from 0 to 31, all different within a row; in each aligned block of 128 rows (0 to 127, 128 to 255, ...) at most 64 rows name the same one
- weights_int: int32 [4096, 8], P('ep'), may hold values from 1 to 63
- capacity: int32 [32], replicated, may hold values from 12 to 24, as said below
- spill_size: int32 [32], replicated, may hold values from 1 to 24, as said below
- gate_weight: bfloat16 [32, 7168, 1024], P('ep', 'dp'), may hold values from -0.0625 to 0.0625
- up_weight: bfloat16 [32, 7168, 1024], P('ep', 'dp'), may hold values from -0.0625 to 0.0625
- down_weight: bfloat16 [32, 1024, 7168], P('ep', None, 'dp'), may hold values from -0.1875 to 0.1875
Outputs:
- mixed: bfloat16 [4096, 7168], P('ep', 'dp')
Inputs may be any that keep to these rules, and one draw needn't show every extreme that they name: `capacity`: each expert's primary slots; the largest, 24, is taken by some expert in every draw. `spill_size`: each expert's overflow slots; the largest, 24, is taken by some expert in every draw. `routes`: A token names 8 different experts; in each aligned block of 128 tokens no expert is named by more than 64 tokens.
All inputs are finite; a program needn't handle non-finite values.
Results may differ from a plain program's by a relative error of at most 0.012.
Values may be sent and summed in bfloat16 or wider, within the bound.
No kernel may reach another device: no remote copies, remote signals or barrier semaphores. Data moves between devices by JAX's collectives and lax.ppermute only.
A program may use at most 128 MiB of HBM per device.

v0:
```python
import jax
import jax.numpy as jnp
from jax import lax
from jax.sharding import PartitionSpec as P

CAP = 24
SPILL = 24


def slot_tables(slot_ids, shares_of, slot_total):
    columns = jnp.arange(slot_total, dtype=jnp.int32)
    hits = (slot_ids[:, :, None] == columns[None, None, :]).astype(jnp.float32)
    select = jnp.sum(hits, axis=1)
    weigh = jnp.sum(hits * shares_of[:, :, None], axis=1)
    return (select, weigh)


def route_tables(routes, weights_int, capacity, spill_size, cap_slots, spill_slots):
    experts = capacity.shape[0]
    onehot = (routes[:, :, None] == jnp.arange(experts, dtype=jnp.int32)[None, None, :]).astype(
        jnp.int32
    )
    named_count = jnp.sum(onehot, axis=1)
    before = jnp.cumsum(named_count, axis=0) - named_count
    rank_in = jnp.sum(onehot * before[:, None, :], axis=2)
    cap_each = jnp.sum(onehot * capacity[None, None, :], axis=2)
    spill_each = jnp.sum(onehot * spill_size[None, None, :], axis=2)
    weight_float = weights_int.astype(jnp.float32)
    shares_of = weight_float / jnp.sum(weight_float, axis=1, keepdims=True)
    own_mask = rank_in < cap_each
    spill_mask = (rank_in >= cap_each) & (rank_in < cap_each + spill_each)
    own_slot = jnp.where(own_mask, routes * cap_slots + rank_in, -1)
    spill_slot = jnp.where(spill_mask, routes * spill_slots + rank_in - cap_each, -1)
    own_select, own_weigh = slot_tables(own_slot, shares_of, experts * cap_slots)
    spill_select, spill_weigh = slot_tables(spill_slot, shares_of, experts * spill_slots)
    return (own_select, own_weigh, spill_select, spill_weigh)


def select_rows(select, tokens):
    picked = lax.dot_general(
        select.astype(jnp.bfloat16),
        tokens,
        (((0,), (0,)), ((), ())),
        preferred_element_type=jnp.float32,
    )
    return picked.astype(jnp.bfloat16)


def by_expert(received, groups, local_experts, slots):
    features = received.shape[2]
    shaped = received.reshape(groups, local_experts, slots, features).transpose(1, 0, 2, 3)
    return shaped.reshape(local_experts, groups * slots, features)


def to_groups(outputs, groups, local_experts, slots):
    features = outputs.shape[2]
    shaped = outputs.reshape(local_experts, groups, slots, features).transpose(1, 0, 2, 3)
    return shaped.reshape(groups, local_experts * slots, features)


def project_in(rows_in, gate_weight, up_weight):
    gate_terms = jnp.einsum(
        "erd,edf->erf", rows_in, gate_weight, preferred_element_type=jnp.float32
    )
    up_terms = jnp.einsum("erd,edf->erf", rows_in, up_weight, preferred_element_type=jnp.float32)
    return (gate_terms, up_terms)


def project_out(hidden, down_weight):
    return jnp.einsum(
        "erf,efd->erd", hidden, down_weight, preferred_element_type=jnp.float32
    ).astype(jnp.bfloat16)


def weigh_values(weigh, values):
    upper = weigh.astype(jnp.bfloat16)
    lower = (weigh - upper.astype(jnp.float32)).astype(jnp.bfloat16)
    first = jnp.dot(upper, values, preferred_element_type=jnp.float32)
    return first + jnp.dot(lower, values, preferred_element_type=jnp.float32)


def on_device(
    tokens, routes, weights_int, capacity, spill_size, gate_weight, up_weight, down_weight
):
    experts = capacity.shape[0]
    groups = lax.axis_size("ep")
    local_experts = gate_weight.shape[0]
    features = tokens.shape[1]
    cap_slots = CAP
    spill_slots = SPILL
    own_select, own_weigh, spill_select, spill_weigh = route_tables(
        routes, weights_int, capacity, spill_size, cap_slots, spill_slots
    )
    own_buffer = select_rows(own_select, tokens).reshape(
        groups, local_experts * cap_slots, features
    )
    spill_buffer = select_rows(spill_select, tokens).reshape(
        groups, local_experts * spill_slots, features
    )
    got_own, got_spill = (
        lax.all_to_all(own_buffer, "ep", split_axis=0, concat_axis=0, tiled=True),
        lax.all_to_all(spill_buffer, "ep", split_axis=0, concat_axis=0, tiled=True),
    )
    own_rows = by_expert(got_own, groups, local_experts, cap_slots)
    spill_rows = by_expert(got_spill, groups, local_experts, spill_slots)
    rows_all = jnp.concatenate([own_rows, spill_rows], axis=1)
    gate_terms, up_terms = project_in(rows_all, gate_weight, up_weight)
    gate_sum, up_sum = lax.psum((gate_terms, up_terms), "dp")
    hidden = (jax.nn.silu(gate_sum) * up_sum).astype(jnp.bfloat16)
    own_count = groups * cap_slots
    own_hidden = hidden[:, :own_count]
    spill_hidden = hidden[:, own_count:]
    own_out = project_out(own_hidden, down_weight)
    spill_out = project_out(spill_hidden, down_weight)
    send_own = to_groups(own_out, groups, local_experts, cap_slots)
    send_spill = to_groups(spill_out, groups, local_experts, spill_slots)
    back_own, back_spill = (
        lax.all_to_all(send_own, "ep", split_axis=0, concat_axis=0, tiled=True),
        lax.all_to_all(send_spill, "ep", split_axis=0, concat_axis=0, tiled=True),
    )
    own_values = back_own.reshape(experts * cap_slots, features)
    spill_values = back_spill.reshape(experts * spill_slots, features)
    mixed = weigh_values(own_weigh, own_values) + weigh_values(spill_weigh, spill_values)
    return mixed.astype(jnp.bfloat16)


def solution(mesh):
    placed = (
        P("ep", "dp"),
        P("ep", None),
        P("ep", None),
        P(),
        P(),
        P("ep", "dp", None),
        P("ep", "dp", None),
        P("ep", None, "dp"),
    )
    return jax.shard_map(
        on_device, mesh=mesh, in_specs=placed, out_specs=P("ep", "dp"), check_vma=False
    )
```

profile of v0, /device:TPU:72, one launch (start us, length us, event | category | flops | bytes accessed | tf_op | source)
XLA Modules:
  0.0 330.0 jit_solution(16422530604865924986)
XLA Ops:
  6.5 0.0 copy-start
  6.5 0.0 copy-start.2
  6.5 0.8 convert_reduce_fusion.3
  7.3 0.7 convert_divide_fusion
  8.0 0.7 convert_reduce_fusion.2
  8.7 0.1 copy.21
  8.8 0.1 copy.25
  8.9 0.2 reduce_window_sum.11
  9.1 0.1 copy.23
  9.2 0.8 select_reduce_fusion.2
  10.0 0.7 subtract_select_fusion
  10.7 0.1 copy.27
  10.8 0.1 copy.24
  10.9 4.3 %select_reduce_fusion.1 = (f32[128,768]{1,0:T(8,128)S(1)}, bf16[128,768]{1,0:T(8,128)(2,1)S(1)}, f32[128,768]{1,0:T(8,128)S(1)}, bf16[128,768]{1,0:T(8,128)(2,1)S(1)}) fusion(f32[128,8]{1,0:T(8,128)S(1)} %copy.25, s32[128,8]{1,0:T(8,128)S(1)} %copy.24, s32[128,8]{1,0:T(8,128)S(1)} %copy.27), kind=kLoop, calls=%fused_computation.7 | loop fusion | flops 7471104 | bytes 1191936 | tf_op jit(solution)/shard_map/reduce_sum | solution.py:14
  15.2 1.2 convolution_convert_fusion.1
  16.4 1.2 copy.26
  17.6 10.2 %all-to-all-start = ((bf16[32,24,448]{2,1,0:T(8,128)(2,1)}), bf16[32,24,448]{2,1,0:T(8,128)(2,1)}, u32[]{:S(2)}, u32[]{:S(2)}) async-start(bf16[32,24,448]{2,1,0:T(8,128)(2,1)} %bitcast), calls=%async_computation | async-start | bytes 1572864 | tf_op jit(solution)/shard_map/all_to_all | solution.py:101
  27.8 0.0 all-reduce.3.cloned.1.call-start
  27.8 0.0 copy-done.2
  27.8 0.3 convolution_convert_fusion
  28.2 0.3 copy.28
  28.4 22.6 %all-to-all-done = bf16[32,24,448]{2,1,0:T(8,128)(2,1)} async-done(((bf16[32,24,448]{2,1,0:T(8,128)(2,1)}), bf16[32,24,448]{2,1,0:T(8,128)(2,1)}, u32[]{:S(2)}, u32[]{:S(2)}) %all-to-all-start) | async-done | bytes 688160 | tf_op jit(solution)/shard_map/all_to_all | solution.py:101
  51.0 27.4 %all_to_all.20 = bf16[32,24,448]{2,1,0:T(8,128)(2,1)S(1)} all-to-all(bf16[32,24,448]{2,1,0:T(8,128)(2,1)S(1)} %bitcast.50), channel_id=1, replica_groups=mesh['ep'=32,'dp'=16] {'ep'}, dimensions={0} | all-to-all | bytes 1376256 | tf_op jit(solution)/shard_map/all_to_all | solution.py:102
  78.4 0.0 copy-done
  78.4 0.0 copy-start.3
  78.4 5.7 %convolution_bitcast_fusion = f32[1,1536,1024]{2,1,0:T(8,128)} fusion(bf16[1,768,448]{2,1,0:T(8,128)(2,1)S(1)} %bitcast.51, bf16[1,768,448]{2,1,0:T(8,128)(2,1)} %bitcast.1, bf16[1,448,1024]{2,1,0:T(8,128)(2,1)S(1)} %copy-done), kind=kOutput, calls=%fused_computation.1 | convolution fusion | flops 1412038656 | bytes 8585216 | tf_op jit(solution)/shard_map/erd,edf->erf/dot_general | solution.py:65
  84.1 0.0 copy-done.3
  84.1 5.6 %convolution_bitcast_fusion.1 = f32[1,1536,1024]{2,1,0:T(8,128)} fusion(bf16[1,768,448]{2,1,0:T(8,128)(2,1)S(1)} %bitcast.52, bf16[1,768,448]{2,1,0:T(8,128)(2,1)} %bitcast.1, bf16[1,448,1024]{2,1,0:T(8,128)(2,1)S(1)} %copy-done.3), kind=kOutput, calls=%fused_computation.2 | convolution fusion | flops 1412038656 | bytes 8585216 | tf_op jit(solution)/shard_map/erd,edf->erf/dot_general | solution.py:62
  89.7 0.0 all-reduce.3.cloned.1.call-update
  89.7 160.0 %all-reduce.3.cloned.1.call-done = (f32[1,1536,1024]{2,1,0:T(8,128)}, f32[1,1536,1024]{2,1,0:T(8,128)}) async-done(((f32[1,1536,1024]{2,1,0:T(8,128)}, f32[1,1536,1024]{2,1,0:T(8,128)}), (f32[1,1536,1024]{2,1,0:T(8,128)}, f32[1,1536,1024]{2,1,0:T(8,128)})) %all-reduce.3.cloned.1.call-update) | async-done | bytes 12582928 | tf_op jit(solution)/shard_map/psum | solution.py:108
  249.7 0.0 copy-start.4
  249.7 5.7 %multiply_convert_fusion = bf16[1,1536,1024]{2,1,0:T(8,128)(2,1)S(1)} fusion(f32[1,1536,1024]{2,1,0:T(8,128)} %get-tuple-element.12, f32[1,1536,1024]{2,1,0:T(8,128)} %get-tuple-element.13), kind=kLoop, calls=%fused_computation | loop fusion | flops 9437184 | bytes 15728640 | tf_op jit(solution)/shard_map/convert_element_type | solution.py:109
  255.4 0.0 copy-start.1
  255.4 1.7 copy-done.1
  257.0 0.0 copy-done.4
  257.0 0.9 fusion.3
  258.0 1.2 copy.30
  259.1 9.8 %all-to-all-start.3 = ((bf16[32,24,448]{2,1,0:T(8,128)(2,1)}), bf16[32,24,448]{2,1,0:T(8,128)(2,1)S(1)}, u32[]{:S(2)}, u32[]{:S(2)}) async-start(bf16[32,24,448]{2,1,0:T(8,128)(2,1)} %bitcast.14), calls=%async_computation.3 | async-start | bytes 1572864 | tf_op jit(solution)/shard_map/all_to_all | solution.py:119
  269.0 2.6 fusion.2
  271.6 1.2 copy.29
  272.7 20.3 %all-to-all-done.3 = bf16[32,24,448]{2,1,0:T(8,128)(2,1)S(1)} async-done(((bf16[32,24,448]{2,1,0:T(8,128)(2,1)}), bf16[32,24,448]{2,1,0:T(8,128)(2,1)S(1)}, u32[]{:S(2)}, u32[]{:S(2)}) %all-to-all-start.3) | async-done | bytes 688160 | tf_op jit(solution)/shard_map/all_to_all | solution.py:119
  293.0 5.3 %all-to-all-start.2 = ((bf16[32,24,448]{2,1,0:T(8,128)(2,1)}), bf16[32,24,448]{2,1,0:T(8,128)(2,1)S(1)}, u32[]{:S(2)}, u32[]{:S(2)}) async-start(bf16[32,24,448]{2,1,0:T(8,128)(2,1)} %bitcast.49), calls=%async_computation.2 | async-start | bytes 1572864 | tf_op jit(solution)/shard_map/all_to_all | solution.py:118
  298.3 0.4 fusion.13
  298.8 0.4 convolution_add_fusion
  299.2 22.4 %all-to-all-done.2 = bf16[32,24,448]{2,1,0:T(8,128)(2,1)S(1)} async-done(((bf16[32,24,448]{2,1,0:T(8,128)(2,1)}), bf16[32,24,448]{2,1,0:T(8,128)(2,1)S(1)}, u32[]{:S(2)}, u32[]{:S(2)}) %all-to-all-start.2) | async-done | bytes 688160 | tf_op jit(solution)/shard_map/all_to_all | solution.py:118
  321.6 0.4 fusion.16
  322.1 1.1 fusion.5
  (1 shorter events, 0.0 us)
Async XLA Ops:
  6.5 71.9 %copy-start = (bf16[1,448,1024]{2,1,0:T(8,128)(2,1)S(1)}, bf16[1,448,1024]{2,1,0:T(8,128)(2,1)}, u32[]{:S(2)}) copy-start(bf16[1,448,1024]{2,1,0:T(8,128)(2,1)} %param.14) | copy-start | bytes 2752516
  6.5 21.3 %copy-start.2 = (bf16[128,448]{0,1:T(8,128)(2,1)S(1)}, bf16[128,448]{0,1:T(8,128)(2,1)}, u32[]{:S(2)}) copy-start(bf16[128,448]{0,1:T(8,128)(2,1)} %param.8) | copy-start | bytes 344068
  17.6 33.4 %all-to-all-start = ((bf16[32,24,448]{2,1,0:T(8,128)(2,1)}), bf16[32,24,448]{2,1,0:T(8,128)(2,1)}, u32[]{:S(2)}, u32[]{:S(2)}) async-start(bf16[32,24,448]{2,1,0:T(8,128)(2,1)} %bitcast), calls=%async_computation | async-start | bytes 1572864 | tf_op jit(solution)/shard_map/all_to_all | solution.py:101
  27.8 221.9 %all-reduce.3.cloned.1.call-start = ((), (), s32[]{:S(2)}) async-start(), calls=%async_computation.4 | async-start | bytes 25165824 | tf_op jit(solution)/shard_map/psum | solution.py:108
  78.4 5.7 %copy-start.3 = (bf16[1,448,1024]{2,1,0:T(8,128)(2,1)S(1)}, bf16[1,448,1024]{2,1,0:T(8,128)(2,1)}, u32[]{:S(2)}) copy-start(bf16[1,448,1024]{2,1,0:T(8,128)(2,1)} %param.13) | copy-start | bytes 2752516
  249.7 7.4 %copy-start.4 = (bf16[1,1024,448]{1,2,0:T(8,128)(2,1)S(1)}, bf16[1,1024,448]{1,2,0:T(8,128)(2,1)}, u32[]{:S(2)}) copy-start(bf16[1,1024,448]{1,2,0:T(8,128)(2,1)} %param.15) | copy-start | bytes 2752516
  255.4 1.7 copy-start.1
  259.1 33.9 %all-to-all-start.3 = ((bf16[32,24,448]{2,1,0:T(8,128)(2,1)}), bf16[32,24,448]{2,1,0:T(8,128)(2,1)S(1)}, u32[]{:S(2)}, u32[]{:S(2)}) async-start(bf16[32,24,448]{2,1,0:T(8,128)(2,1)} %bitcast.14), calls=%async_computation.3 | async-start | bytes 1572864 | tf_op jit(solution)/shard_map/all_to_all | solution.py:119
  293.0 28.6 %all-to-all-start.2 = ((bf16[32,24,448]{2,1,0:T(8,128)(2,1)}), bf16[32,24,448]{2,1,0:T(8,128)(2,1)S(1)}, u32[]{:S(2)}, u32[]{:S(2)}) async-start(bf16[32,24,448]{2,1,0:T(8,128)(2,1)} %bitcast.49), calls=%async_computation.2 | async-start | bytes 1572864 | tf_op jit(solution)/shard_map/all_to_all | solution.py:118
Sparse Core Ops, SparseCore 0:
  89.8 159.8 all-reduce.2
where the time goes:
time: 331 us; the launch traced here: 330 us
  waiting for transfers between devices  225 us (68%)
  blocking collectives  27.4 us (8%)
  starting transfers between devices  25.4 us (8%)
  matrix products  18.7 us (6%)
  other arithmetic  13.9 us (4%)
  between operations  13.5 us (4%)
  local copies, waits for them, and re-layouts  5.87 us (2%)
    psum x1, waiting for transfers between devices, on_device(): gate_sum, up_sum = lax.psum((gate_terms, up_terms), 'dp')  160 us
    all_to_all x1, blocking collectives, on_device(): lax.all_to_all(spill_buffer, 'ep', split_axis=0, concat_axis=0, tiled=True)  27.4 us
    all_to_all x1, waiting for transfers between devices, on_device(): lax.all_to_all(own_buffer, 'ep', split_axis=0, concat_axis=0, tiled=True)  22.6 us
    all_to_all x1, waiting for transfers between devices, on_device(): lax.all_to_all(send_own, 'ep', split_axis=0, concat_axis=0, tiled=True)  22.4 us
    all_to_all x1, waiting for transfers between devices, on_device(): lax.all_to_all(send_spill, 'ep', split_axis=0, concat_axis=0, tiled=True)  20.3 us
    all_to_all x1, starting transfers between devices, on_device(): lax.all_to_all(own_buffer, 'ep', split_axis=0, concat_axis=0, tiled=True)  10.2 us
    all_to_all x1, starting transfers between devices, on_device(): lax.all_to_all(send_spill, 'ep', split_axis=0, concat_axis=0, tiled=True)  9.85 us
  transfers between devices with their start and end apart: 4, of which 4 were waited for; matrix products, arithmetic and copies ran while one was open for 2% of the time, Pallas kernels for 0%

commit v1 on v0

v1 whole, which is shorter than its diff:
```python
import functools

import jax
import jax.numpy as jnp
from jax import lax
from jax.experimental import pallas as pl
from jax.experimental.pallas import tpu as pltpu
from jax.sharding import PartitionSpec as P

SLOTS = 48
HALF = 24
STRIP = 256

VMEM = pl.BlockSpec(memory_space=pltpu.VMEM)
SMEM = pl.BlockSpec(memory_space=pltpu.SMEM)
NT = (((1,), (1,)), ((), ()))
LIMIT = pltpu.CompilerParams(vmem_limit_bytes=40 * 1024 * 1024)


def column(row, experts):
    first = lax.broadcasted_iota(jnp.int32, (experts, experts), 0)
    second = lax.broadcasted_iota(jnp.int32, (experts, experts), 1)
    spread = jnp.where(first == second, jnp.broadcast_to(row, (experts, experts)), 0.0)
    return jnp.sum(spread, axis=1, keepdims=True)


def ranks(routes, capacity, spill):
    experts = capacity.shape[1]
    top, tokens = routes.shape
    number = lax.broadcasted_iota(jnp.int32, (experts, tokens), 0)
    named = jnp.zeros((experts, tokens), jnp.float32)
    for k in range(top):
        named = named + jnp.where(routes[k : k + 1, :] == number, 1.0, 0.0)
    earlier = lax.broadcasted_iota(jnp.int32, (tokens, tokens), 0) < lax.broadcasted_iota(
        jnp.int32, (tokens, tokens), 1
    )
    before = jnp.dot(
        named.astype(jnp.bfloat16),
        jnp.where(earlier, 1.0, 0.0).astype(jnp.bfloat16),
        preferred_element_type=jnp.float32,
    )
    limit = column((capacity + spill).astype(jnp.float32), experts)
    return jnp.where((named > 0.0) & (before < limit), before, -1.0)


def pick_kernel(core, routes, capacity, spill, tokens, tokens_other, rows):
    rank = ranks(routes[...], capacity[...], spill[...])
    experts, count = rank.shape
    slot = lax.broadcasted_iota(jnp.int32, (experts, HALF, count), 1) + core[0] * HALF
    pick = jnp.where(rank[:, None, :] == slot.astype(jnp.float32), 1.0, 0.0)
    pick = pick.reshape(experts * HALF, count).astype(jnp.bfloat16)
    features = jnp.concatenate([tokens[...], tokens_other[...]], axis=0)
    picked = lax.dot_general(pick, features, NT, preferred_element_type=jnp.float32)
    rows[...] = picked.astype(jnp.bfloat16)


def weigh_kernel(routes, weights, capacity, spill, weigh):
    rank = ranks(routes[...], capacity[...], spill[...])
    experts, count = rank.shape
    value = weights[...].astype(jnp.float32)
    share = value / jnp.sum(value, axis=0, keepdims=True)
    number = lax.broadcasted_iota(jnp.int32, (experts, count), 0)
    share_of = jnp.zeros((experts, count), jnp.float32)
    for k in range(value.shape[0]):
        share_of = share_of + jnp.where(routes[k : k + 1, :] == number, share[k : k + 1, :], 0.0)
    slot = lax.broadcasted_iota(jnp.int32, (experts, SLOTS, count), 1).astype(jnp.float32)
    table = jnp.where(rank[:, None, :] == slot, share_of[:, None, :], 0.0)
    table = table.reshape(experts * SLOTS, count).T
    upper = table.astype(jnp.bfloat16)
    lower = (table - upper.astype(jnp.float32)).astype(jnp.bfloat16)
    weigh[0:count, :] = upper
    weigh[count : 2 * count, :] = lower


def project_kernel(rows, gate, gate_other, up, up_other, sums):
    for at, (own, other) in enumerate(((gate, gate_other), (up, up_other))):
        weight = jnp.concatenate([own[...], other[...]], axis=0)
        part = jnp.dot(rows[...], weight, preferred_element_type=jnp.float32)
        sums[:, at * STRIP : (at + 1) * STRIP] = part.astype(jnp.bfloat16)


def hidden_kernel(sums, hidden):
    for strip in range(hidden.shape[1] // STRIP):
        at = 2 * STRIP * strip
        gate = sums[:, at : at + STRIP].astype(jnp.float32)
        up = sums[:, at + STRIP : at + 2 * STRIP].astype(jnp.float32)
        value = gate / (1.0 + jnp.exp(-gate)) * up
        hidden[:, STRIP * strip : STRIP * (strip + 1)] = value.astype(jnp.bfloat16)


def down_kernel(hidden, down, out):
    pairs, _, depth, width = hidden.shape
    for pair in range(pairs):
        both = hidden[pair].reshape(2 * depth, width)
        value = lax.dot_general(both, down[...], NT, preferred_element_type=jnp.float32)
        for j in range(depth // HALF):
            first = value[j * HALF : (j + 1) * HALF]
            second = value[depth + j * HALF : depth + (j + 1) * HALF]
            block = jnp.concatenate([first, second], axis=0)
            out[pair * (depth // HALF) + j] = block.astype(jnp.bfloat16)


def mix_kernel(weigh, values, mixed):
    total = jnp.dot(weigh[...], values[...], preferred_element_type=jnp.float32)
    count = total.shape[0] // 2
    mixed[...] = (total[:count] + total[count:]).T.astype(jnp.bfloat16)


def cost(flops, moved):
    return pl.CostEstimate(flops=flops, bytes_accessed=moved, transcendentals=0)


def on_device(
    tokens, routes, weights_int, capacity, spill_size, gate_weight, up_weight, down_weight
):
    experts = capacity.shape[0]
    groups = lax.axis_size("ep")
    planes = lax.axis_size("dp") // 2
    count, features = tokens.shape
    units = gate_weight.shape[2]
    bf16 = jnp.bfloat16
    core = (lax.axis_index("dp") % 2).astype(jnp.int32).reshape(1)
    swap = [(i, i ^ 1) for i in range(2 * planes)]
    same_core = [[2 * z + c for z in range(planes)] for c in range(2)]

    own_tokens = tokens.T
    own_routes = routes.T
    own_weights = weights_int.T
    cap_row = capacity.reshape(1, experts)
    spill_row = spill_size.reshape(1, experts)
    gate = gate_weight[0]
    up = up_weight[0]
    down = down_weight[0].T

    tokens_other = lax.ppermute(own_tokens, "dp", swap)
    gate_other = lax.ppermute(gate, "dp", swap)
    up_other = lax.ppermute(up, "dp", swap)

    send = pl.pallas_call(
        pick_kernel,
        out_shape=jax.ShapeDtypeStruct((experts * HALF, 2 * features), bf16),
        in_specs=[SMEM] + [VMEM] * 5,
        out_specs=VMEM,
        compiler_params=LIMIT,
        cost_estimate=cost(2 * experts * HALF * count * 2 * features, 2000000),
        name="pick_rows",
    )(core, own_routes, cap_row, spill_row, own_tokens, tokens_other)
    got = lax.all_to_all(
        send.reshape(groups, HALF, 2 * features), "ep", split_axis=0, concat_axis=0, tiled=True
    ).reshape(groups * HALF, 2 * features)

    depth = groups * HALF
    wide = pl.BlockSpec((features, STRIP), lambda i: (0, i))
    sums = pl.pallas_call(
        project_kernel,
        grid=(units // STRIP,),
        out_shape=jax.ShapeDtypeStruct((depth, 2 * units), bf16),
        in_specs=[pl.BlockSpec((depth, 2 * features), lambda i: (0, 0))] + [wide] * 4,
        out_specs=pl.BlockSpec((depth, 2 * STRIP), lambda i: (0, i)),
        compiler_params=LIMIT,
        cost_estimate=cost(2 * depth * 2 * features * 2 * units, 8000000),
        name="project_in",
    )(got, gate, gate_other, up, up_other)
    summed = lax.psum_scatter(
        sums, "dp", scatter_dimension=0, tiled=True, axis_index_groups=same_core
    )
    weigh = pl.pallas_call(
        weigh_kernel,
        out_shape=jax.ShapeDtypeStruct((2 * count, experts * SLOTS), bf16),
        in_specs=[VMEM] * 4,
        out_specs=VMEM,
        compiler_params=LIMIT,
        cost_estimate=cost(2 * experts * count * count, 4000000),
        name="weigh_table",
    )(own_routes, own_weights, cap_row, spill_row)
    part = depth // planes
    hidden = pl.pallas_call(
        hidden_kernel,
        out_shape=jax.ShapeDtypeStruct((part, units), bf16),
        in_specs=[VMEM],
        out_specs=VMEM,
        compiler_params=LIMIT,
        cost_estimate=cost(8 * part * units, 600000),
        name="hidden_units",
    )(summed)
    all_hidden = lax.all_gather(hidden, "dp", axis=0, tiled=True)
    all_hidden = all_hidden.reshape(planes, 2, part, units)

    at_once = 2
    blocks = at_once * part // HALF
    back = pl.pallas_call(
        down_kernel,
        grid=(planes // at_once,),
        out_shape=jax.ShapeDtypeStruct((groups, SLOTS, features), bf16),
        in_specs=[
            pl.BlockSpec((at_once, 2, part, units), lambda i: (i, 0, 0, 0)),
            pl.BlockSpec((features, units), lambda i: (0, 0)),
        ],
        out_specs=pl.BlockSpec((blocks, SLOTS, features), lambda i: (i, 0, 0)),
        compiler_params=LIMIT,
        cost_estimate=cost(2 * 2 * depth * units * features, 6000000),
        name="project_out",
    )(all_hidden, down)
    values = lax.all_to_all(back, "ep", split_axis=0, concat_axis=0, tiled=True)
    mixed = pl.pallas_call(
        mix_kernel,
        out_shape=jax.ShapeDtypeStruct((features, count), bf16),
        in_specs=[VMEM] * 2,
        out_specs=VMEM,
        compiler_params=LIMIT,
        cost_estimate=cost(4 * count * experts * SLOTS * features, 3000000),
        name="mix_rows",
    )(weigh, values.reshape(experts * SLOTS, features))
    return mixed.T


def solution(mesh):
    placed = (
        P("ep", "dp"),
        P("ep", None),
        P("ep", None),
        P(),
        P(),
        P("ep", "dp", None),
        P("ep", "dp", None),
        P("ep", None, "dp"),
    )
    return jax.shard_map(
        on_device, mesh=mesh, in_specs=placed, out_specs=P("ep", "dp"), check_vma=False
    )
```

time: 331 us -> 227 us (0.69)
  the two profiles are of different devices: /device:TPU:72 before, /device:TPU:9 now
where the time goes in v1:
time: 227 us; the launch traced here: 226 us
  waiting for transfers between devices  163 us (72%)
  starting transfers between devices  26.6 us (12%)
  between operations  13.5 us (6%)
  Pallas kernels  13.2 us (6%)
  local copies, waits for them, and re-layouts  10 us (4%)
    reduce_scatter x1, waiting for transfers between devices, on_device(): lax.psum_scatter(sums, 'dp', scatter_dimension=0, tiled=True, axis_index_...  48 us
    all_gather x1, waiting for transfers between devices, on_device(): all_hidden = lax.all_gather(hidden, 'dp', axis=0, tiled=True)  46.3 us
    all_to_all x1, waiting for transfers between devices, on_device(): values = lax.all_to_all(back, 'ep', split_axis=0, concat_axis=0, tiled=True)  38.6 us
    all_to_all x1, waiting for transfers between devices, on_device(): lax.all_to_all(send.reshape(groups, HALF, 2 * features), 'ep', split_axis...  27.1 us
    unnamed x34, local copies, waits for them, and re-layouts  10 us
    all_to_all x1, starting transfers between devices, on_device(): lax.all_to_all(send.reshape(groups, HALF, 2 * features), 'ep', split_axis...  9.73 us
    all_to_all x1, starting transfers between devices, on_device(): values = lax.all_to_all(back, 'ep', split_axis=0, concat_axis=0, tiled=True)  9.43 us
    pallas_call x1, Pallas kernels, on_device(): pl.pallas_call(project_kernel, grid=(units // STRIP,), out_shape=jax.Shap...  5.39 us
  transfers between devices with their start and end apart: 7, of which 7 were waited for; matrix products, arithmetic and copies ran while one was open for 0% of the time, Pallas kernels for 0%

profile of v1, /device:TPU:9, one launch (start us, length us, event | category | flops | bytes accessed | tf_op | source)
XLA Modules:
  0.0 226.1 jit_solution(15016571641726638376)
XLA Ops:
  6.5 2.6 %collective-permute-start = (bf16[448,128]{1,0:T(8,128)(2,1)}, bf16[448,128]{1,0:T(8,128)(2,1)S(1)}, u32[]{:S(2)}, u32[]{:S(2)}) collective-permute-start(bf16[448,128]{1,0:T(8,128)(2,1)} %bitcast.20), channel_id=1, source_target_pairs={{0,1},{1,0},{2,3},{3,2},{4,5},{5,4},{6,7},{7,6},{8,9},{9,8},{10,11... | collective-permute-start | bytes 344072 | tf_op jit(solution)/shard_map/ppermute | solution.py:135
  9.1 1.1 collective-permute-done.tokens_other
  10.3 0.0 copy-start.3
  10.3 0.9 copy-done.3
  11.2 0.0 copy-start.4
  11.2 0.7 copy-done.4
  11.9 0.0 copy-start.7
  11.9 0.7 copy-done.7
  12.5 0.0 copy-start.9
  12.5 0.7 copy-done.9
  13.2 1.8 pick_rows.1
  14.9 0.0 copy-start.11
  14.9 0.0 copy-start.12
  14.9 9.7 %all-to-all-start = ((bf16[32,24,896]{2,1,0:T(8,128)(2,1)}), bf16[32,24,896]{2,1,0:T(8,128)(2,1)S(1)}, u32[]{:S(2)}, u32[]{:S(2)}) async-start(bf16[32,24,896]{2,1,0:T(8,128)(2,1)} %bitcast.6), calls=%async_computation | async-start | bytes 2752512 | tf_op jit(solution)/shard_map/all_to_all | solution.py:148
  24.7 0.0 reduce-scatter.2.cloned.1.call-start
  24.7 0.0 copy-done.11
  24.7 2.8 %collective-permute-start.1 = (bf16[448,1024]{1,0:T(8,128)(2,1)S(1)}, bf16[448,1024]{1,0:T(8,128)(2,1)S(1)}, u32[]{:S(2)}, u32[]{:S(2)}) collective-permute-start(bf16[448,1024]{1,0:T(8,128)(2,1)S(1)} %bitcast.29), channel_id=1, source_target_pairs={{0,1},{1,0},{2,3},{3,2},{4,5},{5,4},{6,7},{7,6},{8,9},{9,8},{10,11... | collective-permute-start | bytes 2752520 | tf_op jit(solution)/shard_map/ppermute | solution.py:136
  27.6 0.0 copy-done.12
  27.6 1.9 collective-permute-start.2
  29.5 0.1 collective-permute-done.1.gate_other
  29.6 0.0 copy-start.13
  29.6 0.9 copy-done.13
  30.6 1.4 collective-permute-done.2.up_other
  31.9 0.0 copy-start.15
  31.9 0.9 copy-done.15
  32.9 27.1 %all-to-all-done = bf16[32,24,896]{2,1,0:T(8,128)(2,1)S(1)} async-done(((bf16[32,24,896]{2,1,0:T(8,128)(2,1)}), bf16[32,24,896]{2,1,0:T(8,128)(2,1)S(1)}, u32[]{:S(2)}, u32[]{:S(2)}) %all-to-all-start) | async-done | bytes 1376288 | tf_op jit(solution)/shard_map/all_to_all | solution.py:148
  60.0 0.0 copy-start.14
  60.0 1.2 copy-done.14
  61.2 0.0 copy-start.16
  61.2 1.2 copy-done.16
  62.4 5.4 %project_in.1 = bf16[768,2048]{1,0:T(8,128)(2,1)} custom-call(bf16[768,896]{1,0:T(8,128)(2,1)S(1)} %bitcast.18, bf16[448,1024]{1,0:T(8,128)(2,1)S(1)} %bitcast.30, bf16[448,1024]{1,0:T(8,128)(2,1)S(1)} %copy-done.14, bf16[448,1024]{1,0:T(8,128)(2,1)S(1)} %bitcast.32, bf16[448,1024]{1,0:T(8,128)(2,1)S(1)} %copy-done.16), custom_call_target="tpu_custom_call" | custom-call | flops 2818572288 | bytes 8000000 | tf_op jit(solution)/shard_map/project_in/pallas_call | solution.py:154
  67.8 0.0 copy-start.1
  67.8 0.0 reduce-scatter.2.cloned.1.call-update
  67.8 0.0 all-gather.2.cloned.1.call-start
  67.8 48.0 %reduce-scatter.2.cloned.1.call-done.sums = bf16[96,2048]{1,0:T(8,128)(2,1)} async-done(((bf16[768,2048]{1,0:T(8,128)(2,1)}), bf16[96,2048]{1,0:T(8,128)(2,1)}) %reduce-scatter.2.cloned.1.call-update) | async-done | bytes 393232 | tf_op jit(solution)/shard_map/reduce_scatter | solution.py:164
  115.9 0.0 copy-start.2
  115.9 1.0 copy-done.2
  116.9 0.8 hidden_units.1
  117.7 0.0 all-gather.2.cloned.1.call-update
  117.7 46.3 %all-gather.2.cloned.1.call-done = bf16[1536,1024]{1,0:T(8,128)(2,1)} async-done(((bf16[96,1024]{1,0:T(8,128)(2,1)}), bf16[1536,1024]{1,0:T(8,128)(2,1)}) %all-gather.2.cloned.1.call-update) | async-done | bytes 3145744 | tf_op jit(solution)/shard_map/all_gather | solution.py:186
  164.0 0.0 copy-done.1
  164.0 0.0 copy-start
  164.0 1.9 copy-done
  165.9 3.5 %project_out.1 = bf16[32,48,448]{2,1,0:T(8,128)(2,1)} custom-call(bf16[8,2,96,1024]{3,2,1,0:T(8,128)(2,1)S(1)} %bitcast.17, bf16[448,1024]{1,0:T(8,128)(2,1)S(1)} %bitcast.19), custom_call_target="tpu_custom_call" | custom-call | flops 1409286144 | bytes 6000000 | tf_op jit(solution)/shard_map/project_out/pallas_call | solution.py:191
  169.5 0.0 copy-start.5
  169.5 0.0 copy-start.6
  169.5 0.0 copy-start.8
  169.5 0.0 copy-start.10
  169.5 9.4 %all-to-all-start.1 = ((bf16[32,48,448]{2,1,0:T(8,128)(2,1)}), bf16[32,48,448]{2,1,0:T(8,128)(2,1)S(1)}, u32[]{:S(2)}, u32[]{:S(2)}) async-start(bf16[32,48,448]{2,1,0:T(8,128)(2,1)} %project_out.1), calls=%async_computation.2 | async-start | bytes 3145728 | tf_op jit(solution)/shard_map/all_to_all | solution.py:204
  178.9 0.0 copy-done.5
  178.9 0.0 copy-done.6
  178.9 0.0 copy-done.8
  178.9 0.0 copy-done.10
  178.9 0.4 weigh_table.1.weigh
  179.4 38.6 %all-to-all-done.1 = bf16[32,48,448]{2,1,0:T(8,128)(2,1)S(1)} async-done(((bf16[32,48,448]{2,1,0:T(8,128)(2,1)}), bf16[32,48,448]{2,1,0:T(8,128)(2,1)S(1)}, u32[]{:S(2)}, u32[]{:S(2)}) %all-to-all-start.1) | async-done | bytes 1376288 | tf_op jit(solution)/shard_map/all_to_all | solution.py:204
  217.9 1.3 mix_rows.1
Async XLA Ops:
  6.5 3.7 %collective-permute-start = (bf16[448,128]{1,0:T(8,128)(2,1)}, bf16[448,128]{1,0:T(8,128)(2,1)S(1)}, u32[]{:S(2)}, u32[]{:S(2)}) collective-permute-start(bf16[448,128]{1,0:T(8,128)(2,1)} %bitcast.20), channel_id=1, source_target_pairs={{0,1},{1,0},{2,3},{3,2},{4,5},{5,4},{6,7},{7,6},{8,9},{9,8},{10,11... | collective-permute-start | bytes 344072 | tf_op jit(solution)/shard_map/ppermute | solution.py:135
  10.3 0.9 copy-start.3
  11.2 0.7 copy-start.4
  11.9 0.7 copy-start.7
  12.5 0.7 copy-start.9
  14.9 9.8 %copy-start.11 = (bf16[1,448,1024]{2,1,0:T(8,128)(2,1)S(1)}, bf16[1,448,1024]{2,1,0:T(8,128)(2,1)}, u32[]{:S(2)}) copy-start(bf16[1,448,1024]{2,1,0:T(8,128)(2,1)} %param.13) | copy-start | bytes 2752516
  14.9 12.6 %copy-start.12 = (bf16[1,448,1024]{2,1,0:T(8,128)(2,1)S(1)}, bf16[1,448,1024]{2,1,0:T(8,128)(2,1)}, u32[]{:S(2)}) copy-start(bf16[1,448,1024]{2,1,0:T(8,128)(2,1)} %param.14) | copy-start | bytes 2752516
  14.9 45.1 %all-to-all-start = ((bf16[32,24,896]{2,1,0:T(8,128)(2,1)}), bf16[32,24,896]{2,1,0:T(8,128)(2,1)S(1)}, u32[]{:S(2)}, u32[]{:S(2)}) async-start(bf16[32,24,896]{2,1,0:T(8,128)(2,1)} %bitcast.6), calls=%async_computation | async-start | bytes 2752512 | tf_op jit(solution)/shard_map/all_to_all | solution.py:148
  24.7 91.2 %reduce-scatter.2.cloned.1.call-start = ((), (), s32[]{:S(2)}) async-start(), calls=%async_computation.3 | async-start | bytes 3538944 | tf_op jit(solution)/shard_map/reduce_scatter | solution.py:164
  24.7 4.9 %collective-permute-start.1 = (bf16[448,1024]{1,0:T(8,128)(2,1)S(1)}, bf16[448,1024]{1,0:T(8,128)(2,1)S(1)}, u32[]{:S(2)}, u32[]{:S(2)}) collective-permute-start(bf16[448,1024]{1,0:T(8,128)(2,1)S(1)} %bitcast.29), channel_id=1, source_target_pairs={{0,1},{1,0},{2,3},{3,2},{4,5},{5,4},{6,7},{7,6},{8,9},{9,8},{10,11... | collective-permute-start | bytes 2752520 | tf_op jit(solution)/shard_map/ppermute | solution.py:136
  27.6 4.4 %collective-permute-start.2 = (bf16[448,1024]{1,0:T(8,128)(2,1)S(1)}, bf16[448,1024]{1,0:T(8,128)(2,1)S(1)}, u32[]{:S(2)}, u32[]{:S(2)}) collective-permute-start(bf16[448,1024]{1,0:T(8,128)(2,1)S(1)} %bitcast.31), channel_id=1, source_target_pairs={{0,1},{1,0},{2,3},{3,2},{4,5},{5,4},{6,7},{7,6},{8,9},{9,8},{10,11... | collective-permute-start | bytes 2752520 | tf_op jit(solution)/shard_map/ppermute | solution.py:137
  29.6 0.9 copy-start.13
  31.9 0.9 copy-start.15
  60.0 1.2 copy-start.14
  61.2 1.2 copy-start.16
  67.8 96.3 %copy-start.1 = (bf16[1,1024,448]{1,2,0:T(8,128)(2,1)S(1)}, bf16[1,1024,448]{1,2,0:T(8,128)(2,1)}, u32[]{:S(2)}) copy-start(bf16[1,1024,448]{1,2,0:T(8,128)(2,1)} %param.15) | copy-start | bytes 2752516
  67.8 96.2 %all-gather.2.cloned.1.call-start = ((), (), s32[]{:S(2)}) async-start(), calls=%async_computation.4 | async-start | bytes 3342336 | tf_op jit(solution)/shard_map/all_gather | solution.py:186
  115.9 1.0 copy-start.2
  164.0 1.9 copy-start
  169.5 9.4 %copy-start.5 = (s32[128,8]{0,1:T(8,128)S(1)}, s32[128,8]{0,1:T(8,128)}, u32[]{:S(2)}) copy-start(s32[128,8]{0,1:T(8,128)} %param.9) | copy-start | bytes 12292
  169.5 9.5 %copy-start.6 = (s32[128,8]{0,1:T(8,128)S(1)}, s32[128,8]{0,1:T(8,128)}, u32[]{:S(2)}) copy-start(s32[128,8]{0,1:T(8,128)} %param.10) | copy-start | bytes 12292
  169.5 9.5 %copy-start.8 = (s32[32]{0:T(128)S(1)}, s32[32]{0:T(128)}, u32[]{:S(2)}) copy-start(s32[32]{0:T(128)} %param.11) | copy-start | bytes 388
  169.5 9.5 %copy-start.10 = (s32[32]{0:T(128)S(1)}, s32[32]{0:T(128)}, u32[]{:S(2)}) copy-start(s32[32]{0:T(128)} %param.12) | copy-start | bytes 388
  169.5 48.5 %all-to-all-start.1 = ((bf16[32,48,448]{2,1,0:T(8,128)(2,1)}), bf16[32,48,448]{2,1,0:T(8,128)(2,1)S(1)}, u32[]{:S(2)}, u32[]{:S(2)}) async-start(bf16[32,48,448]{2,1,0:T(8,128)(2,1)} %project_out.1), calls=%async_computation.2 | async-start | bytes 3145728 | tf_op jit(solution)/shard_map/all_to_all | solution.py:204
Sparse Core Ops, SparseCore 0:
  67.9 47.9 reduce-scatter.1
  118.0 45.9 all-gather.1

commit v2 on v1

--- a/solution.py
+++ b/solution.py
@@ -7,14 +7,13 @@
 from jax.experimental.pallas import tpu as pltpu
 from jax.sharding import PartitionSpec as P
 
-SLOTS = 48
 HALF = 24
 STRIP = 256
 
 VMEM = pl.BlockSpec(memory_space=pltpu.VMEM)
 SMEM = pl.BlockSpec(memory_space=pltpu.SMEM)
 NT = (((1,), (1,)), ((), ()))
-LIMIT = pltpu.CompilerParams(vmem_limit_bytes=40 * 1024 * 1024)
+LIMIT = pltpu.CompilerParams(vmem_limit_bytes=60 * 1024 * 1024)
 
 
 def column(row, experts):
@@ -63,13 +62,14 @@
     share_of = jnp.zeros((experts, count), jnp.float32)
     for k in range(value.shape[0]):
         share_of = share_of + jnp.where(routes[k : k + 1, :] == number, share[k : k + 1, :], 0.0)
-    slot = lax.broadcasted_iota(jnp.int32, (experts, SLOTS, count), 1).astype(jnp.float32)
-    table = jnp.where(rank[:, None, :] == slot, share_of[:, None, :], 0.0)
-    table = table.reshape(experts * SLOTS, count).T
-    upper = table.astype(jnp.bfloat16)
-    lower = (table - upper.astype(jnp.float32)).astype(jnp.bfloat16)
-    weigh[0:count, :] = upper
-    weigh[count : 2 * count, :] = lower
+    slot = lax.broadcasted_iota(jnp.int32, (experts, HALF, count), 1).astype(jnp.float32)
+    for half in range(2):
+        table = jnp.where(rank[:, None, :] == slot + half * HALF, share_of[:, None, :], 0.0)
+        table = table.reshape(experts * HALF, count).T
+        upper = table.astype(jnp.bfloat16)
+        lower = (table - upper.astype(jnp.float32)).astype(jnp.bfloat16)
+        weigh[half, 0:count, :] = upper
+        weigh[half, count : 2 * count, :] = lower
 
 
 def project_kernel(rows, gate, gate_other, up, up_other, sums):
@@ -90,20 +90,21 @@
 
 def down_kernel(hidden, down, out):
     pairs, _, depth, width = hidden.shape
-    for pair in range(pairs):
-        both = hidden[pair].reshape(2 * depth, width)
-        value = lax.dot_general(both, down[...], NT, preferred_element_type=jnp.float32)
-        for j in range(depth // HALF):
-            first = value[j * HALF : (j + 1) * HALF]
-            second = value[depth + j * HALF : depth + (j + 1) * HALF]
-            block = jnp.concatenate([first, second], axis=0)
-            out[pair * (depth // HALF) + j] = block.astype(jnp.bfloat16)
+    features = down.shape[0]
+    for half in range(2):
+        rows = hidden[:, half].reshape(pairs * depth, width)
+        value = lax.dot_general(rows, down[...], NT, preferred_element_type=jnp.float32)
+        out[:, half * features : (half + 1) * features] = value.astype(jnp.bfloat16)
 
 
 def mix_kernel(weigh, values, mixed):
-    total = jnp.dot(weigh[...], values[...], preferred_element_type=jnp.float32)
-    count = total.shape[0] // 2
-    mixed[...] = (total[:count] + total[count:]).T.astype(jnp.bfloat16)
+    features, count = mixed.shape
+    total = jnp.zeros((features, count), jnp.float32)
+    for half in range(2):
+        part = jnp.dot(weigh[half], values[...], preferred_element_type=jnp.float32)
+        part = (part[:count] + part[count:]).T
+        total = total + part[half * features : (half + 1) * features]
+    mixed[...] = total.astype(jnp.bfloat16)
 
 
 def cost(flops, moved):
@@ -166,7 +167,7 @@
     )
     weigh = pl.pallas_call(
         weigh_kernel,
-        out_shape=jax.ShapeDtypeStruct((2 * count, experts * SLOTS), bf16),
+        out_shape=jax.ShapeDtypeStruct((2, 2 * count, experts * HALF), bf16),
         in_specs=[VMEM] * 4,
         out_specs=VMEM,
         compiler_params=LIMIT,
@@ -187,20 +188,20 @@
     all_hidden = all_hidden.reshape(planes, 2, part, units)
 
     at_once = 2
-    blocks = at_once * part // HALF
     back = pl.pallas_call(
         down_kernel,
         grid=(planes // at_once,),
-        out_shape=jax.ShapeDtypeStruct((groups, SLOTS, features), bf16),
+        out_shape=jax.ShapeDtypeStruct((depth, 2 * features), bf16),
         in_specs=[
             pl.BlockSpec((at_once, 2, part, units), lambda i: (i, 0, 0, 0)),
             pl.BlockSpec((features, units), lambda i: (0, 0)),
         ],
-        out_specs=pl.BlockSpec((blocks, SLOTS, features), lambda i: (i, 0, 0)),
+        out_specs=pl.BlockSpec((at_once * part, 2 * features), lambda i: (i, 0)),
         compiler_params=LIMIT,
         cost_estimate=cost(2 * 2 * depth * units * features, 6000000),
         name="project_out",
     )(all_hidden, down)
+    back = back.reshape(groups, HALF, 2 * features)
     values = lax.all_to_all(back, "ep", split_axis=0, concat_axis=0, tiled=True)
     mixed = pl.pallas_call(
         mix_kernel,
@@ -208,9 +209,9 @@
         in_specs=[VMEM] * 2,
         out_specs=VMEM,
         compiler_params=LIMIT,
-        cost_estimate=cost(4 * count * experts * SLOTS * features, 3000000),
+        cost_estimate=cost(8 * count * experts * HALF * 2 * features, 3000000),
         name="mix_rows",
-    )(weigh, values.reshape(experts * SLOTS, features))
+    )(weigh, values.reshape(experts * HALF, 2 * features))
     return mixed.T
 
 

time: 227 us -> 226 us (level)
  Pallas kernels: 13.2 us -> 22.7 us
  local copies, waits for them, and re-layouts: 10 us -> 3.81 us
  waiting for transfers between devices: 163 us -> 159 us
    unnamed x34 -> x12, local copies, waits for them, and re-layouts: 10 us -> 3.81 us
    all_to_all x1, waiting for transfers between devices: 38.6 us -> 33.3 us  [on_device(): values = lax.all_to_all(back, 'ep', split_axis=0, concat_axis=0, tiled=True)]
  transfers between devices with their start and end apart: 7 -> 7, of which waited for: 7 -> 7; matrix products, arithmetic and copies ran while one was open for 0% -> 0% of each run, Pallas kernels for 0% -> 1%
where the time goes in v2:
time: 226 us; the launch traced here: 225 us
  waiting for transfers between devices  159 us (70%)
  starting transfers between devices  26.4 us (12%)
  Pallas kernels  22.7 us (10%)
  between operations  13.5 us (6%)
  local copies, waits for them, and re-layouts  3.81 us (2%)
    reduce_scatter x1, waiting for transfers between devices, on_device(): lax.psum_scatter(sums, 'dp', scatter_dimension=0, tiled=True, axis_index_...  48 us
    all_gather x1, waiting for transfers between devices, on_device(): all_hidden = lax.all_gather(hidden, 'dp', axis=0, tiled=True)  46.6 us
    all_to_all x1, waiting for transfers between devices, on_device(): values = lax.all_to_all(back, 'ep', split_axis=0, concat_axis=0, tiled=True)  33.3 us
    all_to_all x1, waiting for transfers between devices, on_device(): lax.all_to_all(send.reshape(groups, HALF, 2 * features), 'ep', split_axis...  27.9 us
    all_to_all x1, starting transfers between devices, on_device(): lax.all_to_all(send.reshape(groups, HALF, 2 * features), 'ep', split_axis...  9.73 us
    all_to_all x1, starting transfers between devices, on_device(): values = lax.all_to_all(back, 'ep', split_axis=0, concat_axis=0, tiled=True)  9.28 us
    pallas_call x1, Pallas kernels, on_device(): pl.pallas_call(project_kernel, grid=(units // STRIP,), out_shape=jax.Shap...  7.35 us
    pallas_call x1, Pallas kernels, on_device(): pl.pallas_call(down_kernel, grid=(planes // at_once,), out_shape=jax.Shap...  5.78 us
  transfers between devices with their start and end apart: 7, of which 7 were waited for; matrix products, arithmetic and copies ran while one was open for 0% of the time, Pallas kernels for 1%

profile of v2, /device:TPU:9, one launch (start us, length us, event | category | flops | bytes accessed | tf_op | source)
XLA Modules:
  0.0 225.0 jit_solution(18188586149236056735)
XLA Ops:
  6.5 2.6 %collective-permute-start = (bf16[448,128]{1,0:T(8,128)(2,1)}, bf16[448,128]{1,0:T(8,128)(2,1)S(1)}, u32[]{:S(2)}, u32[]{:S(2)}) collective-permute-start(bf16[448,128]{1,0:T(8,128)(2,1)} %bitcast.23), channel_id=1, source_target_pairs={{0,1},{1,0},{2,3},{3,2},{4,5},{5,4},{6,7},{7,6},{8,9},{9,8},{10,11... | collective-permute-start | bytes 344072 | tf_op jit(solution)/shard_map/ppermute | solution.py:136
  9.1 1.1 collective-permute-done.tokens_other
  10.3 0.0 copy-start.2
  10.3 0.6 copy-done.2
  10.9 2.7 %pick_rows.1 = bf16[768,896]{1,0:T(8,128)(2,1)} custom-call(s32[1]{0:T(128)} %bitcast.4.core, s32[8,128]{1,0:T(8,128)} %bitcast.25, s32[1,32]{1,0:T(1,128)} %bitcast.28, s32[1,32]{1,0:T(1,128)} %bitcast.30, bf16[448,128]{1,0:T(8,128)(2,1)} %bitcast.24, bf16[448,128]{1,0:T(8,128)(2,1)} %copy-done.2), custom_call_target="tpu_custom_call" | custom-call | flops 176160768 | bytes 2000000 | tf_op jit(solution)/shard_map/pick_rows/pallas_call | solution.py:140
  13.7 0.0 copy-start.3
  13.7 0.0 copy-start.4
  13.7 9.7 %all-to-all-start = ((bf16[32,24,896]{2,1,0:T(8,128)(2,1)}), bf16[32,24,896]{2,1,0:T(8,128)(2,1)S(1)}, u32[]{:S(2)}, u32[]{:S(2)}) async-start(bf16[32,24,896]{2,1,0:T(8,128)(2,1)} %bitcast.17), calls=%async_computation | async-start | bytes 2752512 | tf_op jit(solution)/shard_map/all_to_all | solution.py:149
  23.4 0.0 reduce-scatter.2.cloned.1.call-start
  23.5 0.0 copy-done.3
  23.5 2.8 %collective-permute-start.1 = (bf16[448,1024]{1,0:T(8,128)(2,1)S(1)}, bf16[448,1024]{1,0:T(8,128)(2,1)S(1)}, u32[]{:S(2)}, u32[]{:S(2)}) collective-permute-start(bf16[448,1024]{1,0:T(8,128)(2,1)S(1)} %bitcast.33), channel_id=1, source_target_pairs={{0,1},{1,0},{2,3},{3,2},{4,5},{5,4},{6,7},{7,6},{8,9},{9,8},{10,11... | collective-permute-start | bytes 2752520 | tf_op jit(solution)/shard_map/ppermute | solution.py:137
  26.3 0.0 copy-done.4
  26.3 1.9 collective-permute-start.2
  28.2 0.1 collective-permute-done.1.gate_other
  28.4 0.0 copy-start.5
  28.4 1.0 copy-done.5
  29.4 1.5 collective-permute-done.2.up_other
  30.8 27.9 %all-to-all-done = bf16[32,24,896]{2,1,0:T(8,128)(2,1)S(1)} async-done(((bf16[32,24,896]{2,1,0:T(8,128)(2,1)}), bf16[32,24,896]{2,1,0:T(8,128)(2,1)S(1)}, u32[]{:S(2)}, u32[]{:S(2)}) %all-to-all-start) | async-done | bytes 1376288 | tf_op jit(solution)/shard_map/all_to_all | solution.py:149
  58.7 0.0 copy-start
  58.7 1.1 copy-done
  59.8 7.4 %project_in.1 = bf16[768,2048]{1,0:T(8,128)(2,1)} custom-call(bf16[768,896]{1,0:T(8,128)(2,1)} %bitcast.20, bf16[448,1024]{1,0:T(8,128)(2,1)} %bitcast.32, bf16[448,1024]{1,0:T(8,128)(2,1)} %copy-done.5, bf16[448,1024]{1,0:T(8,128)(2,1)} %bitcast.34, bf16[448,1024]{1,0:T(8,128)(2,1)} %collective-permute-done.2.up_other), custom_call_target="tpu_custom_call" | custom-call | flops 2818572288 | bytes 8000000 | tf_op jit(solution)/shard_map/project_in/pallas_call | solution.py:155
  67.2 0.0 reduce-scatter.2.cloned.1.call-update
  67.2 0.0 all-gather.2.cloned.1.call-start
  67.2 48.0 %reduce-scatter.2.cloned.1.call-done.sums = bf16[96,2048]{1,0:T(8,128)(2,1)} async-done(((bf16[768,2048]{1,0:T(8,128)(2,1)}), bf16[96,2048]{1,0:T(8,128)(2,1)}) %reduce-scatter.2.cloned.1.call-update) | async-done | bytes 393232 | tf_op jit(solution)/shard_map/reduce_scatter | solution.py:165
  115.3 1.8 hidden_units.1
  117.1 0.0 all-gather.2.cloned.1.call-update
  117.1 46.6 %all-gather.2.cloned.1.call-done = bf16[1536,1024]{1,0:T(8,128)(2,1)} async-done(((bf16[96,1024]{1,0:T(8,128)(2,1)}), bf16[1536,1024]{1,0:T(8,128)(2,1)}) %all-gather.2.cloned.1.call-update) | async-done | bytes 3145744 | tf_op jit(solution)/shard_map/all_gather | solution.py:187
  163.6 5.8 %project_out.1 = bf16[768,896]{1,0:T(8,128)(2,1)} custom-call(bf16[8,2,96,1024]{3,2,1,0:T(8,128)(2,1)} %bitcast.19, bf16[448,1024]{1,0:T(8,128)(2,1)} %bitcast.22), custom_call_target="tpu_custom_call" | custom-call | flops 1409286144 | bytes 6000000 | tf_op jit(solution)/shard_map/project_out/pallas_call | solution.py:191
  169.4 9.3 %all-to-all-start.1 = ((bf16[32,24,896]{2,1,0:T(8,128)(2,1)}), bf16[32,24,896]{2,1,0:T(8,128)(2,1)S(1)}, u32[]{:S(2)}, u32[]{:S(2)}) async-start(bf16[32,24,896]{2,1,0:T(8,128)(2,1)} %bitcast.18), calls=%async_computation.2 | async-start | bytes 2752512 | tf_op jit(solution)/shard_map/all_to_all | solution.py:205
  178.7 2.0 weigh_table.1.weigh
  180.8 33.3 %all-to-all-done.1 = bf16[32,24,896]{2,1,0:T(8,128)(2,1)S(1)} async-done(((bf16[32,24,896]{2,1,0:T(8,128)(2,1)}), bf16[32,24,896]{2,1,0:T(8,128)(2,1)S(1)}, u32[]{:S(2)}, u32[]{:S(2)}) %all-to-all-start.1) | async-done | bytes 1376288 | tf_op jit(solution)/shard_map/all_to_all | solution.py:205
  214.1 0.0 copy-start.1
  214.1 1.1 copy-done.1
  215.2 3.0 %mix_rows.1 = bf16[448,128]{1,0:T(8,128)(2,1)} custom-call(bf16[2,256,768]{2,1,0:T(8,128)(2,1)} %weigh_table.1.weigh, bf16[768,896]{1,0:T(8,128)(2,1)} %bitcast.21), custom_call_target="tpu_custom_call" | custom-call | flops 704643072 | bytes 3000000 | tf_op jit(solution)/shard_map/mix_rows/pallas_call | solution.py:206
Async XLA Ops:
  6.5 3.7 %collective-permute-start = (bf16[448,128]{1,0:T(8,128)(2,1)}, bf16[448,128]{1,0:T(8,128)(2,1)S(1)}, u32[]{:S(2)}, u32[]{:S(2)}) collective-permute-start(bf16[448,128]{1,0:T(8,128)(2,1)} %bitcast.23), channel_id=1, source_target_pairs={{0,1},{1,0},{2,3},{3,2},{4,5},{5,4},{6,7},{7,6},{8,9},{9,8},{10,11... | collective-permute-start | bytes 344072 | tf_op jit(solution)/shard_map/ppermute | solution.py:136
  10.3 0.6 copy-start.2
  13.7 9.8 %copy-start.3 = (bf16[1,448,1024]{2,1,0:T(8,128)(2,1)S(1)}, bf16[1,448,1024]{2,1,0:T(8,128)(2,1)}, u32[]{:S(2)}) copy-start(bf16[1,448,1024]{2,1,0:T(8,128)(2,1)} %param.13) | copy-start | bytes 2752516
  13.7 12.6 %copy-start.4 = (bf16[1,448,1024]{2,1,0:T(8,128)(2,1)S(1)}, bf16[1,448,1024]{2,1,0:T(8,128)(2,1)}, u32[]{:S(2)}) copy-start(bf16[1,448,1024]{2,1,0:T(8,128)(2,1)} %param.14) | copy-start | bytes 2752516
  13.7 45.1 %all-to-all-start = ((bf16[32,24,896]{2,1,0:T(8,128)(2,1)}), bf16[32,24,896]{2,1,0:T(8,128)(2,1)S(1)}, u32[]{:S(2)}, u32[]{:S(2)}) async-start(bf16[32,24,896]{2,1,0:T(8,128)(2,1)} %bitcast.17), calls=%async_computation | async-start | bytes 2752512 | tf_op jit(solution)/shard_map/all_to_all | solution.py:149
  23.4 91.9 %reduce-scatter.2.cloned.1.call-start = ((), (), s32[]{:S(2)}) async-start(), calls=%async_computation.3 | async-start | bytes 3538944 | tf_op jit(solution)/shard_map/reduce_scatter | solution.py:165
  23.5 4.9 %collective-permute-start.1 = (bf16[448,1024]{1,0:T(8,128)(2,1)S(1)}, bf16[448,1024]{1,0:T(8,128)(2,1)S(1)}, u32[]{:S(2)}, u32[]{:S(2)}) collective-permute-start(bf16[448,1024]{1,0:T(8,128)(2,1)S(1)} %bitcast.33), channel_id=1, source_target_pairs={{0,1},{1,0},{2,3},{3,2},{4,5},{5,4},{6,7},{7,6},{8,9},{9,8},{10,11... | collective-permute-start | bytes 2752520 | tf_op jit(solution)/shard_map/ppermute | solution.py:137
  26.3 4.5 %collective-permute-start.2 = (bf16[448,1024]{1,0:T(8,128)(2,1)S(1)}, bf16[448,1024]{1,0:T(8,128)(2,1)}, u32[]{:S(2)}, u32[]{:S(2)}) collective-permute-start(bf16[448,1024]{1,0:T(8,128)(2,1)S(1)} %bitcast.35), channel_id=1, source_target_pairs={{0,1},{1,0},{2,3},{3,2},{4,5},{5,4},{6,7},{7,6},{8,9},{9,8},{10,11... | collective-permute-start | bytes 2752520 | tf_op jit(solution)/shard_map/ppermute | solution.py:138
  28.4 1.0 copy-start.5
  58.7 1.1 copy-start
  67.2 96.5 %all-gather.2.cloned.1.call-start = ((), (), s32[]{:S(2)}) async-start(), calls=%async_computation.4 | async-start | bytes 3342336 | tf_op jit(solution)/shard_map/all_gather | solution.py:187
  169.4 44.7 %all-to-all-start.1 = ((bf16[32,24,896]{2,1,0:T(8,128)(2,1)}), bf16[32,24,896]{2,1,0:T(8,128)(2,1)S(1)}, u32[]{:S(2)}, u32[]{:S(2)}) async-start(bf16[32,24,896]{2,1,0:T(8,128)(2,1)} %bitcast.18), calls=%async_computation.2 | async-start | bytes 2752512 | tf_op jit(solution)/shard_map/all_to_all | solution.py:205
  214.1 1.1 copy-start.1
Sparse Core Ops, SparseCore 0:
  67.3 47.9 reduce-scatter.1
  117.4 46.2 all-gather.1

commit v3 on v2

--- a/solution.py
+++ b/solution.py
@@ -1,5 +1,3 @@
-import functools
-
 import jax
 import jax.numpy as jnp
 from jax import lax
@@ -8,12 +6,15 @@
 from jax.sharding import PartitionSpec as P
 
 HALF = 24
+PIECES = 4
 STRIP = 256
 
 VMEM = pl.BlockSpec(memory_space=pltpu.VMEM)
 SMEM = pl.BlockSpec(memory_space=pltpu.SMEM)
 NT = (((1,), (1,)), ((), ()))
-LIMIT = pltpu.CompilerParams(vmem_limit_bytes=60 * 1024 * 1024)
+HBM = pl.BlockSpec(memory_space=pltpu.HBM)
+LIMIT = pltpu.CompilerParams(vmem_limit_bytes=40 * 1024 * 1024)
+LARGE = pltpu.CompilerParams(vmem_limit_bytes=60 * 1024 * 1024)
 
 
 def column(row, experts):
@@ -42,15 +43,37 @@
     return jnp.where((named > 0.0) & (before < limit), before, -1.0)
 
 
-def pick_kernel(core, routes, capacity, spill, tokens, tokens_other, rows):
-    rank = ranks(routes[...], capacity[...], spill[...])
+def table_kernel(core, routes, capacity, spill, tokens, pick, kept, named, limits, sem):
+    copies = [
+        pltpu.make_async_copy(routes, named, sem.at[0]),
+        pltpu.make_async_copy(capacity, limits.at[0:1], sem.at[1]),
+        pltpu.make_async_copy(spill, limits.at[1:2], sem.at[2]),
+        pltpu.make_async_copy(tokens, kept, sem.at[3]),
+    ]
+    for copy in copies:
+        copy.start()
+    for copy in copies[:3]:
+        copy.wait()
+    rank = ranks(named[...], limits[0:1, :], limits[1:2, :])
     experts, count = rank.shape
     slot = lax.broadcasted_iota(jnp.int32, (experts, HALF, count), 1) + core[0] * HALF
-    pick = jnp.where(rank[:, None, :] == slot.astype(jnp.float32), 1.0, 0.0)
-    pick = pick.reshape(experts * HALF, count).astype(jnp.bfloat16)
+    chosen = jnp.where(rank[:, None, :] == slot.astype(jnp.float32), 1.0, 0.0)
+    pick[...] = chosen.reshape(experts * HALF, count).astype(jnp.bfloat16)
+    copies[3].wait()
+
+
+def pick_kernel(pick, tokens, tokens_other, rows, held, sem):
     features = jnp.concatenate([tokens[...], tokens_other[...]], axis=0)
-    picked = lax.dot_general(pick, features, NT, preferred_element_type=jnp.float32)
-    rows[...] = picked.astype(jnp.bfloat16)
+    piece = rows.shape[0] // PIECES
+    copies = []
+    for k in range(PIECES):
+        at = pl.ds(k * piece, piece)
+        picked = lax.dot_general(pick[at, :], features, NT, preferred_element_type=jnp.float32)
+        held[at, :] = picked.astype(jnp.bfloat16)
+        copies.append(pltpu.make_async_copy(held.at[at], rows.at[at], sem.at[k]))
+        copies[-1].start()
+    for copy in copies:
+        copy.wait()
 
 
 def weigh_kernel(routes, weights, capacity, spill, weigh):
@@ -72,11 +95,47 @@
         weigh[half, count : 2 * count, :] = lower
 
 
-def project_kernel(rows, gate, gate_other, up, up_other, sums):
-    for at, (own, other) in enumerate(((gate, gate_other), (up, up_other))):
-        weight = jnp.concatenate([own[...], other[...]], axis=0)
-        part = jnp.dot(rows[...], weight, preferred_element_type=jnp.float32)
-        sums[:, at * STRIP : (at + 1) * STRIP] = part.astype(jnp.bfloat16)
+def project_kernel(rows, gate, gate_other, up, up_other, sums, held, weight, result, came, went):
+    depth, width = held.shape
+    features = width // 2
+    strips = gate.shape[1] // STRIP
+    piece = depth // PIECES
+    loads = []
+    for k in range(PIECES):
+        at = pl.ds(k * piece, piece)
+        loads.append(pltpu.make_async_copy(rows.at[at], held.at[at], came.at[k]))
+        loads[-1].start()
+    sources = ((gate, 0, 0), (gate_other, 1, 0), (up, 0, 1), (up_other, 1, 1))
+    fetched = []
+    for strip in range(strips):
+        for n, (source, low, kind) in enumerate(sources):
+            copy = pltpu.make_async_copy(
+                source.at[:, pl.ds(strip * STRIP, STRIP)],
+                weight.at[strip, kind, pl.ds(low * features, features)],
+                came.at[PIECES + strip * len(sources) + n],
+            )
+            copy.start()
+            fetched.append(copy)
+    for copy in loads:
+        copy.wait()
+    stores = []
+    for strip in range(strips):
+        for copy in fetched[strip * len(sources) : (strip + 1) * len(sources)]:
+            copy.wait()
+        for kind in range(2):
+            part = jnp.dot(held[...], weight[strip, kind], preferred_element_type=jnp.float32)
+            result[strip, :, kind * STRIP : (kind + 1) * STRIP] = part.astype(jnp.bfloat16)
+        for k in range(PIECES):
+            at = pl.ds(k * piece, piece)
+            copy = pltpu.make_async_copy(
+                result.at[strip, at],
+                sums.at[at, pl.ds(strip * 2 * STRIP, 2 * STRIP)],
+                went.at[strip * PIECES + k],
+            )
+            copy.start()
+            stores.append(copy)
+    for copy in stores:
+        copy.wait()
 
 
 def hidden_kernel(sums, hidden):
@@ -88,13 +147,42 @@
         hidden[:, STRIP * strip : STRIP * (strip + 1)] = value.astype(jnp.bfloat16)
 
 
-def down_kernel(hidden, down, out):
-    pairs, _, depth, width = hidden.shape
+def down_kernel(places, parts, down, out, held, sem, first):
+    depth = held.shape[1]
     features = down.shape[0]
-    for half in range(2):
-        rows = hidden[:, half].reshape(pairs * depth, width)
-        value = lax.dot_general(rows, down[...], NT, preferred_element_type=jnp.float32)
-        out[:, half * features : (half + 1) * features] = value.astype(jnp.bfloat16)
+    copies = []
+    for part, chips in parts:
+        value = lax.dot_general(part, down[...], NT, preferred_element_type=jnp.float32)
+        value = value.astype(jnp.bfloat16)
+        for n, chip in enumerate(chips):
+            low = value[2 * n * depth : (2 * n + 1) * depth]
+            high = value[(2 * n + 1) * depth : (2 * n + 2) * depth]
+            swapped = places[1, chip] == 1
+            slot = chip - first
+            held[slot, :, 0:features] = jnp.where(swapped, high, low)
+            held[slot, :, features : 2 * features] = jnp.where(swapped, low, high)
+            place = pl.multiple_of(places[0, chip] * depth, depth)
+            copies.append(
+                pltpu.make_async_copy(held.at[slot], out.at[pl.ds(place, depth)], sem.at[slot])
+            )
+            copies[-1].start()
+    for copy in copies:
+        copy.wait()
+
+
+def early_kernel(places, own, near, far, swapped_pair, down, out, held, sem):
+    rows = jnp.concatenate([own[...], near[...], far[...]], axis=0)
+    parts = ((rows, (0, 1, 2)), (swapped_pair[...], (3, 4)))
+    down_kernel(places, parts, down, out, held, sem, 0)
+
+
+def late_kernel(places, third, fourth, swapped, down, filled, out, held, sem):
+    del filled
+    depth = fourth.shape[0]
+    rows = jnp.concatenate([third[...], swapped[0 : 2 * depth]], axis=0)
+    last = jnp.concatenate([fourth[...], swapped[2 * depth : 3 * depth]], axis=0)
+    parts = ((rows, (5, 6)), (last, (7,)))
+    down_kernel(places, parts, down, out, held, sem, 5)
 
 
 def mix_kernel(weigh, values, mixed):
@@ -137,28 +225,55 @@
     gate_other = lax.ppermute(gate, "dp", swap)
     up_other = lax.ppermute(up, "dp", swap)
 
+    pick, kept_tokens = pl.pallas_call(
+        table_kernel,
+        out_shape=[
+            jax.ShapeDtypeStruct((experts * HALF, count), bf16),
+            jax.ShapeDtypeStruct((features, count), bf16),
+        ],
+        in_specs=[SMEM] + [HBM] * 4,
+        out_specs=[VMEM] * 2,
+        scratch_shapes=[
+            pltpu.VMEM(own_routes.shape, jnp.int32),
+            pltpu.VMEM((2, experts), jnp.int32),
+            pltpu.SemaphoreType.DMA((4,)),
+        ],
+        compiler_params=LIMIT,
+        cost_estimate=cost(2 * experts * count * count, 600000),
+        name="pick_table",
+    )(core, own_routes, cap_row, spill_row, own_tokens)
     send = pl.pallas_call(
         pick_kernel,
         out_shape=jax.ShapeDtypeStruct((experts * HALF, 2 * features), bf16),
-        in_specs=[SMEM] + [VMEM] * 5,
-        out_specs=VMEM,
+        in_specs=[VMEM] * 3,
+        out_specs=HBM,
+        scratch_shapes=[
+            pltpu.VMEM((experts * HALF, 2 * features), bf16),
+            pltpu.SemaphoreType.DMA((PIECES,)),
+        ],
         compiler_params=LIMIT,
         cost_estimate=cost(2 * experts * HALF * count * 2 * features, 2000000),
         name="pick_rows",
-    )(core, own_routes, cap_row, spill_row, own_tokens, tokens_other)
+    )(pick, kept_tokens, tokens_other)
     got = lax.all_to_all(
         send.reshape(groups, HALF, 2 * features), "ep", split_axis=0, concat_axis=0, tiled=True
     ).reshape(groups * HALF, 2 * features)
 
     depth = groups * HALF
-    wide = pl.BlockSpec((features, STRIP), lambda i: (0, i))
+    strips = units // STRIP
     sums = pl.pallas_call(
         project_kernel,
-        grid=(units // STRIP,),
         out_shape=jax.ShapeDtypeStruct((depth, 2 * units), bf16),
-        in_specs=[pl.BlockSpec((depth, 2 * features), lambda i: (0, 0))] + [wide] * 4,
-        out_specs=pl.BlockSpec((depth, 2 * STRIP), lambda i: (0, i)),
-        compiler_params=LIMIT,
+        in_specs=[HBM] * 5,
+        out_specs=HBM,
+        scratch_shapes=[
+            pltpu.VMEM((depth, 2 * features), bf16),
+            pltpu.VMEM((strips, 2, 2 * features, STRIP), bf16),
+            pltpu.VMEM((strips, depth, 2 * STRIP), bf16),
+            pltpu.SemaphoreType.DMA((PIECES + 4 * strips,)),
+            pltpu.SemaphoreType.DMA((strips * PIECES,)),
+        ],
+        compiler_params=LARGE,
         cost_estimate=cost(2 * depth * 2 * features * 2 * units, 8000000),
         name="project_in",
     )(got, gate, gate_other, up, up_other)
@@ -184,23 +299,56 @@
         cost_estimate=cost(8 * part * units, 600000),
         name="hidden_units",
     )(summed)
-    all_hidden = lax.all_gather(hidden, "dp", axis=0, tiled=True)
-    all_hidden = all_hidden.reshape(planes, 2, part, units)
-
-    at_once = 2
+
+    def flow(rows, hops):
+        steps = [
+            (2 * z + c, 2 * ((z + (hops, -hops)[c]) % planes) + c)
+            for z in range(planes)
+            for c in range(2)
+        ]
+        return lax.ppermute(rows, "dp", steps)
+
+    own = jnp.concatenate([hidden, lax.ppermute(hidden, "dp", swap)], axis=0)
+    near, far = flow(own, 1), flow(own, 2)
+    third, fourth = flow(far, 1), flow(far[:part], 2)
+    swapped_pair = lax.ppermute(jnp.concatenate([near, far], axis=0), "dp", swap)
+    swapped_last = lax.ppermute(jnp.concatenate([third, fourth], axis=0), "dp", swap)
+    plane = lax.axis_index("dp") // 2
+    sense = 2 * core[0] - 1
+    chips = [0, sense, 2 * sense, -sense, -2 * sense, 3 * sense, -3 * sense, 4]
+    orders = [core[0]] * 3 + [1 - core[0]] * 2 + [core[0], 1 - core[0], core[0]]
+    places = jnp.stack(
+        [jnp.stack([(plane + chip + planes) % planes for chip in chips]), jnp.stack(orders)]
+    ).astype(jnp.int32)
+    back_shape = jax.ShapeDtypeStruct((depth, 2 * features), bf16)
+
+    def scratch(held):
+        return [
+            pltpu.VMEM((held, part, 2 * features), bf16),
+            pltpu.SemaphoreType.DMA((held,)),
+        ]
+
     back = pl.pallas_call(
-        down_kernel,
-        grid=(planes // at_once,),
-        out_shape=jax.ShapeDtypeStruct((depth, 2 * features), bf16),
-        in_specs=[
-            pl.BlockSpec((at_once, 2, part, units), lambda i: (i, 0, 0, 0)),
-            pl.BlockSpec((features, units), lambda i: (0, 0)),
-        ],
-        out_specs=pl.BlockSpec((at_once * part, 2 * features), lambda i: (i, 0)),
-        compiler_params=LIMIT,
-        cost_estimate=cost(2 * 2 * depth * units * features, 6000000),
-        name="project_out",
-    )(all_hidden, down)
+        early_kernel,
+        out_shape=back_shape,
+        in_specs=[SMEM] + [VMEM] * 5,
+        out_specs=HBM,
+        scratch_shapes=scratch(5),
+        compiler_params=LIMIT,
+        cost_estimate=cost(20 * part * units * features, 4000000),
+        name="project_out_early",
+    )(places, own, near, far, swapped_pair, down)
+    back = pl.pallas_call(
+        late_kernel,
+        out_shape=back_shape,
+        in_specs=[SMEM] + [VMEM] * 4 + [HBM],
+        out_specs=HBM,
+        scratch_shapes=scratch(3),
+        input_output_aliases={5: 0},
+        compiler_params=LIMIT,
+        cost_estimate=cost(12 * part * units * features, 4000000),
+        name="project_out_late",
+    )(places, third, fourth, swapped_last, down, back)
     back = back.reshape(groups, HALF, 2 * features)
     values = lax.all_to_all(back, "ep", split_axis=0, concat_axis=0, tiled=True)
     mixed = pl.pallas_call(

time: 226 us -> 215 us (0.951)
  waiting for transfers between devices: 159 us -> 124 us
  starting transfers between devices: 26.4 us -> 52.6 us
  Pallas kernels: 22.7 us -> 15.7 us
  local copies, waits for them, and re-layouts: 3.81 us -> 6.14 us
    all_gather x1 -> x0, waiting for transfers between devices: 46.6 us -> none  [on_device(): all_hidden = lax.all_gather(hidden, 'dp', axis=0, tiled=True)]
    ppermute x0 -> x7, starting transfers between devices: none -> 25.6 us  [the longest x4 12.8 us: flow(): return lax.ppermute(rows, 'dp', steps)]
    ppermute x0 -> x7, waiting for transfers between devices: none -> 10.7 us  [the longest x4 9.62 us: flow(): return lax.ppermute(rows, 'dp', steps)]
    unnamed x12 -> x28, local copies, waits for them, and re-layouts: 3.81 us -> 5.95 us
    pallas_call x2 -> x4, Pallas kernels: 13.1 us -> 12.3 us  [the longest x1 6.74 us: on_device(): pl.pallas_call(project_kernel, out_shape=jax.ShapeDtypeStruct((depth, 2 *...]
  transfers between devices with their start and end apart: 7 -> 13, of which waited for: 7 -> 8; matrix products, arithmetic and copies ran while one was open for 0% -> 1% of each run, Pallas kernels for 1% -> 2%
where the time goes in v3:
time: 215 us; the launch traced here: 214 us
  waiting for transfers between devices  124 us (58%)
  starting transfers between devices  52.6 us (24%)
  Pallas kernels  15.7 us (7%)
  between operations  13.9 us (6%)
  local copies, waits for them, and re-layouts  6.14 us (3%)
    reduce_scatter x1, waiting for transfers between devices, on_device(): lax.psum_scatter(sums, 'dp', scatter_dimension=0, tiled=True, axis_index_...  48.1 us
    all_to_all x1, waiting for transfers between devices, on_device(): values = lax.all_to_all(back, 'ep', split_axis=0, concat_axis=0, tiled=True)  35 us
    all_to_all x1, waiting for transfers between devices, on_device(): lax.all_to_all(send.reshape(groups, HALF, 2 * features), 'ep', split_axis...  28.4 us
    ppermute x4, starting transfers between devices, flow(): return lax.ppermute(rows, 'dp', steps)  12.8 us
    all_to_all x1, starting transfers between devices, on_device(): values = lax.all_to_all(back, 'ep', split_axis=0, concat_axis=0, tiled=True)  10.2 us
    all_to_all x1, starting transfers between devices, on_device(): lax.all_to_all(send.reshape(groups, HALF, 2 * features), 'ep', split_axis...  9.75 us
    ppermute x4, waiting for transfers between devices, flow(): return lax.ppermute(rows, 'dp', steps)  9.62 us
    pallas_call x1, Pallas kernels, on_device(): pl.pallas_call(project_kernel, out_shape=jax.ShapeDtypeStruct((depth, 2 *...  6.74 us
  transfers between devices with their start and end apart: 13, of which 8 were waited for; matrix products, arithmetic and copies ran while one was open for 1% of the time, Pallas kernels for 2%

profile of v3, /device:TPU:9, one launch (start us, length us, event | category | flops | bytes accessed | tf_op | source)
XLA Modules:
  0.0 214.0 jit_solution(3696513178138106697)
XLA Ops:
  6.5 2.6 %collective-permute-start = (bf16[448,128]{1,0:T(8,128)(2,1)}, bf16[448,128]{1,0:T(8,128)(2,1)S(1)}, u32[]{:S(2)}, u32[]{:S(2)}) collective-permute-start(bf16[448,128]{1,0:T(8,128)(2,1)} %bitcast.30), channel_id=1, source_target_pairs={{0,1},{1,0},{2,3},{3,2},{4,5},{5,4},{6,7},{7,6},{8,9},{9,8},{10,11... | collective-permute-start | bytes 344072 | tf_op jit(solution)/shard_map/ppermute | solution.py:224
  9.1 0.0 copy-start.2
  9.1 0.9 copy-done.2
  10.0 0.7 copy-done.3
  10.7 0.0 copy-start.6
  10.7 0.7 copy-done.6
  11.4 0.0 copy-start.8
  11.4 0.7 copy-done.8
  12.0 0.4 pick_table.1
  12.4 0.0 collective-permute-done.tokens_other
  12.4 1.4 pick_rows.1
  13.8 0.0 copy-start.11
  13.8 0.0 copy-start.12
  13.8 9.7 %all-to-all-start = ((bf16[32,24,896]{2,1,0:T(8,128)(2,1)}), bf16[32,24,896]{2,1,0:T(8,128)(2,1)S(1)}, u32[]{:S(2)}, u32[]{:S(2)}) async-start(bf16[32,24,896]{2,1,0:T(8,128)(2,1)} %bitcast.17), calls=%async_computation | async-start | bytes 2752512 | tf_op jit(solution)/shard_map/all_to_all | solution.py:258
  23.6 0.0 reduce-scatter.2.cloned.1.call-start
  23.6 0.0 copy-done.11
  23.7 2.5 %collective-permute-start.1 = (bf16[448,1024]{1,0:T(8,128)(2,1)S(1)}, bf16[448,1024]{1,0:T(8,128)(2,1)S(1)}, u32[]{:S(2)}, u32[]{:S(2)}) collective-permute-start(bf16[448,1024]{1,0:T(8,128)(2,1)S(1)} %bitcast.43), channel_id=1, source_target_pairs={{0,1},{1,0},{2,3},{3,2},{4,5},{5,4},{6,7},{7,6},{8,9},{9,8},{10,11... | collective-permute-start | bytes 2752520 | tf_op jit(solution)/shard_map/ppermute | solution.py:225
  26.1 0.0 copy-done.12
  26.1 1.9 collective-permute-start.2
  28.1 0.1 collective-permute-done.1.gate_other
  28.2 0.0 copy-start.13
  28.2 0.9 copy-done.13
  29.2 1.5 collective-permute-done.2.up_other
  30.6 28.4 %all-to-all-done = bf16[32,24,896]{2,1,0:T(8,128)(2,1)S(1)} async-done(((bf16[32,24,896]{2,1,0:T(8,128)(2,1)}), bf16[32,24,896]{2,1,0:T(8,128)(2,1)S(1)}, u32[]{:S(2)}, u32[]{:S(2)}) %all-to-all-start) | async-done | bytes 1376288 | tf_op jit(solution)/shard_map/all_to_all | solution.py:258
  59.1 1.1 copy-done.10
  60.2 6.7 %project_in.1 = bf16[768,2048]{1,0:T(8,128)(2,1)} custom-call(bf16[768,896]{1,0:T(8,128)(2,1)} %bitcast.39, bf16[448,1024]{1,0:T(8,128)(2,1)} %bitcast.42, bf16[448,1024]{1,0:T(8,128)(2,1)} %copy-done.13, bf16[448,1024]{1,0:T(8,128)(2,1)} %bitcast.44, bf16[448,1024]{1,0:T(8,128)(2,1)} %collective-permute-done.2.up_other), custom_call_target="tpu_custom_call" | custom-call | flops 2818572288 | bytes 8000000 | tf_op jit(solution)/shard_map/project_in/pallas_call | solution.py:264
  66.9 0.0 reduce-scatter.2.cloned.1.call-update
  66.9 48.1 %reduce-scatter.2.cloned.1.call-done.sums = bf16[96,2048]{1,0:T(8,128)(2,1)} async-done(((bf16[768,2048]{1,0:T(8,128)(2,1)}), bf16[96,2048]{1,0:T(8,128)(2,1)}) %reduce-scatter.2.cloned.1.call-update) | async-done | bytes 393232 | tf_op jit(solution)/shard_map/reduce_scatter | solution.py:280
  115.0 1.0 copy-done.1
  116.0 0.1 hidden_units.1
  116.2 4.9 %collective-permute-start.3 = (bf16[96,1024]{1,0:T(8,128)(2,1)S(1)}, bf16[96,1024]{1,0:T(8,128)(2,1)S(1)}, u32[]{:S(2)}, u32[]{:S(2)}) collective-permute-start(bf16[96,1024]{1,0:T(8,128)(2,1)S(1)} %hidden_units.1), channel_id=1, source_target_pairs={{0,1},{1,0},{2,3},{3,2},{4,5},{5,4},{6,7},{7,6},{8,9},{9,8},{10,11... | collective-permute-start | bytes 589832 | tf_op jit(solution)/shard_map/ppermute | solution.py:311
  121.1 1.0 collective-permute-done.3
  122.1 3.2 %collective-permute-start.4 = (bf16[192,1024]{1,0:T(8,128)(2,1)S(1)}, bf16[192,1024]{1,0:T(8,128)(2,1)S(1)}, u32[]{:S(2)}, u32[]{:S(2)}) collective-permute-start(bf16[192,1024]{1,0:T(8,128)(2,1)S(1)} %pad_maximum_fusion.2.own), channel_id=1, source_target_pairs={{0,4},{1,13},{2,6},{3,15},{4,8},{5,1},{6,10},{7,3},{8,12},{9,5},{1... | collective-permute-start | bytes 1179656 | tf_op jit(solution)/shard_map/ppermute | solution.py:309
  125.3 3.5 %collective-permute-start.8 = (bf16[192,1024]{1,0:T(8,128)(2,1)S(1)}, bf16[192,1024]{1,0:T(8,128)(2,1)S(1)}, u32[]{:S(2)}, u32[]{:S(2)}) collective-permute-start(bf16[192,1024]{1,0:T(8,128)(2,1)S(1)} %pad_maximum_fusion.2.own), channel_id=1, source_target_pairs={{0,2},{1,15},{2,4},{3,1},{4,6},{5,3},{6,8},{7,5},{8,10},{9,7},{10,... | collective-permute-start | bytes 1179656 | tf_op jit(solution)/shard_map/ppermute | solution.py:309
  128.8 7.3 %collective-permute-done.4.far = bf16[192,1024]{1,0:T(8,128)(2,1)S(1)} collective-permute-done((bf16[192,1024]{1,0:T(8,128)(2,1)S(1)}, bf16[192,1024]{1,0:T(8,128)(2,1)S(1)}, u32[]{:S(2)}, u32[]{:S(2)}) %collective-permute-start.4) | collective-permute-done | bytes 393248 | tf_op jit(solution)/shard_map/ppermute | solution.py:309
  136.2 2.4 %collective-permute-start.5 = (bf16[192,1024]{1,0:T(8,128)(2,1)S(1)}, bf16[192,1024]{1,0:T(8,128)(2,1)S(1)}, u32[]{:S(2)}, u32[]{:S(2)}) collective-permute-start(bf16[192,1024]{1,0:T(8,128)(2,1)S(1)} %collective-permute-done.4.far), channel_id=1, source_target_pairs={{0,2},{1,15},{2,4},{3,1},{4,6},{5,3},{6,8},{7,5},{8,10},{9,7},{10,... | collective-permute-start | bytes 1179656 | tf_op jit(solution)/shard_map/ppermute | solution.py:309
  138.6 0.0 copy-start
  138.6 3.7 %collective-permute-start.6 = (bf16[96,1024]{1,0:T(8,128)(2,1)S(1)}, bf16[96,1024]{1,0:T(8,128)(2,1)S(1)}, u32[]{:S(2)}, u32[]{:S(2)}) collective-permute-start(bf16[96,1024]{1,0:T(8,128)(2,1)S(1)} %slice.4), channel_id=1, source_target_pairs={{0,4},{1,13},{2,6},{3,15},{4,8},{5,1},{6,10},{7,3},{8,12},{9,5},{1... | collective-permute-start | bytes 589832 | tf_op jit(solution)/shard_map/ppermute | solution.py:309
  142.4 0.0 collective-permute-done.8.near
  142.4 0.9 pad_maximum_fusion
  143.3 3.8 %collective-permute-start.9 = (bf16[384,1024]{1,0:T(8,128)(2,1)}, bf16[384,1024]{1,0:T(8,128)(2,1)S(1)}, u32[]{:S(2)}, u32[]{:S(2)}) collective-permute-start(bf16[384,1024]{1,0:T(8,128)(2,1)} %pad_maximum_fusion), channel_id=1, source_target_pairs={{0,1},{1,0},{2,3},{3,2},{4,5},{5,4},{6,7},{7,6},{8,9},{9,8},{10,11... | collective-permute-start | bytes 2359304 | tf_op jit(solution)/shard_map/ppermute | solution.py:314
  147.2 2.3 %collective-permute-done.6.fourth = bf16[96,1024]{1,0:T(8,128)(2,1)S(1)} collective-permute-done((bf16[96,1024]{1,0:T(8,128)(2,1)S(1)}, bf16[96,1024]{1,0:T(8,128)(2,1)S(1)}, u32[]{:S(2)}, u32[]{:S(2)}) %collective-permute-start.6) | collective-permute-done | bytes 196640 | tf_op jit(solution)/shard_map/ppermute | solution.py:309
  149.4 0.0 collective-permute-done.5.third
  149.5 0.9 pad_maximum_fusion.1
  150.3 4.0 %collective-permute-start.7 = (bf16[288,1024]{1,0:T(8,128)(2,1)}, bf16[288,1024]{1,0:T(8,128)(2,1)}, u32[]{:S(2)}, u32[]{:S(2)}) collective-permute-start(bf16[288,1024]{1,0:T(8,128)(2,1)} %pad_maximum_fusion.1), channel_id=1, source_target_pairs={{0,1},{1,0},{2,3},{3,2},{4,5},{5,4},{6,7},{7,6},{8,9},{9,8},{10,11... | collective-permute-start | bytes 1769480 | tf_op jit(solution)/shard_map/ppermute | solution.py:315
  154.5 0.1 stack.55
  154.6 0.1 stack.52
  154.7 0.0 collective-permute-done.9.swapped_pair
  154.7 0.0 copy-done
  154.7 2.5 %project_out_early.1.filled = bf16[768,896]{1,0:T(8,128)(2,1)} custom-call(s32[2,8]{1,0:T(2,128)S(1)} %pad_add_fusion.places, bf16[192,1024]{1,0:T(8,128)(2,1)S(1)} %pad_maximum_fusion.2.own, bf16[192,1024]{1,0:T(8,128)(2,1)S(1)} %collective-permute-done.8.near, bf16[192,1024]{1,0:T(8,128)(2,1)S(1)} %collective-permute-done.4.far, ...), custom_call_target="tpu_custom_call" | custom-call | flops 880803840 | bytes 4000000 | tf_op jit(solution)/shard_map/project_out_early/pallas_call | solution.py:331
  157.2 0.0 collective-permute-done.7.swapped
  157.3 2.7 %project_out_late.1 = bf16[768,896]{1,0:T(8,128)(2,1)} custom-call(s32[2,8]{1,0:T(2,128)S(1)} %pad_add_fusion.places, bf16[192,1024]{1,0:T(8,128)(2,1)S(1)} %collective-permute-done.5.third, bf16[96,1024]{1,0:T(8,128)(2,1)S(1)} %collective-permute-done.6.fourth, bf16[288,1024]{1,0:T(8,128)(2,1)} %collective-permute-done.7.swapped, ...), custom_call_target="tpu_custom_call", output_to_operand_aliasing={{}: (5, {})} | custom-call | flops 528482304 | bytes 4000000 | tf_op jit(solution)/shard_map/project_out_late/pallas_call | solution.py:341
  159.9 0.0 copy-start.4
  160.0 0.0 copy-start.5
  160.0 0.0 copy-start.7
  160.0 0.0 copy-start.9
  160.0 10.2 %all-to-all-start.1 = ((bf16[32,24,896]{2,1,0:T(8,128)(2,1)}), bf16[32,24,896]{2,1,0:T(8,128)(2,1)S(1)}, u32[]{:S(2)}, u32[]{:S(2)}) async-start(bf16[32,24,896]{2,1,0:T(8,128)(2,1)} %bitcast.24), calls=%async_computation.2 | async-start | bytes 2752512 | tf_op jit(solution)/shard_map/all_to_all | solution.py:353
  170.2 0.0 copy-done.4
  170.2 0.0 copy-done.5
  170.3 0.0 copy-done.7
  170.3 0.0 copy-done.9
  170.3 0.4 weigh_table.1.weigh
  170.7 35.0 %all-to-all-done.1 = bf16[32,24,896]{2,1,0:T(8,128)(2,1)S(1)} async-done(((bf16[32,24,896]{2,1,0:T(8,128)(2,1)}), bf16[32,24,896]{2,1,0:T(8,128)(2,1)S(1)}, u32[]{:S(2)}, u32[]{:S(2)}) %all-to-all-start.1) | async-done | bytes 1376288 | tf_op jit(solution)/shard_map/all_to_all | solution.py:353
  205.7 1.4 mix_rows.1
  (6 shorter events, 0.1 us)
Async XLA Ops:
  6.5 5.9 %collective-permute-start = (bf16[448,128]{1,0:T(8,128)(2,1)}, bf16[448,128]{1,0:T(8,128)(2,1)S(1)}, u32[]{:S(2)}, u32[]{:S(2)}) collective-permute-start(bf16[448,128]{1,0:T(8,128)(2,1)} %bitcast.30), channel_id=1, source_target_pairs={{0,1},{1,0},{2,3},{3,2},{4,5},{5,4},{6,7},{7,6},{8,9},{9,8},{10,11... | collective-permute-start | bytes 344072 | tf_op jit(solution)/shard_map/ppermute | solution.py:224
  9.1 0.9 copy-start.2
  10.0 0.7 copy-start.3
  10.7 0.7 copy-start.6
  11.4 0.7 copy-start.8
  13.8 9.8 %copy-start.11 = (bf16[1,448,1024]{2,1,0:T(8,128)(2,1)S(1)}, bf16[1,448,1024]{2,1,0:T(8,128)(2,1)}, u32[]{:S(2)}) copy-start(bf16[1,448,1024]{2,1,0:T(8,128)(2,1)} %param.13) | copy-start | bytes 2752516
  13.8 12.3 %copy-start.12 = (bf16[1,448,1024]{2,1,0:T(8,128)(2,1)S(1)}, bf16[1,448,1024]{2,1,0:T(8,128)(2,1)}, u32[]{:S(2)}) copy-start(bf16[1,448,1024]{2,1,0:T(8,128)(2,1)} %param.14) | copy-start | bytes 2752516
  13.8 45.3 %all-to-all-start = ((bf16[32,24,896]{2,1,0:T(8,128)(2,1)}), bf16[32,24,896]{2,1,0:T(8,128)(2,1)S(1)}, u32[]{:S(2)}, u32[]{:S(2)}) async-start(bf16[32,24,896]{2,1,0:T(8,128)(2,1)} %bitcast.17), calls=%async_computation | async-start | bytes 2752512 | tf_op jit(solution)/shard_map/all_to_all | solution.py:258
  23.6 91.4 %reduce-scatter.2.cloned.1.call-start = ((), (), s32[]{:S(2)}) async-start(), calls=%async_computation.3 | async-start | bytes 3538944 | tf_op jit(solution)/shard_map/reduce_scatter | solution.py:280
  23.7 4.6 %collective-permute-start.1 = (bf16[448,1024]{1,0:T(8,128)(2,1)S(1)}, bf16[448,1024]{1,0:T(8,128)(2,1)S(1)}, u32[]{:S(2)}, u32[]{:S(2)}) collective-permute-start(bf16[448,1024]{1,0:T(8,128)(2,1)S(1)} %bitcast.43), channel_id=1, source_target_pairs={{0,1},{1,0},{2,3},{3,2},{4,5},{5,4},{6,7},{7,6},{8,9},{9,8},{10,11... | collective-permute-start | bytes 2752520 | tf_op jit(solution)/shard_map/ppermute | solution.py:225
  26.1 4.5 %collective-permute-start.2 = (bf16[448,1024]{1,0:T(8,128)(2,1)S(1)}, bf16[448,1024]{1,0:T(8,128)(2,1)}, u32[]{:S(2)}, u32[]{:S(2)}) collective-permute-start(bf16[448,1024]{1,0:T(8,128)(2,1)S(1)} %bitcast.45), channel_id=1, source_target_pairs={{0,1},{1,0},{2,3},{3,2},{4,5},{5,4},{6,7},{7,6},{8,9},{9,8},{10,11... | collective-permute-start | bytes 2752520 | tf_op jit(solution)/shard_map/ppermute | solution.py:226
  28.2 0.9 copy-start.13
  59.1 1.1 copy-start.10
  115.0 1.0 copy-start.1
  116.2 6.0 %collective-permute-start.3 = (bf16[96,1024]{1,0:T(8,128)(2,1)S(1)}, bf16[96,1024]{1,0:T(8,128)(2,1)S(1)}, u32[]{:S(2)}, u32[]{:S(2)}) collective-permute-start(bf16[96,1024]{1,0:T(8,128)(2,1)S(1)} %hidden_units.1), channel_id=1, source_target_pairs={{0,1},{1,0},{2,3},{3,2},{4,5},{5,4},{6,7},{7,6},{8,9},{9,8},{10,11... | collective-permute-start | bytes 589832 | tf_op jit(solution)/shard_map/ppermute | solution.py:311
  122.1 14.0 %collective-permute-start.4 = (bf16[192,1024]{1,0:T(8,128)(2,1)S(1)}, bf16[192,1024]{1,0:T(8,128)(2,1)S(1)}, u32[]{:S(2)}, u32[]{:S(2)}) collective-permute-start(bf16[192,1024]{1,0:T(8,128)(2,1)S(1)} %pad_maximum_fusion.2.own), channel_id=1, source_target_pairs={{0,4},{1,13},{2,6},{3,15},{4,8},{5,1},{6,10},{7,3},{8,12},{9,5},{1... | collective-permute-start | bytes 1179656 | tf_op jit(solution)/shard_map/ppermute | solution.py:309
  125.3 17.0 %collective-permute-start.8 = (bf16[192,1024]{1,0:T(8,128)(2,1)S(1)}, bf16[192,1024]{1,0:T(8,128)(2,1)S(1)}, u32[]{:S(2)}, u32[]{:S(2)}) collective-permute-start(bf16[192,1024]{1,0:T(8,128)(2,1)S(1)} %pad_maximum_fusion.2.own), channel_id=1, source_target_pairs={{0,2},{1,15},{2,4},{3,1},{4,6},{5,3},{6,8},{7,5},{8,10},{9,7},{10,... | collective-permute-start | bytes 1179656 | tf_op jit(solution)/shard_map/ppermute | solution.py:309
  136.2 13.3 %collective-permute-start.5 = (bf16[192,1024]{1,0:T(8,128)(2,1)S(1)}, bf16[192,1024]{1,0:T(8,128)(2,1)S(1)}, u32[]{:S(2)}, u32[]{:S(2)}) collective-permute-start(bf16[192,1024]{1,0:T(8,128)(2,1)S(1)} %collective-permute-done.4.far), channel_id=1, source_target_pairs={{0,2},{1,15},{2,4},{3,1},{4,6},{5,3},{6,8},{7,5},{8,10},{9,7},{10,... | collective-permute-start | bytes 1179656 | tf_op jit(solution)/shard_map/ppermute | solution.py:309
  138.6 16.1 %copy-start = (bf16[1,1024,448]{1,2,0:T(8,128)(2,1)S(1)}, bf16[1,1024,448]{1,2,0:T(8,128)(2,1)}, u32[]{:S(2)}) copy-start(bf16[1,1024,448]{1,2,0:T(8,128)(2,1)} %param.15) | copy-start | bytes 2752516
  138.6 10.8 %collective-permute-start.6 = (bf16[96,1024]{1,0:T(8,128)(2,1)S(1)}, bf16[96,1024]{1,0:T(8,128)(2,1)S(1)}, u32[]{:S(2)}, u32[]{:S(2)}) collective-permute-start(bf16[96,1024]{1,0:T(8,128)(2,1)S(1)} %slice.4), channel_id=1, source_target_pairs={{0,4},{1,13},{2,6},{3,15},{4,8},{5,1},{6,10},{7,3},{8,12},{9,5},{1... | collective-permute-start | bytes 589832 | tf_op jit(solution)/shard_map/ppermute | solution.py:309
  143.3 11.4 %collective-permute-start.9 = (bf16[384,1024]{1,0:T(8,128)(2,1)}, bf16[384,1024]{1,0:T(8,128)(2,1)S(1)}, u32[]{:S(2)}, u32[]{:S(2)}) collective-permute-start(bf16[384,1024]{1,0:T(8,128)(2,1)} %pad_maximum_fusion), channel_id=1, source_target_pairs={{0,1},{1,0},{2,3},{3,2},{4,5},{5,4},{6,7},{7,6},{8,9},{9,8},{10,11... | collective-permute-start | bytes 2359304 | tf_op jit(solution)/shard_map/ppermute | solution.py:314
  150.3 6.9 %collective-permute-start.7 = (bf16[288,1024]{1,0:T(8,128)(2,1)}, bf16[288,1024]{1,0:T(8,128)(2,1)}, u32[]{:S(2)}, u32[]{:S(2)}) collective-permute-start(bf16[288,1024]{1,0:T(8,128)(2,1)} %pad_maximum_fusion.1), channel_id=1, source_target_pairs={{0,1},{1,0},{2,3},{3,2},{4,5},{5,4},{6,7},{7,6},{8,9},{9,8},{10,11... | collective-permute-start | bytes 1769480 | tf_op jit(solution)/shard_map/ppermute | solution.py:315
  159.9 10.3 %copy-start.4 = (s32[128,8]{0,1:T(8,128)S(1)}, s32[128,8]{0,1:T(8,128)}, u32[]{:S(2)}) copy-start(s32[128,8]{0,1:T(8,128)} %param.9) | copy-start | bytes 12292
  160.0 10.3 %copy-start.5 = (s32[128,8]{0,1:T(8,128)S(1)}, s32[128,8]{0,1:T(8,128)}, u32[]{:S(2)}) copy-start(s32[128,8]{0,1:T(8,128)} %param.10) | copy-start | bytes 12292
  160.0 10.3 %copy-start.7 = (s32[32]{0:T(128)S(1)}, s32[32]{0:T(128)}, u32[]{:S(2)}) copy-start(s32[32]{0:T(128)} %param.11) | copy-start | bytes 388
  160.0 10.3 %copy-start.9 = (s32[32]{0:T(128)S(1)}, s32[32]{0:T(128)}, u32[]{:S(2)}) copy-start(s32[32]{0:T(128)} %param.12) | copy-start | bytes 388
  160.0 45.7 %all-to-all-start.1 = ((bf16[32,24,896]{2,1,0:T(8,128)(2,1)}), bf16[32,24,896]{2,1,0:T(8,128)(2,1)S(1)}, u32[]{:S(2)}, u32[]{:S(2)}) async-start(bf16[32,24,896]{2,1,0:T(8,128)(2,1)} %bitcast.24), calls=%async_computation.2 | async-start | bytes 2752512 | tf_op jit(solution)/shard_map/all_to_all | solution.py:353
Sparse Core Ops, SparseCore 0:
  67.1 47.9 reduce-scatter.1

commit v4 on v3

--- a/solution.py
+++ b/solution.py
@@ -1,3 +1,5 @@
+import functools
+
 import jax
 import jax.numpy as jnp
 from jax import lax
@@ -6,6 +8,8 @@
 from jax.sharding import PartitionSpec as P
 
 HALF = 24
+ROOM = 77824
+HELD = 20
 PIECES = 4
 STRIP = 256
 
@@ -43,12 +47,14 @@
     return jnp.where((named > 0.0) & (before < limit), before, -1.0)
 
 
-def table_kernel(core, routes, capacity, spill, tokens, pick, kept, named, limits, sem):
+def table_kernel(
+    core, routes, capacity, spill, tokens, kept, named, limits, features, pick, sem
+):
     copies = [
         pltpu.make_async_copy(routes, named, sem.at[0]),
         pltpu.make_async_copy(capacity, limits.at[0:1], sem.at[1]),
         pltpu.make_async_copy(spill, limits.at[1:2], sem.at[2]),
-        pltpu.make_async_copy(tokens, kept, sem.at[3]),
+        pltpu.make_async_copy(tokens, features, sem.at[3]),
     ]
     for copy in copies:
         copy.start()
@@ -60,15 +66,38 @@
     chosen = jnp.where(rank[:, None, :] == slot.astype(jnp.float32), 1.0, 0.0)
     pick[...] = chosen.reshape(experts * HALF, count).astype(jnp.bfloat16)
     copies[3].wait()
-
-
-def pick_kernel(pick, tokens, tokens_other, rows, held, sem):
-    features = jnp.concatenate([tokens[...], tokens_other[...]], axis=0)
-    piece = rows.shape[0] // PIECES
+    size = experts * HALF
+    stores = [
+        pltpu.make_async_copy(pick, kept.at[pl.ds(0, size)], sem.at[4]),
+        pltpu.make_async_copy(features, kept.at[pl.ds(size, features.shape[0])], sem.at[5]),
+    ]
+    for copy in stores:
+        copy.start()
+    for copy in stores:
+        copy.wait()
+
+
+def pick_kernel(kept, tokens_other, rows, pick, features, held, sem):
+    size = pick.shape[0]
+    depth = tokens_other.shape[0]
+    loads = [
+        pltpu.make_async_copy(kept.at[pl.ds(0, size)], pick, sem.at[PIECES]),
+        pltpu.make_async_copy(
+            kept.at[pl.ds(size, depth)], features.at[pl.ds(0, depth)], sem.at[PIECES + 1]
+        ),
+    ]
+    for copy in loads:
+        copy.start()
+    features[depth:, :] = tokens_other[...]
+    for copy in loads:
+        copy.wait()
+    piece = size // PIECES
     copies = []
     for k in range(PIECES):
         at = pl.ds(k * piece, piece)
-        picked = lax.dot_general(pick[at, :], features, NT, preferred_element_type=jnp.float32)
+        picked = lax.dot_general(
+            pick[at, :], features[...], NT, preferred_element_type=jnp.float32
+        )
         held[at, :] = picked.astype(jnp.bfloat16)
         copies.append(pltpu.make_async_copy(held.at[at], rows.at[at], sem.at[k]))
         copies[-1].start()
@@ -95,54 +124,61 @@
         weigh[half, count : 2 * count, :] = lower
 
 
-def project_kernel(rows, gate, gate_other, up, up_other, sums, held, weight, result, came, went):
-    depth, width = held.shape
-    features = width // 2
-    strips = gate.shape[1] // STRIP
-    piece = depth // PIECES
-    loads = []
-    for k in range(PIECES):
-        at = pl.ds(k * piece, piece)
-        loads.append(pltpu.make_async_copy(rows.at[at], held.at[at], came.at[k]))
+def gather_kernel(gate, gate_other, up, up_other, weights, held, came, went):
+    loads, stores = [], []
+    for n, source in enumerate((gate, gate_other, up, up_other)):
+        loads.append(pltpu.make_async_copy(source, held.at[n], came.at[n]))
         loads[-1].start()
-    sources = ((gate, 0, 0), (gate_other, 1, 0), (up, 0, 1), (up_other, 1, 1))
+    for n, load in enumerate(loads):
+        load.wait()
+        stores.append(pltpu.make_async_copy(held.at[n], weights.at[n], went.at[n]))
+        stores[-1].start()
+    for store in stores:
+        store.wait()
+
+
+def project_kernel(parts, chips, rows, weights, *refs):
+    outs, (picked, weight, came) = refs[:-3], refs[-3:]
+    features = rows.shape[1] // 2
+    strips = weights.shape[2] // STRIP
+    sources = ((0, 0), (1, 0), (0, 1), (1, 1))
     fetched = []
     for strip in range(strips):
-        for n, (source, low, kind) in enumerate(sources):
+        for n, (low, kind) in enumerate(sources):
             copy = pltpu.make_async_copy(
-                source.at[:, pl.ds(strip * STRIP, STRIP)],
-                weight.at[strip, kind, pl.ds(low * features, features)],
-                came.at[PIECES + strip * len(sources) + n],
+                weights.at[n, :, pl.ds(strip * STRIP, STRIP)],
+                weight.at[strip, pl.ds(low * features, features), pl.ds(kind * STRIP, STRIP)],
+                came.at[strip * len(sources) + n],
             )
             copy.start()
             fetched.append(copy)
-    for copy in loads:
-        copy.wait()
-    stores = []
+    depth = picked.shape[0] // len(parts)
+    for n, (chip, _) in enumerate(parts):
+        start = pl.multiple_of(chips[chip] * depth, depth)
+        picked[n * depth : (n + 1) * depth, :] = rows[pl.ds(start, depth), :]
     for strip in range(strips):
         for copy in fetched[strip * len(sources) : (strip + 1) * len(sources)]:
             copy.wait()
-        for kind in range(2):
-            part = jnp.dot(held[...], weight[strip, kind], preferred_element_type=jnp.float32)
-            result[strip, :, kind * STRIP : (kind + 1) * STRIP] = part.astype(jnp.bfloat16)
-        for k in range(PIECES):
-            at = pl.ds(k * piece, piece)
-            copy = pltpu.make_async_copy(
-                result.at[strip, at],
-                sums.at[at, pl.ds(strip * 2 * STRIP, 2 * STRIP)],
-                went.at[strip * PIECES + k],
-            )
-            copy.start()
-            stores.append(copy)
-    for copy in stores:
-        copy.wait()
-
-
-def hidden_kernel(sums, hidden):
+        value = jnp.dot(picked[...], weight[strip], preferred_element_type=jnp.float32)
+        value = value.astype(jnp.bfloat16)
+        at = slice(strip * 2 * STRIP, (strip + 1) * 2 * STRIP)
+        out = iter(outs)
+        for n, (_, sizes) in enumerate(parts):
+            low = n * depth
+            for size in sizes:
+                next(out)[:, at] = value[low : low + size]
+                low += size
+
+
+def hidden_kernel(*refs):
+    terms, hidden = refs[:-1], refs[-1]
     for strip in range(hidden.shape[1] // STRIP):
         at = 2 * STRIP * strip
-        gate = sums[:, at : at + STRIP].astype(jnp.float32)
-        up = sums[:, at + STRIP : at + 2 * STRIP].astype(jnp.float32)
+        gate = jnp.zeros((hidden.shape[0], STRIP), jnp.float32)
+        up = gate
+        for term in terms:
+            gate = gate + term[:, at : at + STRIP].astype(jnp.float32)
+            up = up + term[:, at + STRIP : at + 2 * STRIP].astype(jnp.float32)
         value = gate / (1.0 + jnp.exp(-gate)) * up
         hidden[:, STRIP * strip : STRIP * (strip + 1)] = value.astype(jnp.bfloat16)
 
@@ -179,10 +215,10 @@
 def late_kernel(places, third, fourth, swapped, down, filled, out, held, sem):
     del filled
     depth = fourth.shape[0]
-    rows = jnp.concatenate([third[...], swapped[0 : 2 * depth]], axis=0)
-    last = jnp.concatenate([fourth[...], swapped[2 * depth : 3 * depth]], axis=0)
-    parts = ((rows, (5, 6)), (last, (7,)))
-    down_kernel(places, parts, down, out, held, sem, 5)
+    rows = jnp.concatenate(
+        [third[...], swapped[0 : 2 * depth], fourth[...], swapped[2 * depth : 3 * depth]], axis=0
+    )
+    down_kernel(places, ((rows, (5, 6, 7)),), down, out, held, sem, 5)
 
 
 def mix_kernel(weigh, values, mixed):
@@ -210,7 +246,6 @@
     bf16 = jnp.bfloat16
     core = (lax.axis_index("dp") % 2).astype(jnp.int32).reshape(1)
     swap = [(i, i ^ 1) for i in range(2 * planes)]
-    same_core = [[2 * z + c for z in range(planes)] for c in range(2)]
 
     own_tokens = tokens.T
     own_routes = routes.T
@@ -225,61 +260,101 @@
     gate_other = lax.ppermute(gate, "dp", swap)
     up_other = lax.ppermute(up, "dp", swap)
 
-    pick, kept_tokens = pl.pallas_call(
+    kept = pl.pallas_call(
         table_kernel,
-        out_shape=[
-            jax.ShapeDtypeStruct((experts * HALF, count), bf16),
-            jax.ShapeDtypeStruct((features, count), bf16),
-        ],
+        out_shape=jax.ShapeDtypeStruct((ROOM, count), bf16),
         in_specs=[SMEM] + [HBM] * 4,
-        out_specs=[VMEM] * 2,
+        out_specs=HBM,
         scratch_shapes=[
             pltpu.VMEM(own_routes.shape, jnp.int32),
             pltpu.VMEM((2, experts), jnp.int32),
-            pltpu.SemaphoreType.DMA((4,)),
+            pltpu.VMEM((features, count), bf16),
+            pltpu.VMEM((experts * HALF, count), bf16),
+            pltpu.SemaphoreType.DMA((6,)),
         ],
-        compiler_params=LIMIT,
+        compiler_params=pltpu.CompilerParams(vmem_limit_bytes=60 * 1024 * 1024),
         cost_estimate=cost(2 * experts * count * count, 600000),
         name="pick_table",
     )(core, own_routes, cap_row, spill_row, own_tokens)
     send = pl.pallas_call(
         pick_kernel,
         out_shape=jax.ShapeDtypeStruct((experts * HALF, 2 * features), bf16),
-        in_specs=[VMEM] * 3,
+        in_specs=[HBM, VMEM],
         out_specs=HBM,
         scratch_shapes=[
+            pltpu.VMEM((experts * HALF, count), bf16),
+            pltpu.VMEM((2 * features, count), bf16),
             pltpu.VMEM((experts * HALF, 2 * features), bf16),
-            pltpu.SemaphoreType.DMA((PIECES,)),
+            pltpu.SemaphoreType.DMA((PIECES + 2,)),
         ],
-        compiler_params=LIMIT,
+        compiler_params=pltpu.CompilerParams(vmem_limit_bytes=48 * 1024 * 1024),
         cost_estimate=cost(2 * experts * HALF * count * 2 * features, 2000000),
         name="pick_rows",
-    )(pick, kept_tokens, tokens_other)
+    )(kept, tokens_other)
     got = lax.all_to_all(
         send.reshape(groups, HALF, 2 * features), "ep", split_axis=0, concat_axis=0, tiled=True
     ).reshape(groups * HALF, 2 * features)
 
     depth = groups * HALF
-    strips = units // STRIP
-    sums = pl.pallas_call(
-        project_kernel,
-        out_shape=jax.ShapeDtypeStruct((depth, 2 * units), bf16),
-        in_specs=[HBM] * 5,
+    weights = pl.pallas_call(
+        gather_kernel,
+        out_shape=jax.ShapeDtypeStruct((HELD,) + gate.shape, bf16),
+        in_specs=[HBM] * 4,
         out_specs=HBM,
         scratch_shapes=[
-            pltpu.VMEM((depth, 2 * features), bf16),
-            pltpu.VMEM((strips, 2, 2 * features, STRIP), bf16),
-            pltpu.VMEM((strips, depth, 2 * STRIP), bf16),
-            pltpu.SemaphoreType.DMA((PIECES + 4 * strips,)),
-            pltpu.SemaphoreType.DMA((strips * PIECES,)),
+            pltpu.VMEM((4,) + gate.shape, bf16),
+            pltpu.SemaphoreType.DMA((4,)),
+            pltpu.SemaphoreType.DMA((4,)),
         ],
-        compiler_params=LARGE,
-        cost_estimate=cost(2 * depth * 2 * features * 2 * units, 8000000),
-        name="project_in",
-    )(got, gate, gate_other, up, up_other)
-    summed = lax.psum_scatter(
-        sums, "dp", scatter_dimension=0, tiled=True, axis_index_groups=same_core
-    )
+        compiler_params=LIMIT,
+        cost_estimate=cost(0, 7400000),
+        name="gather_weights",
+    )(gate, gate_other, up, up_other)
+    strips = units // STRIP
+    part = depth // planes
+    half = part // 2
+    plane = lax.axis_index("dp") // 2
+    chips = jnp.stack([(plane + k) % planes for k in range(planes)]).astype(jnp.int32)
+
+    def project(parts, name):
+        shapes = [
+            jax.ShapeDtypeStruct((size, 2 * units), bf16) for _, sizes in parts for size in sizes
+        ]
+        held = len(parts) * part
+        return pl.pallas_call(
+            functools.partial(project_kernel, parts),
+            out_shape=shapes,
+            in_specs=[SMEM, VMEM, HBM],
+            out_specs=[VMEM] * len(shapes),
+            scratch_shapes=[
+                pltpu.VMEM((held, 2 * features), bf16),
+                pltpu.VMEM((strips, 2 * features, 2 * STRIP), bf16),
+                pltpu.SemaphoreType.DMA((4 * strips,)),
+            ],
+            compiler_params=pltpu.CompilerParams(vmem_limit_bytes=48 * 1024 * 1024),
+            cost_estimate=cost(2 * held * 2 * features * 2 * units, 6000000),
+            name=name,
+        )(chips, got, weights)
+
+    def hop(rows, hops):
+        steps = [
+            (2 * z + c, 2 * ((z + hops) % planes) + c) for z in range(planes) for c in range(2)
+        ]
+        return lax.ppermute(rows, "dp", steps)
+
+    def add(*terms):
+        return sum(term.astype(jnp.float32) for term in terms).astype(bf16)
+
+    up3, down3, up4, down4 = project(
+        ((3, (part,)), (planes - 3, (part,)), (4, (half, half))), "project_in_far"
+    )
+    here, up1, down1, up2, down2 = project(
+        tuple((k % planes, (part,)) for k in (0, 1, -1, 2, -2)), "project_in_near"
+    )
+    rest = jnp.zeros((half, 2 * units), bf16)
+    up2 = add(up2, hop(up3, 1), jnp.concatenate([hop(up4, 2), rest]))
+    down2 = add(down2, hop(down3, -1), jnp.concatenate([rest, hop(down4, -2)]))
+    terms = (here, hop(up1, 1), hop(down1, -1), hop(up2, 2), hop(down2, -2))
     weigh = pl.pallas_call(
         weigh_kernel,
         out_shape=jax.ShapeDtypeStruct((2, 2 * count, experts * HALF), bf16),
@@ -289,16 +364,15 @@
         cost_estimate=cost(2 * experts * count * count, 4000000),
         name="weigh_table",
     )(own_routes, own_weights, cap_row, spill_row)
-    part = depth // planes
     hidden = pl.pallas_call(
         hidden_kernel,
         out_shape=jax.ShapeDtypeStruct((part, units), bf16),
-        in_specs=[VMEM],
+        in_specs=[VMEM] * len(terms),
         out_specs=VMEM,
         compiler_params=LIMIT,
-        cost_estimate=cost(8 * part * units, 600000),
+        cost_estimate=cost(8 * part * units, 2200000),
         name="hidden_units",
-    )(summed)
+    )(*terms)
 
     def flow(rows, hops):
         steps = [
@@ -313,12 +387,11 @@
     third, fourth = flow(far, 1), flow(far[:part], 2)
     swapped_pair = lax.ppermute(jnp.concatenate([near, far], axis=0), "dp", swap)
     swapped_last = lax.ppermute(jnp.concatenate([third, fourth], axis=0), "dp", swap)
-    plane = lax.axis_index("dp") // 2
     sense = 2 * core[0] - 1
-    chips = [0, sense, 2 * sense, -sense, -2 * sense, 3 * sense, -3 * sense, 4]
+    offsets = [0, sense, 2 * sense, -sense, -2 * sense, 3 * sense, -3 * sense, 4]
     orders = [core[0]] * 3 + [1 - core[0]] * 2 + [core[0], 1 - core[0], core[0]]
     places = jnp.stack(
-        [jnp.stack([(plane + chip + planes) % planes for chip in chips]), jnp.stack(orders)]
+        [jnp.stack([(plane + chip + planes) % planes for chip in offsets]), jnp.stack(orders)]
     ).astype(jnp.int32)
     back_shape = jax.ShapeDtypeStruct((depth, 2 * features), bf16)
 

time: 215 us -> 203 us (0.944)
  waiting for transfers between devices: 124 us -> 94.1 us
  starting transfers between devices: 52.6 us -> 81.3 us
  between operations: 13.9 us -> 0.7 us
  Pallas kernels: 15.7 us -> 23.2 us
  local copies, waits for them, and re-layouts: 6.14 us -> 0.32 us
    reduce_scatter x1 -> x0, waiting for transfers between devices: 48.1 us -> none  [on_device(): lax.psum_scatter(sums, 'dp', scatter_dimension=0, tiled=True, axis_index_...]
    ppermute x0 -> x8, starting transfers between devices: none -> 31 us  [hop(): return lax.ppermute(rows, 'dp', steps)]
    ppermute x0 -> x8, waiting for transfers between devices: none -> 20.8 us  [hop(): return lax.ppermute(rows, 'dp', steps)]
    pallas_call x2 -> x4, Pallas kernels: 7.09 us -> 13.4 us  [the longest x2 8.56 us: project(): pl.pallas_call(functools.partial(project_kernel, parts), out_shape=shapes...]
    unnamed x28 -> x14, local copies, waits for them, and re-layouts: 5.95 us -> 0.04 us
    all_to_all x1, starting transfers between devices: 10.2 us -> 5.35 us  [on_device(): values = lax.all_to_all(back, 'ep', split_axis=0, concat_axis=0, tiled=True)]
    all_to_all x1, waiting for transfers between devices: 28.4 us -> 25.4 us  [on_device(): lax.all_to_all(send.reshape(groups, HALF, 2 * features), 'ep', split_axis...]
    ppermute x1, starting transfers between devices: 4.03 us -> 6.78 us  [on_device(): lax.ppermute(jnp.concatenate([third, fourth], axis=0), 'dp', swap)]
  transfers between devices with their start and end apart: 13 -> 20, of which waited for: 8 -> 10; matrix products, arithmetic and copies ran while one was open for 1% -> 1% of each run, Pallas kernels for 2% -> 6%
where the time goes in v4:
time: 203 us; the launch traced here: 202 us
  waiting for transfers between devices  94.1 us (46%)
  starting transfers between devices  81.3 us (40%)
  Pallas kernels  23.2 us (11%)
  other arithmetic  2.09 us (1%)
    all_to_all x1, waiting for transfers between devices, on_device(): values = lax.all_to_all(back, 'ep', split_axis=0, concat_axis=0, tiled=True)  35 us
    ppermute x8, starting transfers between devices, hop(): return lax.ppermute(rows, 'dp', steps)  31 us
    all_to_all x1, waiting for transfers between devices, on_device(): lax.all_to_all(send.reshape(groups, HALF, 2 * features), 'ep', split_axis...  25.4 us
    ppermute x8, waiting for transfers between devices, hop(): return lax.ppermute(rows, 'dp', steps)  20.8 us
    ppermute x4, starting transfers between devices, flow(): return lax.ppermute(rows, 'dp', steps)  12.8 us
    all_to_all x1, starting transfers between devices, on_device(): lax.all_to_all(send.reshape(groups, HALF, 2 * features), 'ep', split_axis...  9.75 us
    ppermute x4, waiting for transfers between devices, flow(): return lax.ppermute(rows, 'dp', steps)  9.54 us
    pallas_call x2, Pallas kernels, project(): pl.pallas_call(functools.partial(project_kernel, parts), out_shape=shapes...  8.56 us
  transfers between devices with their start and end apart: 20, of which 10 were waited for; matrix products, arithmetic and copies ran while one was open for 1% of the time, Pallas kernels for 6%

profile of v4, /device:TPU:9, one launch (start us, length us, event | category | flops | bytes accessed | tf_op | source)
XLA Modules:
  0.0 201.7 jit_solution(3081353621902115206)
XLA Ops:
  0.0 2.6 %collective-permute-start = (bf16[448,128]{1,0:T(8,128)(2,1)}, bf16[448,128]{1,0:T(8,128)(2,1)S(1)}, u32[]{:S(2)}, u32[]{:S(2)}) collective-permute-start(bf16[448,128]{1,0:T(8,128)(2,1)} %bitcast.51), channel_id=1, source_target_pairs={{0,1},{1,0},{2,3},{3,2},{4,5},{5,4},{6,7},{7,6},{8,9},{9,8},{10,11... | collective-permute-start | bytes 344072 | tf_op jit(solution)/shard_map/ppermute | solution.py:259
  2.6 1.7 pick_table.1.kept
  4.3 0.0 collective-permute-done.tokens_other
  4.3 2.4 %pick_rows.1 = bf16[768,896]{1,0:T(8,128)(2,1)} custom-call(bf16[77824,128]{1,0:T(8,128)(2,1)} %pick_table.1.kept, bf16[448,128]{1,0:T(8,128)(2,1)S(1)} %collective-permute-done.tokens_other), custom_call_target="tpu_custom_call" | custom-call | flops 176160768 | bytes 2000000 | tf_op jit(solution)/shard_map/pick_rows/pallas_call | solution.py:279
  6.7 0.0 copy-start.1
  6.8 0.0 copy-start.2
  6.8 9.7 %all-to-all-start = ((bf16[32,24,896]{2,1,0:T(8,128)(2,1)}), bf16[32,24,896]{2,1,0:T(8,128)(2,1)S(1)}, u32[]{:S(2)}, u32[]{:S(2)}) async-start(bf16[32,24,896]{2,1,0:T(8,128)(2,1)} %bitcast.25), calls=%async_computation | async-start | bytes 2752512 | tf_op jit(solution)/shard_map/all_to_all | solution.py:294
  16.5 2.5 %collective-permute-start.1 = (bf16[448,1024]{1,0:T(8,128)(2,1)S(1)}, bf16[448,1024]{1,0:T(8,128)(2,1)}, u32[]{:S(2)}, u32[]{:S(2)}) collective-permute-start(bf16[448,1024]{1,0:T(8,128)(2,1)S(1)} %bitcast.40), channel_id=1, source_target_pairs={{0,1},{1,0},{2,3},{3,2},{4,5},{5,4},{6,7},{7,6},{8,9},{9,8},{10,11... | collective-permute-start | bytes 2752520 | tf_op jit(solution)/shard_map/ppermute | solution.py:260
  19.0 1.9 collective-permute-start.2
  21.1 0.1 stack.93.chips
  21.2 0.0 collective-permute-done.1.gate_other
  21.2 2.3 %collective-permute-done.2.up_other = bf16[448,1024]{1,0:T(8,128)(2,1)} collective-permute-done((bf16[448,1024]{1,0:T(8,128)(2,1)S(1)}, bf16[448,1024]{1,0:T(8,128)(2,1)}, u32[]{:S(2)}, u32[]{:S(2)}) %collective-permute-start.2) | collective-permute-done | bytes 917536 | tf_op jit(solution)/shard_map/ppermute | solution.py:261
  23.5 3.1 %gather_weights.1.weights = bf16[20,448,1024]{2,1,0:T(8,128)(2,1)} custom-call(bf16[448,1024]{1,0:T(8,128)(2,1)S(1)} %bitcast.41, bf16[448,1024]{1,0:T(8,128)(2,1)} %collective-permute-done.1.gate_other, bf16[448,1024]{1,0:T(8,128)(2,1)S(1)} %bitcast.43, bf16[448,1024]{1,0:T(8,128)(2,1)} %collective-permute-done.2.up_other), custom_call_target="tpu_custom_call" | custom-call | bytes 7400000 | tf_op jit(solution)/shard_map/gather_weights/pallas_call | solution.py:299
  26.7 25.4 %all-to-all-done = bf16[32,24,896]{2,1,0:T(8,128)(2,1)S(1)} async-done(((bf16[32,24,896]{2,1,0:T(8,128)(2,1)}), bf16[32,24,896]{2,1,0:T(8,128)(2,1)S(1)}, u32[]{:S(2)}, u32[]{:S(2)}) %all-to-all-start) | async-done | bytes 1376288 | tf_op jit(solution)/shard_map/all_to_all | solution.py:294
  52.0 3.9 %project_in_far.1 = (bf16[96,2048]{1,0:T(8,128)(2,1)S(1)}, bf16[96,2048]{1,0:T(8,128)(2,1)S(1)}, bf16[48,2048]{1,0:T(8,128)(2,1)S(1)}, bf16[48,2048]{1,0:T(8,128)(2,1)S(1)}) custom-call(s32[8]{0:T(128)S(1)} %stack.93.chips, bf16[768,896]{1,0:T(8,128)(2,1)S(1)} %bitcast.35, bf16[20,448,1024]{2,1,0:T(8,128)(2,1)} %gather_weights.1.weights), custom_call_target="tpu_custom_call" | custom-call | flops 1056964608 | bytes 6000000 | tf_op jit(solution)/shard_map/project_in_far/pallas_call | solution.py:324
  55.9 10.7 %collective-permute-start.8 = (bf16[96,2048]{1,0:T(8,128)(2,1)S(1)}, bf16[96,2048]{1,0:T(8,128)(2,1)S(1)}, u32[]{:S(2)}, u32[]{:S(2)}) collective-permute-start(bf16[96,2048]{1,0:T(8,128)(2,1)S(1)} %get-tuple-element.21), channel_id=1, source_target_pairs={{0,14},{1,15},{2,0},{3,1},{4,2},{5,3},{6,4},{7,5},{8,6},{9,7},{10,... | collective-permute-start | bytes 1179656 | tf_op jit(solution)/shard_map/ppermute | solution.py:343
  66.6 2.2 %collective-permute-start.9 = (bf16[48,2048]{1,0:T(8,128)(2,1)S(1)}, bf16[48,2048]{1,0:T(8,128)(2,1)S(1)}, u32[]{:S(2)}, u32[]{:S(2)}) collective-permute-start(bf16[48,2048]{1,0:T(8,128)(2,1)S(1)} %get-tuple-element.22), channel_id=1, source_target_pairs={{0,12},{1,13},{2,14},{3,15},{4,0},{5,1},{6,2},{7,3},{8,4},{9,5},{1... | collective-permute-start | bytes 589832 | tf_op jit(solution)/shard_map/ppermute | solution.py:343
  68.8 3.1 %collective-permute-start.5 = (bf16[96,2048]{1,0:T(8,128)(2,1)S(1)}, bf16[96,2048]{1,0:T(8,128)(2,1)S(1)}, u32[]{:S(2)}, u32[]{:S(2)}) collective-permute-start(bf16[96,2048]{1,0:T(8,128)(2,1)S(1)} %get-tuple-element.18), channel_id=1, source_target_pairs={{0,2},{1,3},{2,4},{3,5},{4,6},{5,7},{6,8},{7,9},{8,10},{9,11},{10,... | collective-permute-start | bytes 1179656 | tf_op jit(solution)/shard_map/ppermute | solution.py:343
  71.9 2.8 %collective-permute-start.6 = (bf16[48,2048]{1,0:T(8,128)(2,1)S(1)}, bf16[48,2048]{1,0:T(8,128)(2,1)S(1)}, u32[]{:S(2)}, u32[]{:S(2)}) collective-permute-start(bf16[48,2048]{1,0:T(8,128)(2,1)S(1)} %get-tuple-element.19), channel_id=1, source_target_pairs={{0,4},{1,5},{2,6},{3,7},{4,8},{5,9},{6,10},{7,11},{8,12},{9,13},{1... | collective-permute-start | bytes 589832 | tf_op jit(solution)/shard_map/ppermute | solution.py:343
  74.7 4.7 %project_in_near.1 = (bf16[96,2048]{1,0:T(8,128)(2,1)S(1)}, bf16[96,2048]{1,0:T(8,128)(2,1)S(1)}, bf16[96,2048]{1,0:T(8,128)(2,1)S(1)}, bf16[96,2048]{1,0:T(8,128)(2,1)S(1)}, bf16[96,2048]{1,0:T(8,128)(2,1)S(1)}) custom-call(s32[8]{0:T(128)S(1)} %stack.93.chips, bf16[768,896]{1,0:T(8,128)(2,1)S(1)} %bitcast.36, bf16[20,448,1024]{2,1,0:T(8,128)(2,1)} %gather_weights.1.weights), custom_call_target="tpu_custom_call" | custom-call | flops 1761607680 | bytes 6000000 | tf_op jit(solution)/shard_map/project_in_near/pallas_call | solution.py:324
  79.4 2.2 %collective-permute-start.3 = (bf16[96,2048]{1,0:T(8,128)(2,1)S(1)}, bf16[96,2048]{1,0:T(8,128)(2,1)S(1)}, u32[]{:S(2)}, u32[]{:S(2)}) collective-permute-start(bf16[96,2048]{1,0:T(8,128)(2,1)S(1)} %get-tuple-element.15), channel_id=1, source_target_pairs={{0,2},{1,3},{2,4},{3,5},{4,6},{5,7},{6,8},{7,9},{8,10},{9,11},{10,... | collective-permute-start | bytes 1179656 | tf_op jit(solution)/shard_map/ppermute | solution.py:343
  81.6 1.2 collective-permute-done.9
  82.8 3.1 %collective-permute-start.4 = (bf16[96,2048]{1,0:T(8,128)(2,1)S(1)}, bf16[96,2048]{1,0:T(8,128)(2,1)S(1)}, u32[]{:S(2)}, u32[]{:S(2)}) collective-permute-start(bf16[96,2048]{1,0:T(8,128)(2,1)S(1)} %get-tuple-element.16), channel_id=1, source_target_pairs={{0,14},{1,15},{2,0},{3,1},{4,2},{5,3},{6,4},{7,5},{8,6},{9,7},{10,... | collective-permute-start | bytes 1179656 | tf_op jit(solution)/shard_map/ppermute | solution.py:343
  85.9 0.0 collective-permute-done.8
  85.9 0.1 add_convert_fusion
  86.1 5.1 %collective-permute-start.10 = (bf16[96,2048]{1,0:T(8,128)(2,1)S(1)}, bf16[96,2048]{1,0:T(8,128)(2,1)S(1)}, u32[]{:S(2)}, u32[]{:S(2)}) collective-permute-start(bf16[96,2048]{1,0:T(8,128)(2,1)S(1)} %add_convert_fusion), channel_id=1, source_target_pairs={{0,12},{1,13},{2,14},{3,15},{4,0},{5,1},{6,2},{7,3},{8,4},{9,5},{1... | collective-permute-start | bytes 1179656 | tf_op jit(solution)/shard_map/ppermute | solution.py:343
  91.1 0.0 collective-permute-done.6
  91.1 0.0 collective-permute-done.5
  91.1 0.1 add_convert_fusion.1
  91.3 1.9 collective-permute-start.7
  93.2 5.0 %collective-permute-done.3.refs_1_ = bf16[96,2048]{1,0:T(8,128)(2,1)S(1)} collective-permute-done((bf16[96,2048]{1,0:T(8,128)(2,1)S(1)}, bf16[96,2048]{1,0:T(8,128)(2,1)S(1)}, u32[]{:S(2)}, u32[]{:S(2)}) %collective-permute-start.3) | collective-permute-done | bytes 393248 | tf_op jit(solution)/shard_map/ppermute | solution.py:343
  98.2 0.0 collective-permute-done.4.refs_2_
  98.2 8.8 %collective-permute-done.10.refs_4_ = bf16[96,2048]{1,0:T(8,128)(2,1)S(1)} collective-permute-done((bf16[96,2048]{1,0:T(8,128)(2,1)S(1)}, bf16[96,2048]{1,0:T(8,128)(2,1)S(1)}, u32[]{:S(2)}, u32[]{:S(2)}) %collective-permute-start.10) | collective-permute-done | bytes 393248 | tf_op jit(solution)/shard_map/ppermute | solution.py:343
  107.0 5.8 %collective-permute-done.7.refs_3_ = bf16[96,2048]{1,0:T(8,128)(2,1)S(1)} collective-permute-done((bf16[96,2048]{1,0:T(8,128)(2,1)S(1)}, bf16[96,2048]{1,0:T(8,128)(2,1)S(1)}, u32[]{:S(2)}, u32[]{:S(2)}) %collective-permute-start.7) | collective-permute-done | bytes 393248 | tf_op jit(solution)/shard_map/ppermute | solution.py:343
  112.8 0.3 hidden_units.1
  113.1 5.1 %collective-permute-start.11 = (bf16[96,1024]{1,0:T(8,128)(2,1)S(1)}, bf16[96,1024]{1,0:T(8,128)(2,1)S(1)}, u32[]{:S(2)}, u32[]{:S(2)}) collective-permute-start(bf16[96,1024]{1,0:T(8,128)(2,1)S(1)} %hidden_units.1), channel_id=1, source_target_pairs={{0,1},{1,0},{2,3},{3,2},{4,5},{5,4},{6,7},{7,6},{8,9},{9,8},{10,11... | collective-permute-start | bytes 589832 | tf_op jit(solution)/shard_map/ppermute | solution.py:385
  118.2 1.0 collective-permute-done.11
  119.3 1.9 collective-permute-start.12
  121.2 4.5 %collective-permute-start.16 = (bf16[192,1024]{1,0:T(8,128)(2,1)S(1)}, bf16[192,1024]{1,0:T(8,128)(2,1)S(1)}, u32[]{:S(2)}, u32[]{:S(2)}) collective-permute-start(bf16[192,1024]{1,0:T(8,128)(2,1)S(1)} %pad_maximum_fusion.2.own), channel_id=1, source_target_pairs={{0,2},{1,15},{2,4},{3,1},{4,6},{5,3},{6,8},{7,5},{8,10},{9,7},{10,... | collective-permute-start | bytes 1179656 | tf_op jit(solution)/shard_map/ppermute | solution.py:383
  125.8 7.5 %collective-permute-done.12.far = bf16[192,1024]{1,0:T(8,128)(2,1)S(1)} collective-permute-done((bf16[192,1024]{1,0:T(8,128)(2,1)S(1)}, bf16[192,1024]{1,0:T(8,128)(2,1)S(1)}, u32[]{:S(2)}, u32[]{:S(2)}) %collective-permute-start.12) | collective-permute-done | bytes 393248 | tf_op jit(solution)/shard_map/ppermute | solution.py:383
  133.3 3.6 %collective-permute-start.13 = (bf16[192,1024]{1,0:T(8,128)(2,1)S(1)}, bf16[192,1024]{1,0:T(8,128)(2,1)S(1)}, u32[]{:S(2)}, u32[]{:S(2)}) collective-permute-start(bf16[192,1024]{1,0:T(8,128)(2,1)S(1)} %collective-permute-done.12.far), channel_id=1, source_target_pairs={{0,2},{1,15},{2,4},{3,1},{4,6},{5,3},{6,8},{7,5},{8,10},{9,7},{10,... | collective-permute-start | bytes 1179656 | tf_op jit(solution)/shard_map/ppermute | solution.py:383
  137.0 0.0 copy-start
  137.0 2.7 %collective-permute-start.14 = (bf16[96,1024]{1,0:T(8,128)(2,1)S(1)}, bf16[96,1024]{1,0:T(8,128)(2,1)S(1)}, u32[]{:S(2)}, u32[]{:S(2)}) collective-permute-start(bf16[96,1024]{1,0:T(8,128)(2,1)S(1)} %slice.4), channel_id=1, source_target_pairs={{0,4},{1,13},{2,6},{3,15},{4,8},{5,1},{6,10},{7,3},{8,12},{9,5},{1... | collective-permute-start | bytes 589832 | tf_op jit(solution)/shard_map/ppermute | solution.py:383
  139.7 0.0 collective-permute-done.16.near
  139.7 0.9 pad_maximum_fusion
  140.6 3.5 %collective-permute-start.17 = (bf16[384,1024]{1,0:T(8,128)(2,1)}, bf16[384,1024]{1,0:T(8,128)(2,1)S(1)}, u32[]{:S(2)}, u32[]{:S(2)}) collective-permute-start(bf16[384,1024]{1,0:T(8,128)(2,1)} %pad_maximum_fusion), channel_id=1, source_target_pairs={{0,1},{1,0},{2,3},{3,2},{4,5},{5,4},{6,7},{7,6},{8,9},{9,8},{10,11... | collective-permute-start | bytes 2359304 | tf_op jit(solution)/shard_map/ppermute | solution.py:388
  144.1 2.0 collective-permute-done.14.fourth
  146.2 0.0 collective-permute-done.13.third
  146.2 0.9 pad_maximum_fusion.1
  147.0 6.8 %collective-permute-start.15 = (bf16[288,1024]{1,0:T(8,128)(2,1)}, bf16[288,1024]{1,0:T(8,128)(2,1)}, u32[]{:S(2)}, u32[]{:S(2)}) collective-permute-start(bf16[288,1024]{1,0:T(8,128)(2,1)} %pad_maximum_fusion.1), channel_id=1, source_target_pairs={{0,1},{1,0},{2,3},{3,2},{4,5},{5,4},{6,7},{7,6},{8,9},{9,8},{10,11... | collective-permute-start | bytes 1769480 | tf_op jit(solution)/shard_map/ppermute | solution.py:389
  153.9 0.1 stack.82
  154.0 0.1 stack.79
  154.1 0.0 collective-permute-done.17.swapped_pair
  154.2 2.5 %project_out_early.1.filled = bf16[768,896]{1,0:T(8,128)(2,1)} custom-call(s32[2,8]{1,0:T(2,128)S(1)} %pad_add_fusion.places, bf16[192,1024]{1,0:T(8,128)(2,1)S(1)} %pad_maximum_fusion.2.own, bf16[192,1024]{1,0:T(8,128)(2,1)S(1)} %collective-permute-done.16.near, bf16[192,1024]{1,0:T(8,128)(2,1)S(1)} %collective-permute-done.12.far, ...), custom_call_target="tpu_custom_call" | custom-call | flops 880803840 | bytes 4000000 | tf_op jit(solution)/shard_map/project_out_early/pallas_call | solution.py:404
  156.7 0.0 collective-permute-done.15.swapped
  156.7 2.7 %project_out_late.1 = bf16[768,896]{1,0:T(8,128)(2,1)} custom-call(s32[2,8]{1,0:T(2,128)S(1)} %pad_add_fusion.places, bf16[192,1024]{1,0:T(8,128)(2,1)S(1)} %collective-permute-done.13.third, bf16[96,1024]{1,0:T(8,128)(2,1)S(1)} %collective-permute-done.14.fourth, bf16[288,1024]{1,0:T(8,128)(2,1)} %collective-permute-done.15.swapped, ...), custom_call_target="tpu_custom_call", output_to_operand_aliasing={{}: (5, {})} | custom-call | flops 528482304 | bytes 4000000 | tf_op jit(solution)/shard_map/project_out_late/pallas_call | solution.py:414
  159.4 0.0 copy-start.3
  159.4 0.0 copy-start.4
  159.4 0.0 copy-start.5
  159.4 0.0 copy-start.6
  159.4 5.3 %all-to-all-start.1 = ((bf16[32,24,896]{2,1,0:T(8,128)(2,1)}), bf16[32,24,896]{2,1,0:T(8,128)(2,1)S(1)}, u32[]{:S(2)}, u32[]{:S(2)}) async-start(bf16[32,24,896]{2,1,0:T(8,128)(2,1)} %bitcast.32), calls=%async_computation.1 | async-start | bytes 2752512 | tf_op jit(solution)/shard_map/all_to_all | solution.py:426
  164.8 0.4 weigh_table.1.weigh
  165.3 35.0 %all-to-all-done.1 = bf16[32,24,896]{2,1,0:T(8,128)(2,1)S(1)} async-done(((bf16[32,24,896]{2,1,0:T(8,128)(2,1)}), bf16[32,24,896]{2,1,0:T(8,128)(2,1)S(1)}, u32[]{:S(2)}, u32[]{:S(2)}) %all-to-all-start.1) | async-done | bytes 1376288 | tf_op jit(solution)/shard_map/all_to_all | solution.py:426
  200.3 1.4 mix_rows.1
  (10 shorter events, 0.1 us)
Async XLA Ops:
  0.0 4.3 %collective-permute-start = (bf16[448,128]{1,0:T(8,128)(2,1)}, bf16[448,128]{1,0:T(8,128)(2,1)S(1)}, u32[]{:S(2)}, u32[]{:S(2)}) collective-permute-start(bf16[448,128]{1,0:T(8,128)(2,1)} %bitcast.51), channel_id=1, source_target_pairs={{0,1},{1,0},{2,3},{3,2},{4,5},{5,4},{6,7},{7,6},{8,9},{9,8},{10,11... | collective-permute-start | bytes 344072 | tf_op jit(solution)/shard_map/ppermute | solution.py:259
  6.7 9.8 %copy-start.1 = (bf16[1,448,1024]{2,1,0:T(8,128)(2,1)S(1)}, bf16[1,448,1024]{2,1,0:T(8,128)(2,1)}, u32[]{:S(2)}) copy-start(bf16[1,448,1024]{2,1,0:T(8,128)(2,1)} %param.13) | copy-start | bytes 2752516
  6.8 12.3 %copy-start.2 = (bf16[1,448,1024]{2,1,0:T(8,128)(2,1)S(1)}, bf16[1,448,1024]{2,1,0:T(8,128)(2,1)}, u32[]{:S(2)}) copy-start(bf16[1,448,1024]{2,1,0:T(8,128)(2,1)} %param.14) | copy-start | bytes 2752516
  6.8 45.3 %all-to-all-start = ((bf16[32,24,896]{2,1,0:T(8,128)(2,1)}), bf16[32,24,896]{2,1,0:T(8,128)(2,1)S(1)}, u32[]{:S(2)}, u32[]{:S(2)}) async-start(bf16[32,24,896]{2,1,0:T(8,128)(2,1)} %bitcast.25), calls=%async_computation | async-start | bytes 2752512 | tf_op jit(solution)/shard_map/all_to_all | solution.py:294
  16.5 4.7 %collective-permute-start.1 = (bf16[448,1024]{1,0:T(8,128)(2,1)S(1)}, bf16[448,1024]{1,0:T(8,128)(2,1)}, u32[]{:S(2)}, u32[]{:S(2)}) collective-permute-start(bf16[448,1024]{1,0:T(8,128)(2,1)S(1)} %bitcast.40), channel_id=1, source_target_pairs={{0,1},{1,0},{2,3},{3,2},{4,5},{5,4},{6,7},{7,6},{8,9},{9,8},{10,11... | collective-permute-start | bytes 2752520 | tf_op jit(solution)/shard_map/ppermute | solution.py:260
  19.0 4.5 %collective-permute-start.2 = (bf16[448,1024]{1,0:T(8,128)(2,1)S(1)}, bf16[448,1024]{1,0:T(8,128)(2,1)}, u32[]{:S(2)}, u32[]{:S(2)}) collective-permute-start(bf16[448,1024]{1,0:T(8,128)(2,1)S(1)} %bitcast.42), channel_id=1, source_target_pairs={{0,1},{1,0},{2,3},{3,2},{4,5},{5,4},{6,7},{7,6},{8,9},{9,8},{10,11... | collective-permute-start | bytes 2752520 | tf_op jit(solution)/shard_map/ppermute | solution.py:261
  55.9 30.0 %collective-permute-start.8 = (bf16[96,2048]{1,0:T(8,128)(2,1)S(1)}, bf16[96,2048]{1,0:T(8,128)(2,1)S(1)}, u32[]{:S(2)}, u32[]{:S(2)}) collective-permute-start(bf16[96,2048]{1,0:T(8,128)(2,1)S(1)} %get-tuple-element.21), channel_id=1, source_target_pairs={{0,14},{1,15},{2,0},{3,1},{4,2},{5,3},{6,4},{7,5},{8,6},{9,7},{10,... | collective-permute-start | bytes 1179656 | tf_op jit(solution)/shard_map/ppermute | solution.py:343
  66.6 16.3 %collective-permute-start.9 = (bf16[48,2048]{1,0:T(8,128)(2,1)S(1)}, bf16[48,2048]{1,0:T(8,128)(2,1)S(1)}, u32[]{:S(2)}, u32[]{:S(2)}) collective-permute-start(bf16[48,2048]{1,0:T(8,128)(2,1)S(1)} %get-tuple-element.22), channel_id=1, source_target_pairs={{0,12},{1,13},{2,14},{3,15},{4,0},{5,1},{6,2},{7,3},{8,4},{9,5},{1... | collective-permute-start | bytes 589832 | tf_op jit(solution)/shard_map/ppermute | solution.py:343
  68.8 22.4 %collective-permute-start.5 = (bf16[96,2048]{1,0:T(8,128)(2,1)S(1)}, bf16[96,2048]{1,0:T(8,128)(2,1)S(1)}, u32[]{:S(2)}, u32[]{:S(2)}) collective-permute-start(bf16[96,2048]{1,0:T(8,128)(2,1)S(1)} %get-tuple-element.18), channel_id=1, source_target_pairs={{0,2},{1,3},{2,4},{3,5},{4,6},{5,7},{6,8},{7,9},{8,10},{9,11},{10,... | collective-permute-start | bytes 1179656 | tf_op jit(solution)/shard_map/ppermute | solution.py:343
  71.9 19.3 %collective-permute-start.6 = (bf16[48,2048]{1,0:T(8,128)(2,1)S(1)}, bf16[48,2048]{1,0:T(8,128)(2,1)S(1)}, u32[]{:S(2)}, u32[]{:S(2)}) collective-permute-start(bf16[48,2048]{1,0:T(8,128)(2,1)S(1)} %get-tuple-element.19), channel_id=1, source_target_pairs={{0,4},{1,5},{2,6},{3,7},{4,8},{5,9},{6,10},{7,11},{8,12},{9,13},{1... | collective-permute-start | bytes 589832 | tf_op jit(solution)/shard_map/ppermute | solution.py:343
  79.4 18.8 %collective-permute-start.3 = (bf16[96,2048]{1,0:T(8,128)(2,1)S(1)}, bf16[96,2048]{1,0:T(8,128)(2,1)S(1)}, u32[]{:S(2)}, u32[]{:S(2)}) collective-permute-start(bf16[96,2048]{1,0:T(8,128)(2,1)S(1)} %get-tuple-element.15), channel_id=1, source_target_pairs={{0,2},{1,3},{2,4},{3,5},{4,6},{5,7},{6,8},{7,9},{8,10},{9,11},{10,... | collective-permute-start | bytes 1179656 | tf_op jit(solution)/shard_map/ppermute | solution.py:343
  82.8 15.3 %collective-permute-start.4 = (bf16[96,2048]{1,0:T(8,128)(2,1)S(1)}, bf16[96,2048]{1,0:T(8,128)(2,1)S(1)}, u32[]{:S(2)}, u32[]{:S(2)}) collective-permute-start(bf16[96,2048]{1,0:T(8,128)(2,1)S(1)} %get-tuple-element.16), channel_id=1, source_target_pairs={{0,14},{1,15},{2,0},{3,1},{4,2},{5,3},{6,4},{7,5},{8,6},{9,7},{10,... | collective-permute-start | bytes 1179656 | tf_op jit(solution)/shard_map/ppermute | solution.py:343
  86.1 20.9 %collective-permute-start.10 = (bf16[96,2048]{1,0:T(8,128)(2,1)S(1)}, bf16[96,2048]{1,0:T(8,128)(2,1)S(1)}, u32[]{:S(2)}, u32[]{:S(2)}) collective-permute-start(bf16[96,2048]{1,0:T(8,128)(2,1)S(1)} %add_convert_fusion), channel_id=1, source_target_pairs={{0,12},{1,13},{2,14},{3,15},{4,0},{5,1},{6,2},{7,3},{8,4},{9,5},{1... | collective-permute-start | bytes 1179656 | tf_op jit(solution)/shard_map/ppermute | solution.py:343
  91.3 21.5 %collective-permute-start.7 = (bf16[96,2048]{1,0:T(8,128)(2,1)S(1)}, bf16[96,2048]{1,0:T(8,128)(2,1)S(1)}, u32[]{:S(2)}, u32[]{:S(2)}) collective-permute-start(bf16[96,2048]{1,0:T(8,128)(2,1)S(1)} %add_convert_fusion.1), channel_id=1, source_target_pairs={{0,4},{1,5},{2,6},{3,7},{4,8},{5,9},{6,10},{7,11},{8,12},{9,13},{1... | collective-permute-start | bytes 1179656 | tf_op jit(solution)/shard_map/ppermute | solution.py:343
  113.1 6.2 %collective-permute-start.11 = (bf16[96,1024]{1,0:T(8,128)(2,1)S(1)}, bf16[96,1024]{1,0:T(8,128)(2,1)S(1)}, u32[]{:S(2)}, u32[]{:S(2)}) collective-permute-start(bf16[96,1024]{1,0:T(8,128)(2,1)S(1)} %hidden_units.1), channel_id=1, source_target_pairs={{0,1},{1,0},{2,3},{3,2},{4,5},{5,4},{6,7},{7,6},{8,9},{9,8},{10,11... | collective-permute-start | bytes 589832 | tf_op jit(solution)/shard_map/ppermute | solution.py:385
  119.3 14.0 %collective-permute-start.12 = (bf16[192,1024]{1,0:T(8,128)(2,1)S(1)}, bf16[192,1024]{1,0:T(8,128)(2,1)S(1)}, u32[]{:S(2)}, u32[]{:S(2)}) collective-permute-start(bf16[192,1024]{1,0:T(8,128)(2,1)S(1)} %pad_maximum_fusion.2.own), channel_id=1, source_target_pairs={{0,4},{1,13},{2,6},{3,15},{4,8},{5,1},{6,10},{7,3},{8,12},{9,5},{1... | collective-permute-start | bytes 1179656 | tf_op jit(solution)/shard_map/ppermute | solution.py:383
  121.2 18.4 %collective-permute-start.16 = (bf16[192,1024]{1,0:T(8,128)(2,1)S(1)}, bf16[192,1024]{1,0:T(8,128)(2,1)S(1)}, u32[]{:S(2)}, u32[]{:S(2)}) collective-permute-start(bf16[192,1024]{1,0:T(8,128)(2,1)S(1)} %pad_maximum_fusion.2.own), channel_id=1, source_target_pairs={{0,2},{1,15},{2,4},{3,1},{4,6},{5,3},{6,8},{7,5},{8,10},{9,7},{10,... | collective-permute-start | bytes 1179656 | tf_op jit(solution)/shard_map/ppermute | solution.py:383
  133.3 12.9 %collective-permute-start.13 = (bf16[192,1024]{1,0:T(8,128)(2,1)S(1)}, bf16[192,1024]{1,0:T(8,128)(2,1)S(1)}, u32[]{:S(2)}, u32[]{:S(2)}) collective-permute-start(bf16[192,1024]{1,0:T(8,128)(2,1)S(1)} %collective-permute-done.12.far), channel_id=1, source_target_pairs={{0,2},{1,15},{2,4},{3,1},{4,6},{5,3},{6,8},{7,5},{8,10},{9,7},{10,... | collective-permute-start | bytes 1179656 | tf_op jit(solution)/shard_map/ppermute | solution.py:383
  137.0 17.2 %copy-start = (bf16[1,1024,448]{1,2,0:T(8,128)(2,1)S(1)}, bf16[1,1024,448]{1,2,0:T(8,128)(2,1)}, u32[]{:S(2)}) copy-start(bf16[1,1024,448]{1,2,0:T(8,128)(2,1)} %param.15) | copy-start | bytes 2752516
  137.0 9.2 %collective-permute-start.14 = (bf16[96,1024]{1,0:T(8,128)(2,1)S(1)}, bf16[96,1024]{1,0:T(8,128)(2,1)S(1)}, u32[]{:S(2)}, u32[]{:S(2)}) collective-permute-start(bf16[96,1024]{1,0:T(8,128)(2,1)S(1)} %slice.4), channel_id=1, source_target_pairs={{0,4},{1,13},{2,6},{3,15},{4,8},{5,1},{6,10},{7,3},{8,12},{9,5},{1... | collective-permute-start | bytes 589832 | tf_op jit(solution)/shard_map/ppermute | solution.py:383
  140.6 13.5 %collective-permute-start.17 = (bf16[384,1024]{1,0:T(8,128)(2,1)}, bf16[384,1024]{1,0:T(8,128)(2,1)S(1)}, u32[]{:S(2)}, u32[]{:S(2)}) collective-permute-start(bf16[384,1024]{1,0:T(8,128)(2,1)} %pad_maximum_fusion), channel_id=1, source_target_pairs={{0,1},{1,0},{2,3},{3,2},{4,5},{5,4},{6,7},{7,6},{8,9},{9,8},{10,11... | collective-permute-start | bytes 2359304 | tf_op jit(solution)/shard_map/ppermute | solution.py:388
  147.0 9.7 %collective-permute-start.15 = (bf16[288,1024]{1,0:T(8,128)(2,1)}, bf16[288,1024]{1,0:T(8,128)(2,1)}, u32[]{:S(2)}, u32[]{:S(2)}) collective-permute-start(bf16[288,1024]{1,0:T(8,128)(2,1)} %pad_maximum_fusion.1), channel_id=1, source_target_pairs={{0,1},{1,0},{2,3},{3,2},{4,5},{5,4},{6,7},{7,6},{8,9},{9,8},{10,11... | collective-permute-start | bytes 1769480 | tf_op jit(solution)/shard_map/ppermute | solution.py:389
  159.4 5.4 %copy-start.3 = (s32[128,8]{0,1:T(8,128)S(1)}, s32[128,8]{0,1:T(8,128)}, u32[]{:S(2)}) copy-start(s32[128,8]{0,1:T(8,128)} %param.9) | copy-start | bytes 12292
  159.4 5.4 %copy-start.4 = (s32[128,8]{0,1:T(8,128)S(1)}, s32[128,8]{0,1:T(8,128)}, u32[]{:S(2)}) copy-start(s32[128,8]{0,1:T(8,128)} %param.10) | copy-start | bytes 12292
  159.4 5.4 %copy-start.5 = (s32[32]{0:T(128)S(1)}, s32[32]{0:T(128)}, u32[]{:S(2)}) copy-start(s32[32]{0:T(128)} %param.11) | copy-start | bytes 388
  159.4 5.4 %copy-start.6 = (s32[32]{0:T(128)S(1)}, s32[32]{0:T(128)}, u32[]{:S(2)}) copy-start(s32[32]{0:T(128)} %param.12) | copy-start | bytes 388
  159.4 40.9 %all-to-all-start.1 = ((bf16[32,24,896]{2,1,0:T(8,128)(2,1)}), bf16[32,24,896]{2,1,0:T(8,128)(2,1)S(1)}, u32[]{:S(2)}, u32[]{:S(2)}) async-start(bf16[32,24,896]{2,1,0:T(8,128)(2,1)} %bitcast.32), calls=%async_computation.1 | async-start | bytes 2752512 | tf_op jit(solution)/shard_map/all_to_all | solution.py:426

commit v5 on v4

--- a/solution.py
+++ b/solution.py
@@ -8,8 +8,9 @@
 from jax.sharding import PartitionSpec as P
 
 HALF = 24
-ROOM = 77824
 HELD = 20
+ORDER = (3, 4, 2, 1, 0)
+FAR, NEAR = ORDER[:2], ORDER[2:]
 PIECES = 4
 STRIP = 256
 
@@ -47,9 +48,7 @@
     return jnp.where((named > 0.0) & (before < limit), before, -1.0)
 
 
-def table_kernel(
-    core, routes, capacity, spill, tokens, kept, named, limits, features, pick, sem
-):
+def pick_kernel(routes, capacity, spill, tokens, rows, named, limits, features, held, sem):
     copies = [
         pltpu.make_async_copy(routes, named, sem.at[0]),
         pltpu.make_async_copy(capacity, limits.at[0:1], sem.at[1]),
@@ -62,46 +61,28 @@
         copy.wait()
     rank = ranks(named[...], limits[0:1, :], limits[1:2, :])
     experts, count = rank.shape
-    slot = lax.broadcasted_iota(jnp.int32, (experts, HALF, count), 1) + core[0] * HALF
-    chosen = jnp.where(rank[:, None, :] == slot.astype(jnp.float32), 1.0, 0.0)
-    pick[...] = chosen.reshape(experts * HALF, count).astype(jnp.bfloat16)
+    slot = lax.broadcasted_iota(jnp.int32, (experts, HALF, count), 1).astype(jnp.float32)
     copies[3].wait()
-    size = experts * HALF
-    stores = [
-        pltpu.make_async_copy(pick, kept.at[pl.ds(0, size)], sem.at[4]),
-        pltpu.make_async_copy(features, kept.at[pl.ds(size, features.shape[0])], sem.at[5]),
-    ]
-    for copy in stores:
-        copy.start()
-    for copy in stores:
-        copy.wait()
-
-
-def pick_kernel(kept, tokens_other, rows, pick, features, held, sem):
-    size = pick.shape[0]
-    depth = tokens_other.shape[0]
-    loads = [
-        pltpu.make_async_copy(kept.at[pl.ds(0, size)], pick, sem.at[PIECES]),
-        pltpu.make_async_copy(
-            kept.at[pl.ds(size, depth)], features.at[pl.ds(0, depth)], sem.at[PIECES + 1]
-        ),
-    ]
-    for copy in loads:
-        copy.start()
-    features[depth:, :] = tokens_other[...]
-    for copy in loads:
-        copy.wait()
-    piece = size // PIECES
-    copies = []
+    width = features.shape[0]
+    piece = experts * HALF // PIECES
+    picks = []
+    for half in range(2):
+        chosen = jnp.where(rank[:, None, :] == slot + half * HALF, 1.0, 0.0)
+        picks.append(chosen.reshape(experts * HALF, count).astype(jnp.bfloat16))
+    stores = []
     for k in range(PIECES):
         at = pl.ds(k * piece, piece)
-        picked = lax.dot_general(
-            pick[at, :], features[...], NT, preferred_element_type=jnp.float32
-        )
-        held[at, :] = picked.astype(jnp.bfloat16)
-        copies.append(pltpu.make_async_copy(held.at[at], rows.at[at], sem.at[k]))
-        copies[-1].start()
-    for copy in copies:
+        for half in range(2):
+            picked = lax.dot_general(
+                picks[half][k * piece : (k + 1) * piece],
+                features[...],
+                NT,
+                preferred_element_type=jnp.float32,
+            )
+            held[at, half * width : (half + 1) * width] = picked.astype(jnp.bfloat16)
+        stores.append(pltpu.make_async_copy(held.at[at], rows.at[at], sem.at[4 + k]))
+        stores[-1].start()
+    for copy in stores:
         copy.wait()
 
 
@@ -137,7 +118,15 @@
         store.wait()
 
 
-def project_kernel(parts, chips, rows, weights, *refs):
+def held_rows(chip, part):
+    return part // 2 if chip in (0, 4) else part
+
+
+def order_kernel(rows, after, same):
+    del rows, after, same
+
+
+def project_kernel(places, rows, taken, weights, *refs, chips, part):
     outs, (picked, weight, came) = refs[:-3], refs[-3:]
     features = rows.shape[1] // 2
     strips = weights.shape[2] // STRIP
@@ -152,22 +141,40 @@
             )
             copy.start()
             fetched.append(copy)
-    depth = picked.shape[0] // len(parts)
-    for n, (chip, _) in enumerate(parts):
-        start = pl.multiple_of(chips[chip] * depth, depth)
-        picked[n * depth : (n + 1) * depth, :] = rows[pl.ds(start, depth), :]
+    low = 0
+    for chip in chips:
+        size = held_rows(chip, part)
+        start = pl.multiple_of(places[chip], part // 2)
+        own = rows[pl.ds(start, size), :]
+        other = taken[pl.ds(start, size), :]
+        for half in range(2):
+            at = slice(low, low + size)
+            lanes = slice(half * features, (half + 1) * features)
+            picked[at, 0:features] = own[:, lanes]
+            picked[at, features : 2 * features] = other[:, lanes]
+            low += size
     for strip in range(strips):
         for copy in fetched[strip * len(sources) : (strip + 1) * len(sources)]:
             copy.wait()
         value = jnp.dot(picked[...], weight[strip], preferred_element_type=jnp.float32)
         value = value.astype(jnp.bfloat16)
-        at = slice(strip * 2 * STRIP, (strip + 1) * 2 * STRIP)
-        out = iter(outs)
-        for n, (_, sizes) in enumerate(parts):
-            low = n * depth
-            for size in sizes:
-                next(out)[:, at] = value[low : low + size]
-                low += size
+        low = 0
+        for chip, out in zip(chips, outs):
+            size = 2 * held_rows(chip, part)
+            out[:, strip * 2 * STRIP : (strip + 1) * 2 * STRIP] = value[low : low + size]
+            low += size
+
+
+def add_kernel(core, first, second, half, total):
+    size = half.shape[0] // 2
+    low = core[0] == 0
+    for n in range(2):
+        for blocks in range(2):
+            at = slice((2 * n + blocks) * size, (2 * n + blocks + 1) * size)
+            value = first[at, :].astype(jnp.float32) + second[at, :].astype(jnp.float32)
+            more = half[n * size : (n + 1) * size, :].astype(jnp.float32)
+            mine = low if blocks == 0 else jnp.logical_not(low)
+            total[at, :] = jnp.where(mine, value + more, value).astype(jnp.bfloat16)
 
 
 def hidden_kernel(*refs):
@@ -256,41 +263,25 @@
     up = up_weight[0]
     down = down_weight[0].T
 
-    tokens_other = lax.ppermute(own_tokens, "dp", swap)
     gate_other = lax.ppermute(gate, "dp", swap)
     up_other = lax.ppermute(up, "dp", swap)
 
-    kept = pl.pallas_call(
-        table_kernel,
-        out_shape=jax.ShapeDtypeStruct((ROOM, count), bf16),
-        in_specs=[SMEM] + [HBM] * 4,
+    send = pl.pallas_call(
+        pick_kernel,
+        out_shape=jax.ShapeDtypeStruct((experts * HALF, 2 * features), bf16),
+        in_specs=[HBM] * 4,
         out_specs=HBM,
         scratch_shapes=[
             pltpu.VMEM(own_routes.shape, jnp.int32),
             pltpu.VMEM((2, experts), jnp.int32),
             pltpu.VMEM((features, count), bf16),
-            pltpu.VMEM((experts * HALF, count), bf16),
-            pltpu.SemaphoreType.DMA((6,)),
+            pltpu.VMEM((experts * HALF, 2 * features), bf16),
+            pltpu.SemaphoreType.DMA((4 + PIECES,)),
         ],
         compiler_params=pltpu.CompilerParams(vmem_limit_bytes=60 * 1024 * 1024),
-        cost_estimate=cost(2 * experts * count * count, 600000),
-        name="pick_table",
-    )(core, own_routes, cap_row, spill_row, own_tokens)
-    send = pl.pallas_call(
-        pick_kernel,
-        out_shape=jax.ShapeDtypeStruct((experts * HALF, 2 * features), bf16),
-        in_specs=[HBM, VMEM],
-        out_specs=HBM,
-        scratch_shapes=[
-            pltpu.VMEM((experts * HALF, count), bf16),
-            pltpu.VMEM((2 * features, count), bf16),
-            pltpu.VMEM((experts * HALF, 2 * features), bf16),
-            pltpu.SemaphoreType.DMA((PIECES + 2,)),
-        ],
-        compiler_params=pltpu.CompilerParams(vmem_limit_bytes=48 * 1024 * 1024),
         cost_estimate=cost(2 * experts * HALF * count * 2 * features, 2000000),
         name="pick_rows",
-    )(kept, tokens_other)
+    )(own_routes, cap_row, spill_row, own_tokens)
     got = lax.all_to_all(
         send.reshape(groups, HALF, 2 * features), "ep", split_axis=0, concat_axis=0, tiled=True
     ).reshape(groups * HALF, 2 * features)
@@ -312,67 +303,44 @@
     )(gate, gate_other, up, up_other)
     strips = units // STRIP
     part = depth // planes
-    half = part // 2
     plane = lax.axis_index("dp") // 2
-    chips = jnp.stack([(plane + k) % planes for k in range(planes)]).astype(jnp.int32)
-
-    def project(parts, name):
-        shapes = [
-            jax.ShapeDtypeStruct((size, 2 * units), bf16) for _, sizes in parts for size in sizes
+    sense = 1 - 2 * core[0]
+
+    places = jnp.stack(
+        [
+            (plane + sense * k + planes) % planes * part + (core[0] * part // 2 if k in (0, 4) else 0)
+            for k in range(5)
         ]
-        held = len(parts) * part
+    ).astype(jnp.int32)
+    anywhere = pl.BlockSpec(memory_space=pl.ANY)
+    got = pl.pallas_call(
+        order_kernel,
+        out_shape=jax.ShapeDtypeStruct(got.shape, bf16),
+        in_specs=[anywhere] * 2,
+        out_specs=anywhere,
+        input_output_aliases={0: 0},
+        compiler_params=LIMIT,
+        cost_estimate=cost(0, 1000),
+        name="after_weights",
+    )(got, weights)
+    taken = lax.ppermute(got, "dp", swap)
+
+    def project(chips, name):
+        sizes = [2 * held_rows(chip, part) for chip in chips]
         return pl.pallas_call(
-            functools.partial(project_kernel, parts),
-            out_shape=shapes,
-            in_specs=[SMEM, VMEM, HBM],
-            out_specs=[VMEM] * len(shapes),
+            functools.partial(project_kernel, chips=chips, part=part),
+            out_shape=[jax.ShapeDtypeStruct((size, 2 * units), bf16) for size in sizes],
+            in_specs=[SMEM, VMEM, VMEM, HBM],
+            out_specs=[VMEM] * len(sizes),
             scratch_shapes=[
-                pltpu.VMEM((held, 2 * features), bf16),
+                pltpu.VMEM((sum(sizes), 2 * features), bf16),
                 pltpu.VMEM((strips, 2 * features, 2 * STRIP), bf16),
                 pltpu.SemaphoreType.DMA((4 * strips,)),
             ],
             compiler_params=pltpu.CompilerParams(vmem_limit_bytes=48 * 1024 * 1024),
-            cost_estimate=cost(2 * held * 2 * features * 2 * units, 6000000),
+            cost_estimate=cost(2 * sum(sizes) * 2 * features * 2 * units, 6000000),
             name=name,
-        )(chips, got, weights)
-
-    def hop(rows, hops):
-        steps = [
-            (2 * z + c, 2 * ((z + hops) % planes) + c) for z in range(planes) for c in range(2)
-        ]
-        return lax.ppermute(rows, "dp", steps)
-
-    def add(*terms):
-        return sum(term.astype(jnp.float32) for term in terms).astype(bf16)
-
-    up3, down3, up4, down4 = project(
-        ((3, (part,)), (planes - 3, (part,)), (4, (half, half))), "project_in_far"
-    )
-    here, up1, down1, up2, down2 = project(
-        tuple((k % planes, (part,)) for k in (0, 1, -1, 2, -2)), "project_in_near"
-    )
-    rest = jnp.zeros((half, 2 * units), bf16)
-    up2 = add(up2, hop(up3, 1), jnp.concatenate([hop(up4, 2), rest]))
-    down2 = add(down2, hop(down3, -1), jnp.concatenate([rest, hop(down4, -2)]))
-    terms = (here, hop(up1, 1), hop(down1, -1), hop(up2, 2), hop(down2, -2))
-    weigh = pl.pallas_call(
-        weigh_kernel,
-        out_shape=jax.ShapeDtypeStruct((2, 2 * count, experts * HALF), bf16),
-        in_specs=[VMEM] * 4,
-        out_specs=VMEM,
-        compiler_params=LIMIT,
-        cost_estimate=cost(2 * experts * count * count, 4000000),
-        name="weigh_table",
-    )(own_routes, own_weights, cap_row, spill_row)
-    hidden = pl.pallas_call(
-        hidden_kernel,
-        out_shape=jax.ShapeDtypeStruct((part, units), bf16),
-        in_specs=[VMEM] * len(terms),
-        out_specs=VMEM,
-        compiler_params=LIMIT,
-        cost_estimate=cost(8 * part * units, 2200000),
-        name="hidden_units",
-    )(*terms)
+        )(places, got, taken, weights)
 
     def flow(rows, hops):
         steps = [
@@ -382,14 +350,48 @@
         ]
         return lax.ppermute(rows, "dp", steps)
 
-    own = jnp.concatenate([hidden, lax.ppermute(hidden, "dp", swap)], axis=0)
-    near, far = flow(own, 1), flow(own, 2)
-    third, fourth = flow(far, 1), flow(far[:part], 2)
+    def add(first, second, half, name):
+        return pl.pallas_call(
+            add_kernel,
+            out_shape=jax.ShapeDtypeStruct((2 * part, 2 * units), bf16),
+            in_specs=[SMEM] + [VMEM] * 3,
+            out_specs=VMEM,
+            compiler_params=LIMIT,
+            cost_estimate=cost(6 * part * units, 3000000),
+            name=name,
+        )(core, first, second, half)
+
+    third, fourth = project(FAR, "project_in_far")
+    second, first, here = project(NEAR, "project_in_near")
+    second = add(second, flow(third, 1), flow(fourth, 2), "add_passing")
+    reached = add(flow(first, 1), flow(second, 2), here, "add_reached")
+    terms = (reached, lax.ppermute(reached, "dp", swap))
+    weigh = pl.pallas_call(
+        weigh_kernel,
+        out_shape=jax.ShapeDtypeStruct((2, 2 * count, experts * HALF), bf16),
+        in_specs=[VMEM] * 4,
+        out_specs=VMEM,
+        compiler_params=LIMIT,
+        cost_estimate=cost(2 * experts * count * count, 4000000),
+        name="weigh_table",
+    )(own_routes, own_weights, cap_row, spill_row)
+    hidden = pl.pallas_call(
+        hidden_kernel,
+        out_shape=jax.ShapeDtypeStruct((2 * part, units), bf16),
+        in_specs=[VMEM] * len(terms),
+        out_specs=VMEM,
+        compiler_params=LIMIT,
+        cost_estimate=cost(8 * part * units, 2000000),
+        name="hidden_units",
+    )(*terms)
+
+    near, far = flow(hidden, 1), flow(hidden, 2)
+    far_half = jnp.where(core[0] == 0, far[:part], far[part:])
+    third, fourth = flow(far, 1), flow(far_half, 2)
     swapped_pair = lax.ppermute(jnp.concatenate([near, far], axis=0), "dp", swap)
     swapped_last = lax.ppermute(jnp.concatenate([third, fourth], axis=0), "dp", swap)
-    sense = 2 * core[0] - 1
-    offsets = [0, sense, 2 * sense, -sense, -2 * sense, 3 * sense, -3 * sense, 4]
-    orders = [core[0]] * 3 + [1 - core[0]] * 2 + [core[0], 1 - core[0], core[0]]
+    offsets = [0, -sense, -2 * sense, sense, 2 * sense, -3 * sense, 3 * sense, 4]
+    orders = [core[0] * 0] * 7 + [core[0]]
     places = jnp.stack(
         [jnp.stack([(plane + chip + planes) % planes for chip in offsets]), jnp.stack(orders)]
     ).astype(jnp.int32)
@@ -410,7 +412,7 @@
         compiler_params=LIMIT,
         cost_estimate=cost(20 * part * units * features, 4000000),
         name="project_out_early",
-    )(places, own, near, far, swapped_pair, down)
+    )(places, hidden, near, far, swapped_pair, down)
     back = pl.pallas_call(
         late_kernel,
         out_shape=back_shape,

time: 203 us -> 196 us (0.966)
  starting transfers between devices: 81.3 us -> 67.9 us
  waiting for transfers between devices: 94.1 us -> 103 us
    ppermute x10 -> x2, starting transfers between devices: 38.7 us -> 5.77 us  [the longest x1 3.85 us: on_device(): taken = lax.ppermute(got, 'dp', swap)]
    ppermute x4 -> x8, waiting for transfers between devices: 9.54 us -> 36.5 us  [flow(): return lax.ppermute(rows, 'dp', steps)]
    ppermute x4 -> x8, starting transfers between devices: 12.8 us -> 37.4 us  [flow(): return lax.ppermute(rows, 'dp', steps)]
    ppermute x10 -> x2, waiting for transfers between devices: 21.8 us -> 4.77 us  [the longest x1 2.52 us: on_device(): taken = lax.ppermute(got, 'dp', swap)]
    ppermute x1, starting transfers between devices: 6.78 us -> 3 us  [on_device(): lax.ppermute(jnp.concatenate([third, fourth], axis=0), 'dp', swap)]
    pallas_call x4 -> x6, Pallas kernels: 10.6 us -> 9.69 us  [the longest x2 8.67 us: project(): pl.pallas_call(functools.partial(project_kernel, chips=chips, part=part),...]
  transfers between devices with their start and end apart: 20 -> 16, of which waited for: 10 -> 11; matrix products, arithmetic and copies ran while one was open for 1% -> 1% of each run, Pallas kernels for 6% -> 6%
where the time goes in v5:
time: 196 us
  waiting for transfers between devices  103 us (53%)
  starting transfers between devices  67.9 us (35%)
  Pallas kernels  22 us (11%)
    ppermute x8, starting transfers between devices, flow(): return lax.ppermute(rows, 'dp', steps)  37.4 us
    ppermute x8, waiting for transfers between devices, flow(): return lax.ppermute(rows, 'dp', steps)  36.5 us
    all_to_all x1, waiting for transfers between devices, on_device(): values = lax.all_to_all(back, 'ep', split_axis=0, concat_axis=0, tiled=True)  35 us
    all_to_all x1, waiting for transfers between devices, on_device(): lax.all_to_all(send.reshape(groups, HALF, 2 * features), 'ep', split_axis...  24.3 us
    all_to_all x1, starting transfers between devices, on_device(): lax.all_to_all(send.reshape(groups, HALF, 2 * features), 'ep', split_axis...  9.75 us
    pallas_call x2, Pallas kernels, project(): pl.pallas_call(functools.partial(project_kernel, chips=chips, part=part),...  8.67 us
    all_to_all x1, starting transfers between devices, on_device(): values = lax.all_to_all(back, 'ep', split_axis=0, concat_axis=0, tiled=True)  5.01 us
  transfers between devices with their start and end apart: 16, of which 11 were waited for; matrix products, arithmetic and copies ran while one was open for 1% of the time, Pallas kernels for 6%

profile of v5, /device:TPU:9, one launch (start us, length us, event | category | flops | bytes accessed | tf_op | source)
XLA Modules:
  0.0 195.5 jit_solution(9925435453677867056)
XLA Ops:
  0.0 2.5 %pick_rows.1 = bf16[768,896]{1,0:T(8,128)(2,1)} custom-call(s32[8,128]{1,0:T(8,128)} %bitcast.40, s32[1,32]{1,0:T(1,128)} %bitcast.43, s32[1,32]{1,0:T(1,128)} %bitcast.45, bf16[448,128]{1,0:T(8,128)(2,1)} %bitcast.48), custom_call_target="tpu_custom_call" | custom-call | flops 176160768 | bytes 2000000 | tf_op jit(solution)/shard_map/pick_rows/pallas_call | solution.py:269
  2.5 0.0 copy-start.1
  2.5 0.0 copy-start.2
  2.5 9.8 %all-to-all-start = ((bf16[32,24,896]{2,1,0:T(8,128)(2,1)}), bf16[32,24,896]{2,1,0:T(8,128)(2,1)S(1)}, u32[]{:S(2)}, u32[]{:S(2)}) async-start(bf16[32,24,896]{2,1,0:T(8,128)(2,1)} %bitcast.47), calls=%async_computation | async-start | bytes 2752512 | tf_op jit(solution)/shard_map/all_to_all | solution.py:285
  12.2 0.0 copy-done.1
  12.3 3.1 %collective-permute-start = (bf16[448,1024]{1,0:T(8,128)(2,1)S(1)}, bf16[448,1024]{1,0:T(8,128)(2,1)S(1)}, u32[]{:S(2)}, u32[]{:S(2)}) collective-permute-start(bf16[448,1024]{1,0:T(8,128)(2,1)S(1)} %bitcast.36), channel_id=1, source_target_pairs={{0,1},{1,0},{2,3},{3,2},{4,5},{5,4},{6,7},{7,6},{8,9},{9,8},{10,11... | collective-permute-start | bytes 2752520 | tf_op jit(solution)/shard_map/ppermute | solution.py:266
  15.4 0.0 copy-done.2
  15.4 1.9 collective-permute-start.1
  17.3 0.1 collective-permute-done.gate_other
  17.5 2.3 %collective-permute-done.1.up_other = bf16[448,1024]{1,0:T(8,128)(2,1)S(1)} collective-permute-done((bf16[448,1024]{1,0:T(8,128)(2,1)S(1)}, bf16[448,1024]{1,0:T(8,128)(2,1)S(1)}, u32[]{:S(2)}, u32[]{:S(2)}) %collective-permute-start.1) | collective-permute-done | bytes 917536 | tf_op jit(solution)/shard_map/ppermute | solution.py:267
  19.8 2.7 %gather_weights.1.after.weights = bf16[20,448,1024]{2,1,0:T(8,128)(2,1)} custom-call(bf16[448,1024]{1,0:T(8,128)(2,1)S(1)} %bitcast.37, bf16[448,1024]{1,0:T(8,128)(2,1)S(1)} %collective-permute-done.gate_other, bf16[448,1024]{1,0:T(8,128)(2,1)S(1)} %bitcast.39, bf16[448,1024]{1,0:T(8,128)(2,1)S(1)} %collective-permute-done.1.up_other), custom_call_target="tpu_custom_call" | custom-call | bytes 7400000 | tf_op jit(solution)/shard_map/gather_weights/pallas_call | solution.py:290
  22.5 24.3 %all-to-all-done = bf16[32,24,896]{2,1,0:T(8,128)(2,1)S(1)} async-done(((bf16[32,24,896]{2,1,0:T(8,128)(2,1)}), bf16[32,24,896]{2,1,0:T(8,128)(2,1)S(1)}, u32[]{:S(2)}, u32[]{:S(2)}) %all-to-all-start) | async-done | bytes 1376288 | tf_op jit(solution)/shard_map/all_to_all | solution.py:285
  46.8 3.9 %collective-permute-start.2 = (bf16[768,896]{1,0:T(8,128)(2,1)S(1)}, bf16[768,896]{1,0:T(8,128)(2,1)S(1)}, u32[]{:S(2)}, u32[]{:S(2)}) collective-permute-start(bf16[768,896]{1,0:T(8,128)(2,1)S(1)} %after_weights.1.rows), channel_id=1, source_target_pairs={{0,1},{1,0},{2,3},{3,2},{4,5},{5,4},{6,7},{7,6},{8,9},{9,8},{10,11... | collective-permute-start | bytes 4128776 | tf_op jit(solution)/shard_map/ppermute | solution.py:326
  50.8 0.1 stack.75.places
  50.9 2.5 %collective-permute-done.2.taken = bf16[768,896]{1,0:T(8,128)(2,1)S(1)} collective-permute-done((bf16[768,896]{1,0:T(8,128)(2,1)S(1)}, bf16[768,896]{1,0:T(8,128)(2,1)S(1)}, u32[]{:S(2)}, u32[]{:S(2)}) %collective-permute-start.2) | collective-permute-done | bytes 1376288 | tf_op jit(solution)/shard_map/ppermute | solution.py:326
  53.4 3.9 %project_in_far.1 = (bf16[192,2048]{1,0:T(8,128)(2,1)S(1)}, bf16[96,2048]{1,0:T(8,128)(2,1)S(1)}) custom-call(s32[5]{0:T(128)S(1)} %stack.75.places, bf16[768,896]{1,0:T(8,128)(2,1)S(1)} %after_weights.1.rows, bf16[768,896]{1,0:T(8,128)(2,1)S(1)} %collective-permute-done.2.taken, bf16[20,448,1024]{2,1,0:T(8,128)(2,1)} %gather_weights.1.after.weights), custom_call_target="tpu_custom_call" | custom-call | flops 1056964608 | bytes 6000000 | tf_op jit(solution)/shard_map/project_in_far/pallas_call | solution.py:330
  57.3 10.7 %collective-permute-start.4 = (bf16[192,2048]{1,0:T(8,128)(2,1)S(1)}, bf16[192,2048]{1,0:T(8,128)(2,1)S(1)}, u32[]{:S(2)}, u32[]{:S(2)}) collective-permute-start(bf16[192,2048]{1,0:T(8,128)(2,1)S(1)} %get-tuple-element.12), channel_id=1, source_target_pairs={{0,2},{1,15},{2,4},{3,1},{4,6},{5,3},{6,8},{7,5},{8,10},{9,7},{10,... | collective-permute-start | bytes 2359304 | tf_op jit(solution)/shard_map/ppermute | solution.py:351
  68.0 2.2 %collective-permute-start.5 = (bf16[96,2048]{1,0:T(8,128)(2,1)S(1)}, bf16[96,2048]{1,0:T(8,128)(2,1)S(1)}, u32[]{:S(2)}, u32[]{:S(2)}) collective-permute-start(bf16[96,2048]{1,0:T(8,128)(2,1)S(1)} %get-tuple-element.13), channel_id=1, source_target_pairs={{0,4},{1,13},{2,6},{3,15},{4,8},{5,1},{6,10},{7,3},{8,12},{9,5},{1... | collective-permute-start | bytes 1179656 | tf_op jit(solution)/shard_map/ppermute | solution.py:351
  70.2 4.8 %project_in_near.1 = (bf16[192,2048]{1,0:T(8,128)(2,1)S(1)}, bf16[192,2048]{1,0:T(8,128)(2,1)S(1)}, bf16[96,2048]{1,0:T(8,128)(2,1)S(1)}) custom-call(s32[5]{0:T(128)S(1)} %stack.75.places, bf16[768,896]{1,0:T(8,128)(2,1)S(1)} %after_weights.1.rows, bf16[768,896]{1,0:T(8,128)(2,1)S(1)} %collective-permute-done.2.taken, ...), custom_call_target="tpu_custom_call" | custom-call | flops 1761607680 | bytes 6000000 | tf_op jit(solution)/shard_map/project_in_near/pallas_call | solution.py:330
  75.0 2.2 %collective-permute-start.3 = (bf16[192,2048]{1,0:T(8,128)(2,1)S(1)}, bf16[192,2048]{1,0:T(8,128)(2,1)S(1)}, u32[]{:S(2)}, u32[]{:S(2)}) collective-permute-start(bf16[192,2048]{1,0:T(8,128)(2,1)S(1)} %get-tuple-element.10), channel_id=1, source_target_pairs={{0,2},{1,15},{2,4},{3,1},{4,6},{5,3},{6,8},{7,5},{8,10},{9,7},{10,... | collective-permute-start | bytes 2359304 | tf_op jit(solution)/shard_map/ppermute | solution.py:351
  77.2 8.2 %collective-permute-done.5.half = bf16[96,2048]{1,0:T(8,128)(2,1)S(1)} collective-permute-done((bf16[96,2048]{1,0:T(8,128)(2,1)S(1)}, bf16[96,2048]{1,0:T(8,128)(2,1)S(1)}, u32[]{:S(2)}, u32[]{:S(2)}) %collective-permute-start.5) | collective-permute-done | bytes 393248 | tf_op jit(solution)/shard_map/ppermute | solution.py:351
  85.4 0.0 collective-permute-done.4.second
  85.4 0.3 add_passing.1
  85.7 6.0 %collective-permute-start.6 = (bf16[192,2048]{1,0:T(8,128)(2,1)S(1)}, bf16[192,2048]{1,0:T(8,128)(2,1)S(1)}, u32[]{:S(2)}, u32[]{:S(2)}) collective-permute-start(bf16[192,2048]{1,0:T(8,128)(2,1)S(1)} %add_passing.1), channel_id=1, source_target_pairs={{0,4},{1,13},{2,6},{3,15},{4,8},{5,1},{6,10},{7,3},{8,12},{9,5},{1... | collective-permute-start | bytes 2359304 | tf_op jit(solution)/shard_map/ppermute | solution.py:351
  91.7 10.5 %collective-permute-done.3.first = bf16[192,2048]{1,0:T(8,128)(2,1)S(1)} collective-permute-done((bf16[192,2048]{1,0:T(8,128)(2,1)S(1)}, bf16[192,2048]{1,0:T(8,128)(2,1)S(1)}, u32[]{:S(2)}, u32[]{:S(2)}) %collective-permute-start.3) | collective-permute-done | bytes 786464 | tf_op jit(solution)/shard_map/ppermute | solution.py:351
  102.2 8.4 %collective-permute-done.6.second = bf16[192,2048]{1,0:T(8,128)(2,1)S(1)} collective-permute-done((bf16[192,2048]{1,0:T(8,128)(2,1)S(1)}, bf16[192,2048]{1,0:T(8,128)(2,1)S(1)}, u32[]{:S(2)}, u32[]{:S(2)}) %collective-permute-start.6) | collective-permute-done | bytes 786464 | tf_op jit(solution)/shard_map/ppermute | solution.py:351
  110.7 0.3 add_reached.1.refs_0_
  111.0 1.9 collective-permute-start.7
  112.9 2.3 %collective-permute-done.7.refs_1_ = bf16[192,2048]{1,0:T(8,128)(2,1)S(1)} collective-permute-done((bf16[192,2048]{1,0:T(8,128)(2,1)S(1)}, bf16[192,2048]{1,0:T(8,128)(2,1)S(1)}, u32[]{:S(2)}, u32[]{:S(2)}) %collective-permute-start.7) | collective-permute-done | bytes 786464 | tf_op jit(solution)/shard_map/ppermute | solution.py:368
  115.2 0.4 hidden_units.1.own
  115.5 5.9 %collective-permute-start.8 = (bf16[192,1024]{1,0:T(8,128)(2,1)S(1)}, bf16[192,1024]{1,0:T(8,128)(2,1)S(1)}, u32[]{:S(2)}, u32[]{:S(2)}) collective-permute-start(bf16[192,1024]{1,0:T(8,128)(2,1)S(1)} %hidden_units.1.own), channel_id=1, source_target_pairs={{0,4},{1,13},{2,6},{3,15},{4,8},{5,1},{6,10},{7,3},{8,12},{9,5},{1... | collective-permute-start | bytes 1179656 | tf_op jit(solution)/shard_map/ppermute | solution.py:351
  121.5 2.4 %collective-permute-start.12 = (bf16[192,1024]{1,0:T(8,128)(2,1)S(1)}, bf16[192,1024]{1,0:T(8,128)(2,1)S(1)}, u32[]{:S(2)}, u32[]{:S(2)}) collective-permute-start(bf16[192,1024]{1,0:T(8,128)(2,1)S(1)} %hidden_units.1.own), channel_id=1, source_target_pairs={{0,2},{1,15},{2,4},{3,1},{4,6},{5,3},{6,8},{7,5},{8,10},{9,7},{10,... | collective-permute-start | bytes 1179656 | tf_op jit(solution)/shard_map/ppermute | solution.py:351
  123.8 6.5 %collective-permute-done.8.far = bf16[192,1024]{1,0:T(8,128)(2,1)S(1)} collective-permute-done((bf16[192,1024]{1,0:T(8,128)(2,1)S(1)}, bf16[192,1024]{1,0:T(8,128)(2,1)S(1)}, u32[]{:S(2)}, u32[]{:S(2)}) %collective-permute-start.8) | collective-permute-done | bytes 393248 | tf_op jit(solution)/shard_map/ppermute | solution.py:351
  130.4 3.2 %collective-permute-start.9 = (bf16[192,1024]{1,0:T(8,128)(2,1)S(1)}, bf16[192,1024]{1,0:T(8,128)(2,1)S(1)}, u32[]{:S(2)}, u32[]{:S(2)}) collective-permute-start(bf16[192,1024]{1,0:T(8,128)(2,1)S(1)} %collective-permute-done.8.far), channel_id=1, source_target_pairs={{0,2},{1,15},{2,4},{3,1},{4,6},{5,3},{6,8},{7,5},{8,10},{9,7},{10,... | collective-permute-start | bytes 1179656 | tf_op jit(solution)/shard_map/ppermute | solution.py:351
  133.6 0.0 copy-start
  133.6 4.9 %collective-permute-start.10 = (bf16[96,1024]{1,0:T(8,128)(2,1)S(1)}, bf16[96,1024]{1,0:T(8,128)(2,1)S(1)}, u32[]{:S(2)}, u32[]{:S(2)}) collective-permute-start(bf16[96,1024]{1,0:T(8,128)(2,1)S(1)} %slice_select_fusion), channel_id=1, source_target_pairs={{0,4},{1,13},{2,6},{3,15},{4,8},{5,1},{6,10},{7,3},{8,12},{9,5},{1... | collective-permute-start | bytes 589832 | tf_op jit(solution)/shard_map/ppermute | solution.py:351
  138.5 0.0 collective-permute-done.12.near
  138.5 0.9 pad_maximum_fusion
  139.5 1.9 collective-permute-start.13
  141.4 2.8 %collective-permute-done.10.fourth = bf16[96,1024]{1,0:T(8,128)(2,1)S(1)} collective-permute-done((bf16[96,1024]{1,0:T(8,128)(2,1)S(1)}, bf16[96,1024]{1,0:T(8,128)(2,1)S(1)}, u32[]{:S(2)}, u32[]{:S(2)}) %collective-permute-start.10) | collective-permute-done | bytes 196640 | tf_op jit(solution)/shard_map/ppermute | solution.py:351
  144.2 0.0 collective-permute-done.9.third
  144.2 0.8 pad_maximum_fusion.1
  145.0 3.0 %collective-permute-start.11 = (bf16[288,1024]{1,0:T(8,128)(2,1)}, bf16[288,1024]{1,0:T(8,128)(2,1)}, u32[]{:S(2)}, u32[]{:S(2)}) collective-permute-start(bf16[288,1024]{1,0:T(8,128)(2,1)} %pad_maximum_fusion.1), channel_id=1, source_target_pairs={{0,1},{1,0},{2,3},{3,2},{4,5},{5,4},{6,7},{7,6},{8,9},{9,8},{10,11... | collective-permute-start | bytes 1769480 | tf_op jit(solution)/shard_map/ppermute | solution.py:392
  148.1 0.1 stack.65
  148.2 0.1 add_bitcast_fusion
  148.3 0.0 collective-permute-done.13.swapped_pair
  148.3 0.0 copy-done
  148.3 2.6 %project_out_early.1.filled = bf16[768,896]{1,0:T(8,128)(2,1)} custom-call(s32[2,8]{1,0:T(2,128)S(1)} %pad_add_fusion.places, bf16[192,1024]{1,0:T(8,128)(2,1)S(1)} %hidden_units.1.own, bf16[192,1024]{1,0:T(8,128)(2,1)S(1)} %collective-permute-done.12.near, bf16[192,1024]{1,0:T(8,128)(2,1)S(1)} %collective-permute-done.8.far, ...), custom_call_target="tpu_custom_call" | custom-call | flops 880803840 | bytes 4000000 | tf_op jit(solution)/shard_map/project_out_early/pallas_call | solution.py:406
  150.9 0.0 collective-permute-done.11.swapped
  150.9 2.7 %project_out_late.1 = bf16[768,896]{1,0:T(8,128)(2,1)} custom-call(s32[2,8]{1,0:T(2,128)S(1)} %pad_add_fusion.places, bf16[192,1024]{1,0:T(8,128)(2,1)S(1)} %collective-permute-done.9.third, bf16[96,1024]{1,0:T(8,128)(2,1)S(1)} %collective-permute-done.10.fourth, bf16[288,1024]{1,0:T(8,128)(2,1)} %collective-permute-done.11.swapped, ...), custom_call_target="tpu_custom_call", output_to_operand_aliasing={{}: (5, {})} | custom-call | flops 528482304 | bytes 4000000 | tf_op jit(solution)/shard_map/project_out_late/pallas_call | solution.py:416
  153.6 0.0 copy-start.3
  153.6 0.0 copy-start.4
  153.6 0.0 copy-start.5
  153.6 0.0 copy-start.6
  153.6 5.0 %all-to-all-start.1 = ((bf16[32,24,896]{2,1,0:T(8,128)(2,1)}), bf16[32,24,896]{2,1,0:T(8,128)(2,1)S(1)}, u32[]{:S(2)}, u32[]{:S(2)}) async-start(bf16[32,24,896]{2,1,0:T(8,128)(2,1)} %bitcast.28), calls=%async_computation.1 | async-start | bytes 2752512 | tf_op jit(solution)/shard_map/all_to_all | solution.py:428
  158.6 0.0 copy-done.3
  158.6 0.0 copy-done.4
  158.6 0.0 copy-done.5
  158.7 0.0 copy-done.6
  158.7 0.4 weigh_table.1.weigh
  159.1 35.0 %all-to-all-done.1 = bf16[32,24,896]{2,1,0:T(8,128)(2,1)S(1)} async-done(((bf16[32,24,896]{2,1,0:T(8,128)(2,1)}), bf16[32,24,896]{2,1,0:T(8,128)(2,1)S(1)}, u32[]{:S(2)}, u32[]{:S(2)}) %all-to-all-start.1) | async-done | bytes 1376288 | tf_op jit(solution)/shard_map/all_to_all | solution.py:428
  194.1 1.4 mix_rows.1
  (5 shorter events, 0.0 us)
Async XLA Ops:
  2.5 9.8 %copy-start.1 = (bf16[1,448,1024]{2,1,0:T(8,128)(2,1)S(1)}, bf16[1,448,1024]{2,1,0:T(8,128)(2,1)}, u32[]{:S(2)}) copy-start(bf16[1,448,1024]{2,1,0:T(8,128)(2,1)} %param.13) | copy-start | bytes 2752516
  2.5 12.9 %copy-start.2 = (bf16[1,448,1024]{2,1,0:T(8,128)(2,1)S(1)}, bf16[1,448,1024]{2,1,0:T(8,128)(2,1)}, u32[]{:S(2)}) copy-start(bf16[1,448,1024]{2,1,0:T(8,128)(2,1)} %param.14) | copy-start | bytes 2752516
  2.5 44.3 %all-to-all-start = ((bf16[32,24,896]{2,1,0:T(8,128)(2,1)}), bf16[32,24,896]{2,1,0:T(8,128)(2,1)S(1)}, u32[]{:S(2)}, u32[]{:S(2)}) async-start(bf16[32,24,896]{2,1,0:T(8,128)(2,1)} %bitcast.47), calls=%async_computation | async-start | bytes 2752512 | tf_op jit(solution)/shard_map/all_to_all | solution.py:285
  12.3 5.2 %collective-permute-start = (bf16[448,1024]{1,0:T(8,128)(2,1)S(1)}, bf16[448,1024]{1,0:T(8,128)(2,1)S(1)}, u32[]{:S(2)}, u32[]{:S(2)}) collective-permute-start(bf16[448,1024]{1,0:T(8,128)(2,1)S(1)} %bitcast.36), channel_id=1, source_target_pairs={{0,1},{1,0},{2,3},{3,2},{4,5},{5,4},{6,7},{7,6},{8,9},{9,8},{10,11... | collective-permute-start | bytes 2752520 | tf_op jit(solution)/shard_map/ppermute | solution.py:266
  15.4 4.4 %collective-permute-start.1 = (bf16[448,1024]{1,0:T(8,128)(2,1)S(1)}, bf16[448,1024]{1,0:T(8,128)(2,1)S(1)}, u32[]{:S(2)}, u32[]{:S(2)}) collective-permute-start(bf16[448,1024]{1,0:T(8,128)(2,1)S(1)} %bitcast.38), channel_id=1, source_target_pairs={{0,1},{1,0},{2,3},{3,2},{4,5},{5,4},{6,7},{7,6},{8,9},{9,8},{10,11... | collective-permute-start | bytes 2752520 | tf_op jit(solution)/shard_map/ppermute | solution.py:267
  46.8 6.6 %collective-permute-start.2 = (bf16[768,896]{1,0:T(8,128)(2,1)S(1)}, bf16[768,896]{1,0:T(8,128)(2,1)S(1)}, u32[]{:S(2)}, u32[]{:S(2)}) collective-permute-start(bf16[768,896]{1,0:T(8,128)(2,1)S(1)} %after_weights.1.rows), channel_id=1, source_target_pairs={{0,1},{1,0},{2,3},{3,2},{4,5},{5,4},{6,7},{7,6},{8,9},{9,8},{10,11... | collective-permute-start | bytes 4128776 | tf_op jit(solution)/shard_map/ppermute | solution.py:326
  57.3 28.1 %collective-permute-start.4 = (bf16[192,2048]{1,0:T(8,128)(2,1)S(1)}, bf16[192,2048]{1,0:T(8,128)(2,1)S(1)}, u32[]{:S(2)}, u32[]{:S(2)}) collective-permute-start(bf16[192,2048]{1,0:T(8,128)(2,1)S(1)} %get-tuple-element.12), channel_id=1, source_target_pairs={{0,2},{1,15},{2,4},{3,1},{4,6},{5,3},{6,8},{7,5},{8,10},{9,7},{10,... | collective-permute-start | bytes 2359304 | tf_op jit(solution)/shard_map/ppermute | solution.py:351
  68.0 17.4 %collective-permute-start.5 = (bf16[96,2048]{1,0:T(8,128)(2,1)S(1)}, bf16[96,2048]{1,0:T(8,128)(2,1)S(1)}, u32[]{:S(2)}, u32[]{:S(2)}) collective-permute-start(bf16[96,2048]{1,0:T(8,128)(2,1)S(1)} %get-tuple-element.13), channel_id=1, source_target_pairs={{0,4},{1,13},{2,6},{3,15},{4,8},{5,1},{6,10},{7,3},{8,12},{9,5},{1... | collective-permute-start | bytes 1179656 | tf_op jit(solution)/shard_map/ppermute | solution.py:351
  75.0 27.3 %collective-permute-start.3 = (bf16[192,2048]{1,0:T(8,128)(2,1)S(1)}, bf16[192,2048]{1,0:T(8,128)(2,1)S(1)}, u32[]{:S(2)}, u32[]{:S(2)}) collective-permute-start(bf16[192,2048]{1,0:T(8,128)(2,1)S(1)} %get-tuple-element.10), channel_id=1, source_target_pairs={{0,2},{1,15},{2,4},{3,1},{4,6},{5,3},{6,8},{7,5},{8,10},{9,7},{10,... | collective-permute-start | bytes 2359304 | tf_op jit(solution)/shard_map/ppermute | solution.py:351
  85.7 24.9 %collective-permute-start.6 = (bf16[192,2048]{1,0:T(8,128)(2,1)S(1)}, bf16[192,2048]{1,0:T(8,128)(2,1)S(1)}, u32[]{:S(2)}, u32[]{:S(2)}) collective-permute-start(bf16[192,2048]{1,0:T(8,128)(2,1)S(1)} %add_passing.1), channel_id=1, source_target_pairs={{0,4},{1,13},{2,6},{3,15},{4,8},{5,1},{6,10},{7,3},{8,12},{9,5},{1... | collective-permute-start | bytes 2359304 | tf_op jit(solution)/shard_map/ppermute | solution.py:351
  111.0 4.2 %collective-permute-start.7 = (bf16[192,2048]{1,0:T(8,128)(2,1)S(1)}, bf16[192,2048]{1,0:T(8,128)(2,1)S(1)}, u32[]{:S(2)}, u32[]{:S(2)}) collective-permute-start(bf16[192,2048]{1,0:T(8,128)(2,1)S(1)} %add_reached.1.refs_0_), channel_id=1, source_target_pairs={{0,1},{1,0},{2,3},{3,2},{4,5},{5,4},{6,7},{7,6},{8,9},{9,8},{10,11... | collective-permute-start | bytes 2359304 | tf_op jit(solution)/shard_map/ppermute | solution.py:368
  115.5 14.8 %collective-permute-start.8 = (bf16[192,1024]{1,0:T(8,128)(2,1)S(1)}, bf16[192,1024]{1,0:T(8,128)(2,1)S(1)}, u32[]{:S(2)}, u32[]{:S(2)}) collective-permute-start(bf16[192,1024]{1,0:T(8,128)(2,1)S(1)} %hidden_units.1.own), channel_id=1, source_target_pairs={{0,4},{1,13},{2,6},{3,15},{4,8},{5,1},{6,10},{7,3},{8,12},{9,5},{1... | collective-permute-start | bytes 1179656 | tf_op jit(solution)/shard_map/ppermute | solution.py:351
  121.5 17.0 %collective-permute-start.12 = (bf16[192,1024]{1,0:T(8,128)(2,1)S(1)}, bf16[192,1024]{1,0:T(8,128)(2,1)S(1)}, u32[]{:S(2)}, u32[]{:S(2)}) collective-permute-start(bf16[192,1024]{1,0:T(8,128)(2,1)S(1)} %hidden_units.1.own), channel_id=1, source_target_pairs={{0,2},{1,15},{2,4},{3,1},{4,6},{5,3},{6,8},{7,5},{8,10},{9,7},{10,... | collective-permute-start | bytes 1179656 | tf_op jit(solution)/shard_map/ppermute | solution.py:351
  130.4 13.8 %collective-permute-start.9 = (bf16[192,1024]{1,0:T(8,128)(2,1)S(1)}, bf16[192,1024]{1,0:T(8,128)(2,1)S(1)}, u32[]{:S(2)}, u32[]{:S(2)}) collective-permute-start(bf16[192,1024]{1,0:T(8,128)(2,1)S(1)} %collective-permute-done.8.far), channel_id=1, source_target_pairs={{0,2},{1,15},{2,4},{3,1},{4,6},{5,3},{6,8},{7,5},{8,10},{9,7},{10,... | collective-permute-start | bytes 1179656 | tf_op jit(solution)/shard_map/ppermute | solution.py:351
  133.6 14.7 %copy-start = (bf16[1,1024,448]{1,2,0:T(8,128)(2,1)S(1)}, bf16[1,1024,448]{1,2,0:T(8,128)(2,1)}, u32[]{:S(2)}) copy-start(bf16[1,1024,448]{1,2,0:T(8,128)(2,1)} %param.15) | copy-start | bytes 2752516
  133.6 10.5 %collective-permute-start.10 = (bf16[96,1024]{1,0:T(8,128)(2,1)S(1)}, bf16[96,1024]{1,0:T(8,128)(2,1)S(1)}, u32[]{:S(2)}, u32[]{:S(2)}) collective-permute-start(bf16[96,1024]{1,0:T(8,128)(2,1)S(1)} %slice_select_fusion), channel_id=1, source_target_pairs={{0,4},{1,13},{2,6},{3,15},{4,8},{5,1},{6,10},{7,3},{8,12},{9,5},{1... | collective-permute-start | bytes 589832 | tf_op jit(solution)/shard_map/ppermute | solution.py:351
  139.5 8.8 %collective-permute-start.13 = (bf16[384,1024]{1,0:T(8,128)(2,1)}, bf16[384,1024]{1,0:T(8,128)(2,1)S(1)}, u32[]{:S(2)}, u32[]{:S(2)}) collective-permute-start(bf16[384,1024]{1,0:T(8,128)(2,1)} %pad_maximum_fusion), channel_id=1, source_target_pairs={{0,1},{1,0},{2,3},{3,2},{4,5},{5,4},{6,7},{7,6},{8,9},{9,8},{10,11... | collective-permute-start | bytes 2359304 | tf_op jit(solution)/shard_map/ppermute | solution.py:391
  145.0 5.9 %collective-permute-start.11 = (bf16[288,1024]{1,0:T(8,128)(2,1)}, bf16[288,1024]{1,0:T(8,128)(2,1)}, u32[]{:S(2)}, u32[]{:S(2)}) collective-permute-start(bf16[288,1024]{1,0:T(8,128)(2,1)} %pad_maximum_fusion.1), channel_id=1, source_target_pairs={{0,1},{1,0},{2,3},{3,2},{4,5},{5,4},{6,7},{7,6},{8,9},{9,8},{10,11... | collective-permute-start | bytes 1769480 | tf_op jit(solution)/shard_map/ppermute | solution.py:392
  153.6 5.1 %copy-start.3 = (s32[128,8]{0,1:T(8,128)S(1)}, s32[128,8]{0,1:T(8,128)}, u32[]{:S(2)}) copy-start(s32[128,8]{0,1:T(8,128)} %param.9) | copy-start | bytes 12292
  153.6 5.1 %copy-start.4 = (s32[128,8]{0,1:T(8,128)S(1)}, s32[128,8]{0,1:T(8,128)}, u32[]{:S(2)}) copy-start(s32[128,8]{0,1:T(8,128)} %param.10) | copy-start | bytes 12292
  153.6 5.1 %copy-start.5 = (s32[32]{0:T(128)S(1)}, s32[32]{0:T(128)}, u32[]{:S(2)}) copy-start(s32[32]{0:T(128)} %param.11) | copy-start | bytes 388
  153.6 5.1 %copy-start.6 = (s32[32]{0:T(128)S(1)}, s32[32]{0:T(128)}, u32[]{:S(2)}) copy-start(s32[32]{0:T(128)} %param.12) | copy-start | bytes 388
  153.6 40.5 %all-to-all-start.1 = ((bf16[32,24,896]{2,1,0:T(8,128)(2,1)}), bf16[32,24,896]{2,1,0:T(8,128)(2,1)S(1)}, u32[]{:S(2)}, u32[]{:S(2)}) async-start(bf16[32,24,896]{2,1,0:T(8,128)(2,1)} %bitcast.28), calls=%async_computation.1 | async-start | bytes 2752512 | tf_op jit(solution)/shard_map/all_to_all | solution.py:428

commit v6 on v5

--- a/solution.py
+++ b/solution.py
@@ -9,8 +9,6 @@
 
 HALF = 24
 HELD = 20
-ORDER = (3, 4, 2, 1, 0)
-FAR, NEAR = ORDER[:2], ORDER[2:]
 PIECES = 4
 STRIP = 256
 
@@ -126,21 +124,27 @@
     del rows, after, same
 
 
-def project_kernel(places, rows, taken, weights, *refs, chips, part):
-    outs, (picked, weight, came) = refs[:-3], refs[-3:]
+def load_kernel(weights, weight, came):
+    features = weights.shape[1]
+    copies = []
+    for strip in range(weight.shape[0]):
+        for n, (low, kind) in enumerate(((0, 0), (1, 0), (0, 1), (1, 1))):
+            copies.append(
+                pltpu.make_async_copy(
+                    weights.at[n, :, pl.ds(strip * STRIP, STRIP)],
+                    weight.at[strip, pl.ds(low * features, features), pl.ds(kind * STRIP, STRIP)],
+                    came.at[4 * strip + n],
+                )
+            )
+    for copy in copies:
+        copy.start()
+    for copy in copies:
+        copy.wait()
+
+
+def project_kernel(places, rows, taken, weight, *refs, chips, part):
+    outs, picked = refs[:-1], refs[-1]
     features = rows.shape[1] // 2
-    strips = weights.shape[2] // STRIP
-    sources = ((0, 0), (1, 0), (0, 1), (1, 1))
-    fetched = []
-    for strip in range(strips):
-        for n, (low, kind) in enumerate(sources):
-            copy = pltpu.make_async_copy(
-                weights.at[n, :, pl.ds(strip * STRIP, STRIP)],
-                weight.at[strip, pl.ds(low * features, features), pl.ds(kind * STRIP, STRIP)],
-                came.at[strip * len(sources) + n],
-            )
-            copy.start()
-            fetched.append(copy)
     low = 0
     for chip in chips:
         size = held_rows(chip, part)
@@ -153,9 +157,7 @@
             picked[at, 0:features] = own[:, lanes]
             picked[at, features : 2 * features] = other[:, lanes]
             low += size
-    for strip in range(strips):
-        for copy in fetched[strip * len(sources) : (strip + 1) * len(sources)]:
-            copy.wait()
+    for strip in range(weight.shape[0]):
         value = jnp.dot(picked[...], weight[strip], preferred_element_type=jnp.float32)
         value = value.astype(jnp.bfloat16)
         low = 0
@@ -213,19 +215,19 @@
         copy.wait()
 
 
-def early_kernel(places, own, near, far, swapped_pair, down, out, held, sem):
-    rows = jnp.concatenate([own[...], near[...], far[...]], axis=0)
-    parts = ((rows, (0, 1, 2)), (swapped_pair[...], (3, 4)))
-    down_kernel(places, parts, down, out, held, sem, 0)
-
-
-def late_kernel(places, third, fourth, swapped, down, filled, out, held, sem):
+def early_kernel(places, own, near, far, swapped_pair, third, down, out, held, sem):
+    rows = [term[...] for term in (own, near, far, swapped_pair, third)]
+    rows = jnp.concatenate(rows, axis=0)
+    down_kernel(places, ((rows, (0, 1, 2, 3, 4, 5)),), down, out, held, sem, 0)
+
+
+def late_kernel(places, fourth, swapped, down, filled, out, held, sem):
     del filled
     depth = fourth.shape[0]
     rows = jnp.concatenate(
-        [third[...], swapped[0 : 2 * depth], fourth[...], swapped[2 * depth : 3 * depth]], axis=0
+        [swapped[0 : 2 * depth], fourth[...], swapped[2 * depth : 3 * depth]], axis=0
     )
-    down_kernel(places, ((rows, (5, 6, 7)),), down, out, held, sem, 5)
+    down_kernel(places, ((rows, (6, 7)),), down, out, held, sem, 6)
 
 
 def mix_kernel(weigh, values, mixed):
@@ -324,23 +326,29 @@
         name="after_weights",
     )(got, weights)
     taken = lax.ppermute(got, "dp", swap)
+    weight = pl.pallas_call(
+        load_kernel,
+        out_shape=jax.ShapeDtypeStruct((strips, 2 * features, 2 * STRIP), bf16),
+        in_specs=[HBM],
+        out_specs=VMEM,
+        scratch_shapes=[pltpu.SemaphoreType.DMA((4 * strips,))],
+        compiler_params=pltpu.CompilerParams(vmem_limit_bytes=48 * 1024 * 1024),
+        cost_estimate=cost(0, 7400000),
+        name="load_weights",
+    )(weights)
 
     def project(chips, name):
         sizes = [2 * held_rows(chip, part) for chip in chips]
         return pl.pallas_call(
             functools.partial(project_kernel, chips=chips, part=part),
             out_shape=[jax.ShapeDtypeStruct((size, 2 * units), bf16) for size in sizes],
-            in_specs=[SMEM, VMEM, VMEM, HBM],
+            in_specs=[SMEM] + [VMEM] * 3,
             out_specs=[VMEM] * len(sizes),
-            scratch_shapes=[
-                pltpu.VMEM((sum(sizes), 2 * features), bf16),
-                pltpu.VMEM((strips, 2 * features, 2 * STRIP), bf16),
-                pltpu.SemaphoreType.DMA((4 * strips,)),
-            ],
-            compiler_params=pltpu.CompilerParams(vmem_limit_bytes=48 * 1024 * 1024),
+            scratch_shapes=[pltpu.VMEM((sum(sizes), 2 * features), bf16)],
+            compiler_params=LIMIT,
             cost_estimate=cost(2 * sum(sizes) * 2 * features * 2 * units, 6000000),
             name=name,
-        )(places, got, taken, weights)
+        )(places, got, taken, weight)
 
     def flow(rows, hops):
         steps = [
@@ -361,8 +369,9 @@
             name=name,
         )(core, first, second, half)
 
-    third, fourth = project(FAR, "project_in_far")
-    second, first, here = project(NEAR, "project_in_near")
+    (fourth,) = project((4,), "project_in_opposite")
+    (third,) = project((3,), "project_in_third")
+    second, first, here = project((2, 1, 0), "project_in_near")
     second = add(second, flow(third, 1), flow(fourth, 2), "add_passing")
     reached = add(flow(first, 1), flow(second, 2), here, "add_reached")
     terms = (reached, lax.ppermute(reached, "dp", swap))
@@ -403,27 +412,22 @@
             pltpu.SemaphoreType.DMA((held,)),
         ]
 
-    back = pl.pallas_call(
-        early_kernel,
-        out_shape=back_shape,
-        in_specs=[SMEM] + [VMEM] * 5,
-        out_specs=HBM,
-        scratch_shapes=scratch(5),
-        compiler_params=LIMIT,
-        cost_estimate=cost(20 * part * units * features, 4000000),
-        name="project_out_early",
-    )(places, hidden, near, far, swapped_pair, down)
-    back = pl.pallas_call(
-        late_kernel,
-        out_shape=back_shape,
-        in_specs=[SMEM] + [VMEM] * 4 + [HBM],
-        out_specs=HBM,
-        scratch_shapes=scratch(3),
-        input_output_aliases={5: 0},
-        compiler_params=LIMIT,
-        cost_estimate=cost(12 * part * units * features, 4000000),
-        name="project_out_late",
-    )(places, third, fourth, swapped_last, down, back)
+    def project_back(kernel, held, rows, filled, name):
+        return pl.pallas_call(
+            kernel,
+            out_shape=back_shape,
+            in_specs=[SMEM] + [VMEM] * (len(rows) + 1) + [HBM] * len(filled),
+            out_specs=HBM,
+            scratch_shapes=scratch(held),
+            input_output_aliases={len(rows) + 2: 0} if filled else {},
+            compiler_params=LIMIT,
+            cost_estimate=cost(4 * held * part * units * features, 3000000),
+            name=name,
+        )(places, *rows, down, *filled)
+
+    early = [hidden, near, far, swapped_pair, third]
+    back = project_back(early_kernel, 6, early, [], "project_out_early")
+    back = project_back(late_kernel, 2, [fourth, swapped_last], [back], "project_out_late")
     back = back.reshape(groups, HALF, 2 * features)
     values = lax.all_to_all(back, "ep", split_axis=0, concat_axis=0, tiled=True)
     mixed = pl.pallas_call(

time: 196 us -> 194 us (0.990)
  waiting for transfers between devices: 103 us -> 101 us
    pallas_call x2 -> x3, Pallas kernels: 8.67 us -> 5.68 us  [project(): pl.pallas_call(functools.partial(project_kernel, chips=chips, part=part),...]
    pallas_call x2 -> x3, Pallas kernels: 5.23 us -> 7.59 us  [the longest x2 5.28 us: project_back(): pl.pallas_call(kernel, out_shape=back_shape, in_specs=[SMEM] + [VMEM] * (...]
    ppermute x1, waiting for transfers between devices: 2.52 us -> 0.2 us  [on_device(): taken = lax.ppermute(got, 'dp', swap)]
  transfers between devices with their start and end apart: 16 -> 16, of which waited for: 11 -> 11; matrix products, arithmetic and copies ran while one was open for 1% -> 1% of each run, Pallas kernels for 6% -> 7%
where the time goes in v6:
time: 194 us; the launch traced here: 193 us
  waiting for transfers between devices  101 us (52%)
  starting transfers between devices  67.9 us (35%)
  Pallas kernels  21.3 us (11%)
    ppermute x8, starting transfers between devices, flow(): return lax.ppermute(rows, 'dp', steps)  37.4 us
    ppermute x8, waiting for transfers between devices, flow(): return lax.ppermute(rows, 'dp', steps)  37.1 us
    all_to_all x1, waiting for transfers between devices, on_device(): values = lax.all_to_all(back, 'ep', split_axis=0, concat_axis=0, tiled=True)  35 us
    all_to_all x1, waiting for transfers between devices, on_device(): lax.all_to_all(send.reshape(groups, HALF, 2 * features), 'ep', split_axis...  24.3 us
    all_to_all x1, starting transfers between devices, on_device(): lax.all_to_all(send.reshape(groups, HALF, 2 * features), 'ep', split_axis...  9.75 us
    pallas_call x3, Pallas kernels, project(): pl.pallas_call(functools.partial(project_kernel, chips=chips, part=part),...  5.68 us
    pallas_call x2, Pallas kernels, project_back(): pl.pallas_call(kernel, out_shape=back_shape, in_specs=[SMEM] + [VMEM] * (...  5.28 us
    all_to_all x1, starting transfers between devices, on_device(): values = lax.all_to_all(back, 'ep', split_axis=0, concat_axis=0, tiled=True)  5.01 us
  transfers between devices with their start and end apart: 16, of which 11 were waited for; matrix products, arithmetic and copies ran while one was open for 1% of the time, Pallas kernels for 7%

profile of v6, /device:TPU:9, one launch (start us, length us, event | category | flops | bytes accessed | tf_op | source)
XLA Modules:
  0.0 193.2 jit_solution(9488315553397090002)
XLA Ops:
  0.0 2.4 %pick_rows.1 = bf16[768,896]{1,0:T(8,128)(2,1)} custom-call(s32[8,128]{1,0:T(8,128)} %bitcast.40, s32[1,32]{1,0:T(1,128)} %bitcast.43, s32[1,32]{1,0:T(1,128)} %bitcast.45, bf16[448,128]{1,0:T(8,128)(2,1)} %bitcast.48), custom_call_target="tpu_custom_call" | custom-call | flops 176160768 | bytes 2000000 | tf_op jit(solution)/shard_map/pick_rows/pallas_call | solution.py:271
  2.5 0.0 copy-start.1
  2.5 0.0 copy-start.2
  2.5 9.8 %all-to-all-start = ((bf16[32,24,896]{2,1,0:T(8,128)(2,1)}), bf16[32,24,896]{2,1,0:T(8,128)(2,1)S(1)}, u32[]{:S(2)}, u32[]{:S(2)}) async-start(bf16[32,24,896]{2,1,0:T(8,128)(2,1)} %bitcast.47), calls=%async_computation | async-start | bytes 2752512 | tf_op jit(solution)/shard_map/all_to_all | solution.py:287
  12.2 0.0 copy-done.1
  12.2 3.1 %collective-permute-start = (bf16[448,1024]{1,0:T(8,128)(2,1)S(1)}, bf16[448,1024]{1,0:T(8,128)(2,1)S(1)}, u32[]{:S(2)}, u32[]{:S(2)}) collective-permute-start(bf16[448,1024]{1,0:T(8,128)(2,1)S(1)} %bitcast.36), channel_id=1, source_target_pairs={{0,1},{1,0},{2,3},{3,2},{4,5},{5,4},{6,7},{7,6},{8,9},{9,8},{10,11... | collective-permute-start | bytes 2752520 | tf_op jit(solution)/shard_map/ppermute | solution.py:268
  15.4 0.0 copy-done.2
  15.4 1.9 collective-permute-start.1
  17.3 0.1 collective-permute-done.gate_other
  17.5 2.3 %collective-permute-done.1.up_other = bf16[448,1024]{1,0:T(8,128)(2,1)S(1)} collective-permute-done((bf16[448,1024]{1,0:T(8,128)(2,1)S(1)}, bf16[448,1024]{1,0:T(8,128)(2,1)S(1)}, u32[]{:S(2)}, u32[]{:S(2)}) %collective-permute-start.1) | collective-permute-done | bytes 917536 | tf_op jit(solution)/shard_map/ppermute | solution.py:269
  19.8 2.7 %gather_weights.1.after.weights = bf16[20,448,1024]{2,1,0:T(8,128)(2,1)} custom-call(bf16[448,1024]{1,0:T(8,128)(2,1)S(1)} %bitcast.37, bf16[448,1024]{1,0:T(8,128)(2,1)S(1)} %collective-permute-done.gate_other, bf16[448,1024]{1,0:T(8,128)(2,1)S(1)} %bitcast.39, bf16[448,1024]{1,0:T(8,128)(2,1)S(1)} %collective-permute-done.1.up_other), custom_call_target="tpu_custom_call" | custom-call | bytes 7400000 | tf_op jit(solution)/shard_map/gather_weights/pallas_call | solution.py:292
  22.5 24.3 %all-to-all-done = bf16[32,24,896]{2,1,0:T(8,128)(2,1)S(1)} async-done(((bf16[32,24,896]{2,1,0:T(8,128)(2,1)}), bf16[32,24,896]{2,1,0:T(8,128)(2,1)S(1)}, u32[]{:S(2)}, u32[]{:S(2)}) %all-to-all-start) | async-done | bytes 1376288 | tf_op jit(solution)/shard_map/all_to_all | solution.py:287
  46.8 3.9 %collective-permute-start.2 = (bf16[768,896]{1,0:T(8,128)(2,1)S(1)}, bf16[768,896]{1,0:T(8,128)(2,1)S(1)}, u32[]{:S(2)}, u32[]{:S(2)}) collective-permute-start(bf16[768,896]{1,0:T(8,128)(2,1)S(1)} %after_weights.1.rows), channel_id=1, source_target_pairs={{0,1},{1,0},{2,3},{3,2},{4,5},{5,4},{6,7},{7,6},{8,9},{9,8},{10,11... | collective-permute-start | bytes 4128776 | tf_op jit(solution)/shard_map/ppermute | solution.py:328
  50.8 0.1 stack.75.places
  50.9 2.3 %load_weights.1.weight = bf16[4,896,512]{2,1,0:T(8,128)(2,1)S(1)} custom-call(bf16[20,448,1024]{2,1,0:T(8,128)(2,1)} %gather_weights.1.after.weights), custom_call_target="tpu_custom_call" | custom-call | bytes 7400000 | tf_op jit(solution)/shard_map/load_weights/pallas_call | solution.py:329
  53.2 0.2 collective-permute-done.2.taken
  53.4 1.6 project_in_third.1
  55.0 10.7 %collective-permute-start.4 = (bf16[192,2048]{1,0:T(8,128)(2,1)S(1)}, bf16[192,2048]{1,0:T(8,128)(2,1)S(1)}, u32[]{:S(2)}, u32[]{:S(2)}) collective-permute-start(bf16[192,2048]{1,0:T(8,128)(2,1)S(1)} %project_in_third.1), channel_id=1, source_target_pairs={{0,2},{1,15},{2,4},{3,1},{4,6},{5,3},{6,8},{7,5},{8,10},{9,7},{10,... | collective-permute-start | bytes 2359304 | tf_op jit(solution)/shard_map/ppermute | solution.py:359
  65.7 1.3 project_in_opposite.1
  67.0 2.2 %collective-permute-start.5 = (bf16[96,2048]{1,0:T(8,128)(2,1)S(1)}, bf16[96,2048]{1,0:T(8,128)(2,1)S(1)}, u32[]{:S(2)}, u32[]{:S(2)}) collective-permute-start(bf16[96,2048]{1,0:T(8,128)(2,1)S(1)} %project_in_opposite.1), channel_id=1, source_target_pairs={{0,4},{1,13},{2,6},{3,15},{4,8},{5,1},{6,10},{7,3},{8,12},{9,5},{1... | collective-permute-start | bytes 1179656 | tf_op jit(solution)/shard_map/ppermute | solution.py:359
  69.2 2.8 %project_in_near.1 = (bf16[192,2048]{1,0:T(8,128)(2,1)S(1)}, bf16[192,2048]{1,0:T(8,128)(2,1)S(1)}, bf16[96,2048]{1,0:T(8,128)(2,1)S(1)}) custom-call(s32[5]{0:T(128)S(1)} %stack.75.places, bf16[768,896]{1,0:T(8,128)(2,1)S(1)} %after_weights.1.rows, bf16[768,896]{1,0:T(8,128)(2,1)S(1)} %collective-permute-done.2.taken, ...), custom_call_target="tpu_custom_call" | custom-call | flops 1761607680 | bytes 6000000 | tf_op jit(solution)/shard_map/project_in_near/pallas_call | solution.py:342
  72.0 2.2 %collective-permute-start.3 = (bf16[192,2048]{1,0:T(8,128)(2,1)S(1)}, bf16[192,2048]{1,0:T(8,128)(2,1)S(1)}, u32[]{:S(2)}, u32[]{:S(2)}) collective-permute-start(bf16[192,2048]{1,0:T(8,128)(2,1)S(1)} %get-tuple-element.8), channel_id=1, source_target_pairs={{0,2},{1,15},{2,4},{3,1},{4,6},{5,3},{6,8},{7,5},{8,10},{9,7},{10,... | collective-permute-start | bytes 2359304 | tf_op jit(solution)/shard_map/ppermute | solution.py:359
  74.2 8.9 %collective-permute-done.5.half = bf16[96,2048]{1,0:T(8,128)(2,1)S(1)} collective-permute-done((bf16[96,2048]{1,0:T(8,128)(2,1)S(1)}, bf16[96,2048]{1,0:T(8,128)(2,1)S(1)}, u32[]{:S(2)}, u32[]{:S(2)}) %collective-permute-start.5) | collective-permute-done | bytes 393248 | tf_op jit(solution)/shard_map/ppermute | solution.py:359
  83.0 0.0 collective-permute-done.4.second
  83.0 0.3 add_passing.1
  83.4 6.0 %collective-permute-start.6 = (bf16[192,2048]{1,0:T(8,128)(2,1)S(1)}, bf16[192,2048]{1,0:T(8,128)(2,1)S(1)}, u32[]{:S(2)}, u32[]{:S(2)}) collective-permute-start(bf16[192,2048]{1,0:T(8,128)(2,1)S(1)} %add_passing.1), channel_id=1, source_target_pairs={{0,4},{1,13},{2,6},{3,15},{4,8},{5,1},{6,10},{7,3},{8,12},{9,5},{1... | collective-permute-start | bytes 2359304 | tf_op jit(solution)/shard_map/ppermute | solution.py:359
  89.4 10.5 %collective-permute-done.3.first = bf16[192,2048]{1,0:T(8,128)(2,1)S(1)} collective-permute-done((bf16[192,2048]{1,0:T(8,128)(2,1)S(1)}, bf16[192,2048]{1,0:T(8,128)(2,1)S(1)}, u32[]{:S(2)}, u32[]{:S(2)}) %collective-permute-start.3) | collective-permute-done | bytes 786464 | tf_op jit(solution)/shard_map/ppermute | solution.py:359
  99.9 8.4 %collective-permute-done.6.second = bf16[192,2048]{1,0:T(8,128)(2,1)S(1)} collective-permute-done((bf16[192,2048]{1,0:T(8,128)(2,1)S(1)}, bf16[192,2048]{1,0:T(8,128)(2,1)S(1)}, u32[]{:S(2)}, u32[]{:S(2)}) %collective-permute-start.6) | collective-permute-done | bytes 786464 | tf_op jit(solution)/shard_map/ppermute | solution.py:359
  108.3 0.3 add_reached.1.refs_0_
  108.6 1.9 collective-permute-start.7
  110.6 2.3 %collective-permute-done.7.refs_1_ = bf16[192,2048]{1,0:T(8,128)(2,1)S(1)} collective-permute-done((bf16[192,2048]{1,0:T(8,128)(2,1)S(1)}, bf16[192,2048]{1,0:T(8,128)(2,1)S(1)}, u32[]{:S(2)}, u32[]{:S(2)}) %collective-permute-start.7) | collective-permute-done | bytes 786464 | tf_op jit(solution)/shard_map/ppermute | solution.py:377
  112.8 0.4 hidden_units.1.own
  113.2 5.9 %collective-permute-start.8 = (bf16[192,1024]{1,0:T(8,128)(2,1)S(1)}, bf16[192,1024]{1,0:T(8,128)(2,1)S(1)}, u32[]{:S(2)}, u32[]{:S(2)}) collective-permute-start(bf16[192,1024]{1,0:T(8,128)(2,1)S(1)} %hidden_units.1.own), channel_id=1, source_target_pairs={{0,4},{1,13},{2,6},{3,15},{4,8},{5,1},{6,10},{7,3},{8,12},{9,5},{1... | collective-permute-start | bytes 1179656 | tf_op jit(solution)/shard_map/ppermute | solution.py:359
  119.1 2.4 %collective-permute-start.12 = (bf16[192,1024]{1,0:T(8,128)(2,1)S(1)}, bf16[192,1024]{1,0:T(8,128)(2,1)S(1)}, u32[]{:S(2)}, u32[]{:S(2)}) collective-permute-start(bf16[192,1024]{1,0:T(8,128)(2,1)S(1)} %hidden_units.1.own), channel_id=1, source_target_pairs={{0,2},{1,15},{2,4},{3,1},{4,6},{5,3},{6,8},{7,5},{8,10},{9,7},{10,... | collective-permute-start | bytes 1179656 | tf_op jit(solution)/shard_map/ppermute | solution.py:359
  121.5 6.5 %collective-permute-done.8.far = bf16[192,1024]{1,0:T(8,128)(2,1)S(1)} collective-permute-done((bf16[192,1024]{1,0:T(8,128)(2,1)S(1)}, bf16[192,1024]{1,0:T(8,128)(2,1)S(1)}, u32[]{:S(2)}, u32[]{:S(2)}) %collective-permute-start.8) | collective-permute-done | bytes 393248 | tf_op jit(solution)/shard_map/ppermute | solution.py:359
  128.0 3.2 %collective-permute-start.10 = (bf16[192,1024]{1,0:T(8,128)(2,1)S(1)}, bf16[192,1024]{1,0:T(8,128)(2,1)S(1)}, u32[]{:S(2)}, u32[]{:S(2)}) collective-permute-start(bf16[192,1024]{1,0:T(8,128)(2,1)S(1)} %collective-permute-done.8.far), channel_id=1, source_target_pairs={{0,2},{1,15},{2,4},{3,1},{4,6},{5,3},{6,8},{7,5},{8,10},{9,7},{10,... | collective-permute-start | bytes 1179656 | tf_op jit(solution)/shard_map/ppermute | solution.py:359
  131.2 0.0 copy-start
  131.3 4.9 %collective-permute-start.9 = (bf16[96,1024]{1,0:T(8,128)(2,1)S(1)}, bf16[96,1024]{1,0:T(8,128)(2,1)S(1)}, u32[]{:S(2)}, u32[]{:S(2)}) collective-permute-start(bf16[96,1024]{1,0:T(8,128)(2,1)S(1)} %slice_select_fusion), channel_id=1, source_target_pairs={{0,4},{1,13},{2,6},{3,15},{4,8},{5,1},{6,10},{7,3},{8,12},{9,5},{1... | collective-permute-start | bytes 589832 | tf_op jit(solution)/shard_map/ppermute | solution.py:359
  136.2 0.0 collective-permute-done.12.near
  136.2 0.9 pad_maximum_fusion
  137.1 1.9 collective-permute-start.13
  139.0 2.8 %collective-permute-done.9.fourth = bf16[96,1024]{1,0:T(8,128)(2,1)S(1)} collective-permute-done((bf16[96,1024]{1,0:T(8,128)(2,1)S(1)}, bf16[96,1024]{1,0:T(8,128)(2,1)S(1)}, u32[]{:S(2)}, u32[]{:S(2)}) %collective-permute-start.9) | collective-permute-done | bytes 196640 | tf_op jit(solution)/shard_map/ppermute | solution.py:359
  141.8 0.0 collective-permute-done.10.third
  141.8 0.9 pad_maximum_fusion.1
  142.7 3.0 %collective-permute-start.11 = (bf16[288,1024]{1,0:T(8,128)(2,1)}, bf16[288,1024]{1,0:T(8,128)(2,1)}, u32[]{:S(2)}, u32[]{:S(2)}) collective-permute-start(bf16[288,1024]{1,0:T(8,128)(2,1)} %pad_maximum_fusion.1), channel_id=1, source_target_pairs={{0,1},{1,0},{2,3},{3,2},{4,5},{5,4},{6,7},{7,6},{8,9},{9,8},{10,11... | collective-permute-start | bytes 1769480 | tf_op jit(solution)/shard_map/ppermute | solution.py:401
  145.7 0.1 stack.65
  145.8 0.1 add_bitcast_fusion
  145.9 0.0 collective-permute-done.13.swapped_pair
  145.9 0.0 copy-done
  146.0 2.8 %project_out_early.1.filled = bf16[768,896]{1,0:T(8,128)(2,1)} custom-call(s32[2,8]{1,0:T(2,128)S(1)} %pad_add_fusion.places, bf16[192,1024]{1,0:T(8,128)(2,1)S(1)} %hidden_units.1.own, bf16[192,1024]{1,0:T(8,128)(2,1)S(1)} %collective-permute-done.12.near, bf16[192,1024]{1,0:T(8,128)(2,1)S(1)} %collective-permute-done.8.far, ...), custom_call_target="tpu_custom_call" | custom-call | flops 1056964608 | bytes 3000000 | tf_op jit(solution)/shard_map/project_out_early/pallas_call | solution.py:416
  148.8 0.0 collective-permute-done.11.swapped
  148.8 2.5 %project_out_late.1 = bf16[768,896]{1,0:T(8,128)(2,1)} custom-call(s32[2,8]{1,0:T(2,128)S(1)} %pad_add_fusion.places, bf16[96,1024]{1,0:T(8,128)(2,1)S(1)} %collective-permute-done.9.fourth, bf16[288,1024]{1,0:T(8,128)(2,1)} %collective-permute-done.11.swapped, bf16[448,1024]{1,0:T(8,128)(2,1)S(1)} %bitcast.34, ...), custom_call_target="tpu_custom_call", output_to_operand_aliasing={{}: (4, {})} | custom-call | flops 352321536 | bytes 3000000 | tf_op jit(solution)/shard_map/project_out_late/pallas_call | solution.py:416
  151.3 0.0 copy-start.3
  151.3 0.0 copy-start.4
  151.3 0.0 copy-start.5
  151.3 0.0 copy-start.6
  151.3 5.0 %all-to-all-start.1 = ((bf16[32,24,896]{2,1,0:T(8,128)(2,1)}), bf16[32,24,896]{2,1,0:T(8,128)(2,1)S(1)}, u32[]{:S(2)}, u32[]{:S(2)}) async-start(bf16[32,24,896]{2,1,0:T(8,128)(2,1)} %bitcast.28), calls=%async_computation.1 | async-start | bytes 2752512 | tf_op jit(solution)/shard_map/all_to_all | solution.py:432
  156.3 0.0 copy-done.3
  156.3 0.0 copy-done.4
  156.3 0.0 copy-done.5
  156.4 0.0 copy-done.6
  156.4 0.4 weigh_table.1.weigh
  156.8 35.0 %all-to-all-done.1 = bf16[32,24,896]{2,1,0:T(8,128)(2,1)S(1)} async-done(((bf16[32,24,896]{2,1,0:T(8,128)(2,1)}), bf16[32,24,896]{2,1,0:T(8,128)(2,1)S(1)}, u32[]{:S(2)}, u32[]{:S(2)}) %all-to-all-start.1) | async-done | bytes 1376288 | tf_op jit(solution)/shard_map/all_to_all | solution.py:432
  191.8 1.4 mix_rows.1
  (5 shorter events, 0.0 us)
Async XLA Ops:
  2.5 9.8 %copy-start.1 = (bf16[1,448,1024]{2,1,0:T(8,128)(2,1)S(1)}, bf16[1,448,1024]{2,1,0:T(8,128)(2,1)}, u32[]{:S(2)}) copy-start(bf16[1,448,1024]{2,1,0:T(8,128)(2,1)} %param.13) | copy-start | bytes 2752516
  2.5 12.9 %copy-start.2 = (bf16[1,448,1024]{2,1,0:T(8,128)(2,1)S(1)}, bf16[1,448,1024]{2,1,0:T(8,128)(2,1)}, u32[]{:S(2)}) copy-start(bf16[1,448,1024]{2,1,0:T(8,128)(2,1)} %param.14) | copy-start | bytes 2752516
  2.5 44.3 %all-to-all-start = ((bf16[32,24,896]{2,1,0:T(8,128)(2,1)}), bf16[32,24,896]{2,1,0:T(8,128)(2,1)S(1)}, u32[]{:S(2)}, u32[]{:S(2)}) async-start(bf16[32,24,896]{2,1,0:T(8,128)(2,1)} %bitcast.47), calls=%async_computation | async-start | bytes 2752512 | tf_op jit(solution)/shard_map/all_to_all | solution.py:287
  12.2 5.2 %collective-permute-start = (bf16[448,1024]{1,0:T(8,128)(2,1)S(1)}, bf16[448,1024]{1,0:T(8,128)(2,1)S(1)}, u32[]{:S(2)}, u32[]{:S(2)}) collective-permute-start(bf16[448,1024]{1,0:T(8,128)(2,1)S(1)} %bitcast.36), channel_id=1, source_target_pairs={{0,1},{1,0},{2,3},{3,2},{4,5},{5,4},{6,7},{7,6},{8,9},{9,8},{10,11... | collective-permute-start | bytes 2752520 | tf_op jit(solution)/shard_map/ppermute | solution.py:268
  15.4 4.4 %collective-permute-start.1 = (bf16[448,1024]{1,0:T(8,128)(2,1)S(1)}, bf16[448,1024]{1,0:T(8,128)(2,1)S(1)}, u32[]{:S(2)}, u32[]{:S(2)}) collective-permute-start(bf16[448,1024]{1,0:T(8,128)(2,1)S(1)} %bitcast.38), channel_id=1, source_target_pairs={{0,1},{1,0},{2,3},{3,2},{4,5},{5,4},{6,7},{7,6},{8,9},{9,8},{10,11... | collective-permute-start | bytes 2752520 | tf_op jit(solution)/shard_map/ppermute | solution.py:269
  46.8 6.6 %collective-permute-start.2 = (bf16[768,896]{1,0:T(8,128)(2,1)S(1)}, bf16[768,896]{1,0:T(8,128)(2,1)S(1)}, u32[]{:S(2)}, u32[]{:S(2)}) collective-permute-start(bf16[768,896]{1,0:T(8,128)(2,1)S(1)} %after_weights.1.rows), channel_id=1, source_target_pairs={{0,1},{1,0},{2,3},{3,2},{4,5},{5,4},{6,7},{7,6},{8,9},{9,8},{10,11... | collective-permute-start | bytes 4128776 | tf_op jit(solution)/shard_map/ppermute | solution.py:328
  55.0 28.1 %collective-permute-start.4 = (bf16[192,2048]{1,0:T(8,128)(2,1)S(1)}, bf16[192,2048]{1,0:T(8,128)(2,1)S(1)}, u32[]{:S(2)}, u32[]{:S(2)}) collective-permute-start(bf16[192,2048]{1,0:T(8,128)(2,1)S(1)} %project_in_third.1), channel_id=1, source_target_pairs={{0,2},{1,15},{2,4},{3,1},{4,6},{5,3},{6,8},{7,5},{8,10},{9,7},{10,... | collective-permute-start | bytes 2359304 | tf_op jit(solution)/shard_map/ppermute | solution.py:359
  67.0 16.0 %collective-permute-start.5 = (bf16[96,2048]{1,0:T(8,128)(2,1)S(1)}, bf16[96,2048]{1,0:T(8,128)(2,1)S(1)}, u32[]{:S(2)}, u32[]{:S(2)}) collective-permute-start(bf16[96,2048]{1,0:T(8,128)(2,1)S(1)} %project_in_opposite.1), channel_id=1, source_target_pairs={{0,4},{1,13},{2,6},{3,15},{4,8},{5,1},{6,10},{7,3},{8,12},{9,5},{1... | collective-permute-start | bytes 1179656 | tf_op jit(solution)/shard_map/ppermute | solution.py:359
  72.0 27.9 %collective-permute-start.3 = (bf16[192,2048]{1,0:T(8,128)(2,1)S(1)}, bf16[192,2048]{1,0:T(8,128)(2,1)S(1)}, u32[]{:S(2)}, u32[]{:S(2)}) collective-permute-start(bf16[192,2048]{1,0:T(8,128)(2,1)S(1)} %get-tuple-element.8), channel_id=1, source_target_pairs={{0,2},{1,15},{2,4},{3,1},{4,6},{5,3},{6,8},{7,5},{8,10},{9,7},{10,... | collective-permute-start | bytes 2359304 | tf_op jit(solution)/shard_map/ppermute | solution.py:359
  83.4 24.9 %collective-permute-start.6 = (bf16[192,2048]{1,0:T(8,128)(2,1)S(1)}, bf16[192,2048]{1,0:T(8,128)(2,1)S(1)}, u32[]{:S(2)}, u32[]{:S(2)}) collective-permute-start(bf16[192,2048]{1,0:T(8,128)(2,1)S(1)} %add_passing.1), channel_id=1, source_target_pairs={{0,4},{1,13},{2,6},{3,15},{4,8},{5,1},{6,10},{7,3},{8,12},{9,5},{1... | collective-permute-start | bytes 2359304 | tf_op jit(solution)/shard_map/ppermute | solution.py:359
  108.6 4.2 %collective-permute-start.7 = (bf16[192,2048]{1,0:T(8,128)(2,1)S(1)}, bf16[192,2048]{1,0:T(8,128)(2,1)S(1)}, u32[]{:S(2)}, u32[]{:S(2)}) collective-permute-start(bf16[192,2048]{1,0:T(8,128)(2,1)S(1)} %add_reached.1.refs_0_), channel_id=1, source_target_pairs={{0,1},{1,0},{2,3},{3,2},{4,5},{5,4},{6,7},{7,6},{8,9},{9,8},{10,11... | collective-permute-start | bytes 2359304 | tf_op jit(solution)/shard_map/ppermute | solution.py:377
  113.2 14.8 %collective-permute-start.8 = (bf16[192,1024]{1,0:T(8,128)(2,1)S(1)}, bf16[192,1024]{1,0:T(8,128)(2,1)S(1)}, u32[]{:S(2)}, u32[]{:S(2)}) collective-permute-start(bf16[192,1024]{1,0:T(8,128)(2,1)S(1)} %hidden_units.1.own), channel_id=1, source_target_pairs={{0,4},{1,13},{2,6},{3,15},{4,8},{5,1},{6,10},{7,3},{8,12},{9,5},{1... | collective-permute-start | bytes 1179656 | tf_op jit(solution)/shard_map/ppermute | solution.py:359
  119.1 17.0 %collective-permute-start.12 = (bf16[192,1024]{1,0:T(8,128)(2,1)S(1)}, bf16[192,1024]{1,0:T(8,128)(2,1)S(1)}, u32[]{:S(2)}, u32[]{:S(2)}) collective-permute-start(bf16[192,1024]{1,0:T(8,128)(2,1)S(1)} %hidden_units.1.own), channel_id=1, source_target_pairs={{0,2},{1,15},{2,4},{3,1},{4,6},{5,3},{6,8},{7,5},{8,10},{9,7},{10,... | collective-permute-start | bytes 1179656 | tf_op jit(solution)/shard_map/ppermute | solution.py:359
  128.0 13.8 %collective-permute-start.10 = (bf16[192,1024]{1,0:T(8,128)(2,1)S(1)}, bf16[192,1024]{1,0:T(8,128)(2,1)S(1)}, u32[]{:S(2)}, u32[]{:S(2)}) collective-permute-start(bf16[192,1024]{1,0:T(8,128)(2,1)S(1)} %collective-permute-done.8.far), channel_id=1, source_target_pairs={{0,2},{1,15},{2,4},{3,1},{4,6},{5,3},{6,8},{7,5},{8,10},{9,7},{10,... | collective-permute-start | bytes 1179656 | tf_op jit(solution)/shard_map/ppermute | solution.py:359
  131.2 14.7 %copy-start = (bf16[1,1024,448]{1,2,0:T(8,128)(2,1)S(1)}, bf16[1,1024,448]{1,2,0:T(8,128)(2,1)}, u32[]{:S(2)}) copy-start(bf16[1,1024,448]{1,2,0:T(8,128)(2,1)} %param.15) | copy-start | bytes 2752516
  131.3 10.5 %collective-permute-start.9 = (bf16[96,1024]{1,0:T(8,128)(2,1)S(1)}, bf16[96,1024]{1,0:T(8,128)(2,1)S(1)}, u32[]{:S(2)}, u32[]{:S(2)}) collective-permute-start(bf16[96,1024]{1,0:T(8,128)(2,1)S(1)} %slice_select_fusion), channel_id=1, source_target_pairs={{0,4},{1,13},{2,6},{3,15},{4,8},{5,1},{6,10},{7,3},{8,12},{9,5},{1... | collective-permute-start | bytes 589832 | tf_op jit(solution)/shard_map/ppermute | solution.py:359
  137.1 8.8 %collective-permute-start.13 = (bf16[384,1024]{1,0:T(8,128)(2,1)}, bf16[384,1024]{1,0:T(8,128)(2,1)S(1)}, u32[]{:S(2)}, u32[]{:S(2)}) collective-permute-start(bf16[384,1024]{1,0:T(8,128)(2,1)} %pad_maximum_fusion), channel_id=1, source_target_pairs={{0,1},{1,0},{2,3},{3,2},{4,5},{5,4},{6,7},{7,6},{8,9},{9,8},{10,11... | collective-permute-start | bytes 2359304 | tf_op jit(solution)/shard_map/ppermute | solution.py:400
  142.7 6.1 %collective-permute-start.11 = (bf16[288,1024]{1,0:T(8,128)(2,1)}, bf16[288,1024]{1,0:T(8,128)(2,1)}, u32[]{:S(2)}, u32[]{:S(2)}) collective-permute-start(bf16[288,1024]{1,0:T(8,128)(2,1)} %pad_maximum_fusion.1), channel_id=1, source_target_pairs={{0,1},{1,0},{2,3},{3,2},{4,5},{5,4},{6,7},{7,6},{8,9},{9,8},{10,11... | collective-permute-start | bytes 1769480 | tf_op jit(solution)/shard_map/ppermute | solution.py:401
  151.3 5.1 %copy-start.3 = (s32[128,8]{0,1:T(8,128)S(1)}, s32[128,8]{0,1:T(8,128)}, u32[]{:S(2)}) copy-start(s32[128,8]{0,1:T(8,128)} %param.9) | copy-start | bytes 12292
  151.3 5.1 %copy-start.4 = (s32[128,8]{0,1:T(8,128)S(1)}, s32[128,8]{0,1:T(8,128)}, u32[]{:S(2)}) copy-start(s32[128,8]{0,1:T(8,128)} %param.10) | copy-start | bytes 12292
  151.3 5.1 %copy-start.5 = (s32[32]{0:T(128)S(1)}, s32[32]{0:T(128)}, u32[]{:S(2)}) copy-start(s32[32]{0:T(128)} %param.11) | copy-start | bytes 388
  151.3 5.1 %copy-start.6 = (s32[32]{0:T(128)S(1)}, s32[32]{0:T(128)}, u32[]{:S(2)}) copy-start(s32[32]{0:T(128)} %param.12) | copy-start | bytes 388
  151.3 40.5 %all-to-all-start.1 = ((bf16[32,24,896]{2,1,0:T(8,128)(2,1)}), bf16[32,24,896]{2,1,0:T(8,128)(2,1)S(1)}, u32[]{:S(2)}, u32[]{:S(2)}) async-start(bf16[32,24,896]{2,1,0:T(8,128)(2,1)} %bitcast.28), calls=%async_computation.1 | async-start | bytes 2752512 | tf_op jit(solution)/shard_map/all_to_all | solution.py:432

commit v7 on v6

--- a/solution.py
+++ b/solution.py
@@ -62,17 +62,16 @@
     slot = lax.broadcasted_iota(jnp.int32, (experts, HALF, count), 1).astype(jnp.float32)
     copies[3].wait()
     width = features.shape[0]
-    piece = experts * HALF // PIECES
-    picks = []
-    for half in range(2):
-        chosen = jnp.where(rank[:, None, :] == slot + half * HALF, 1.0, 0.0)
-        picks.append(chosen.reshape(experts * HALF, count).astype(jnp.bfloat16))
+    group = experts // PIECES
+    piece = group * HALF
     stores = []
     for k in range(PIECES):
         at = pl.ds(k * piece, piece)
+        ranked = rank[k * group : (k + 1) * group][:, None, :]
         for half in range(2):
+            chosen = jnp.where(ranked == slot[:group] + half * HALF, 1.0, 0.0)
             picked = lax.dot_general(
-                picks[half][k * piece : (k + 1) * piece],
+                chosen.reshape(piece, count).astype(jnp.bfloat16),
                 features[...],
                 NT,
                 preferred_element_type=jnp.float32,
@@ -232,11 +231,16 @@
 
 def mix_kernel(weigh, values, mixed):
     features, count = mixed.shape
+    width = values.shape[1]
+    tiles = -(-features // 128) * 128
     total = jnp.zeros((features, count), jnp.float32)
-    for half in range(2):
-        part = jnp.dot(weigh[half], values[...], preferred_element_type=jnp.float32)
+    for half, low in enumerate((0, width - tiles)):
+        part = jnp.dot(
+            weigh[half], values[:, low : low + tiles], preferred_element_type=jnp.float32
+        )
         part = (part[:count] + part[count:]).T
-        total = total + part[half * features : (half + 1) * features]
+        at = half * features - low
+        total = total + part[at : at + features]
     mixed[...] = total.astype(jnp.bfloat16)
 
 

time: 194 us -> 194 us (level)
  no operation moved by 1% of the time
where the time goes in v7:
time: 194 us; the launch traced here: 193 us
  waiting for transfers between devices  101 us (52%)
  starting transfers between devices  67.9 us (35%)
  Pallas kernels  21.2 us (11%)
    ppermute x8, starting transfers between devices, flow(): return lax.ppermute(rows, 'dp', steps)  37.4 us
    ppermute x8, waiting for transfers between devices, flow(): return lax.ppermute(rows, 'dp', steps)  37.1 us
    all_to_all x1, waiting for transfers between devices, on_device(): values = lax.all_to_all(back, 'ep', split_axis=0, concat_axis=0, tiled=True)  35 us
    all_to_all x1, waiting for transfers between devices, on_device(): lax.all_to_all(send.reshape(groups, HALF, 2 * features), 'ep', split_axis...  24.3 us
    all_to_all x1, starting transfers between devices, on_device(): lax.all_to_all(send.reshape(groups, HALF, 2 * features), 'ep', split_axis...  9.75 us
    pallas_call x3, Pallas kernels, project(): pl.pallas_call(functools.partial(project_kernel, chips=chips, part=part),...  5.68 us
    pallas_call x2, Pallas kernels, project_back(): pl.pallas_call(kernel, out_shape=back_shape, in_specs=[SMEM] + [VMEM] * (...  5.28 us
    all_to_all x1, starting transfers between devices, on_device(): values = lax.all_to_all(back, 'ep', split_axis=0, concat_axis=0, tiled=True)  5.01 us
  transfers between devices with their start and end apart: 16, of which 11 were waited for; matrix products, arithmetic and copies ran while one was open for 1% of the time, Pallas kernels for 7%

profile of v7, /device:TPU:9, one launch (start us, length us, event | category | flops | bytes accessed | tf_op | source)
XLA Modules:
  0.0 193.1 jit_solution(12672284821252200613)
XLA Ops:
  0.0 2.4 %pick_rows.1 = bf16[768,896]{1,0:T(8,128)(2,1)} custom-call(s32[8,128]{1,0:T(8,128)} %bitcast.40, s32[1,32]{1,0:T(1,128)} %bitcast.43, s32[1,32]{1,0:T(1,128)} %bitcast.45, bf16[448,128]{1,0:T(8,128)(2,1)} %bitcast.48), custom_call_target="tpu_custom_call" | custom-call | flops 176160768 | bytes 2000000 | tf_op jit(solution)/shard_map/pick_rows/pallas_call | solution.py:275
  2.5 0.0 copy-start.1
  2.5 0.0 copy-start.2
  2.5 9.8 %all-to-all-start = ((bf16[32,24,896]{2,1,0:T(8,128)(2,1)}), bf16[32,24,896]{2,1,0:T(8,128)(2,1)S(1)}, u32[]{:S(2)}, u32[]{:S(2)}) async-start(bf16[32,24,896]{2,1,0:T(8,128)(2,1)} %bitcast.47), calls=%async_computation | async-start | bytes 2752512 | tf_op jit(solution)/shard_map/all_to_all | solution.py:291
  12.2 0.0 copy-done.1
  12.2 3.1 %collective-permute-start = (bf16[448,1024]{1,0:T(8,128)(2,1)S(1)}, bf16[448,1024]{1,0:T(8,128)(2,1)S(1)}, u32[]{:S(2)}, u32[]{:S(2)}) collective-permute-start(bf16[448,1024]{1,0:T(8,128)(2,1)S(1)} %bitcast.36), channel_id=1, source_target_pairs={{0,1},{1,0},{2,3},{3,2},{4,5},{5,4},{6,7},{7,6},{8,9},{9,8},{10,11... | collective-permute-start | bytes 2752520 | tf_op jit(solution)/shard_map/ppermute | solution.py:272
  15.4 0.0 copy-done.2
  15.4 1.9 collective-permute-start.1
  17.3 0.1 collective-permute-done.gate_other
  17.5 2.3 %collective-permute-done.1.up_other = bf16[448,1024]{1,0:T(8,128)(2,1)S(1)} collective-permute-done((bf16[448,1024]{1,0:T(8,128)(2,1)S(1)}, bf16[448,1024]{1,0:T(8,128)(2,1)S(1)}, u32[]{:S(2)}, u32[]{:S(2)}) %collective-permute-start.1) | collective-permute-done | bytes 917536 | tf_op jit(solution)/shard_map/ppermute | solution.py:273
  19.8 2.7 %gather_weights.1.after.weights = bf16[20,448,1024]{2,1,0:T(8,128)(2,1)} custom-call(bf16[448,1024]{1,0:T(8,128)(2,1)S(1)} %bitcast.37, bf16[448,1024]{1,0:T(8,128)(2,1)S(1)} %collective-permute-done.gate_other, bf16[448,1024]{1,0:T(8,128)(2,1)S(1)} %bitcast.39, bf16[448,1024]{1,0:T(8,128)(2,1)S(1)} %collective-permute-done.1.up_other), custom_call_target="tpu_custom_call" | custom-call | bytes 7400000 | tf_op jit(solution)/shard_map/gather_weights/pallas_call | solution.py:296
  22.5 24.3 %all-to-all-done = bf16[32,24,896]{2,1,0:T(8,128)(2,1)S(1)} async-done(((bf16[32,24,896]{2,1,0:T(8,128)(2,1)}), bf16[32,24,896]{2,1,0:T(8,128)(2,1)S(1)}, u32[]{:S(2)}, u32[]{:S(2)}) %all-to-all-start) | async-done | bytes 1376288 | tf_op jit(solution)/shard_map/all_to_all | solution.py:291
  46.8 3.9 %collective-permute-start.2 = (bf16[768,896]{1,0:T(8,128)(2,1)S(1)}, bf16[768,896]{1,0:T(8,128)(2,1)S(1)}, u32[]{:S(2)}, u32[]{:S(2)}) collective-permute-start(bf16[768,896]{1,0:T(8,128)(2,1)S(1)} %after_weights.1.rows), channel_id=1, source_target_pairs={{0,1},{1,0},{2,3},{3,2},{4,5},{5,4},{6,7},{7,6},{8,9},{9,8},{10,11... | collective-permute-start | bytes 4128776 | tf_op jit(solution)/shard_map/ppermute | solution.py:332
  50.8 0.1 stack.75.places
  50.9 2.3 %load_weights.1.weight = bf16[4,896,512]{2,1,0:T(8,128)(2,1)S(1)} custom-call(bf16[20,448,1024]{2,1,0:T(8,128)(2,1)} %gather_weights.1.after.weights), custom_call_target="tpu_custom_call" | custom-call | bytes 7400000 | tf_op jit(solution)/shard_map/load_weights/pallas_call | solution.py:333
  53.2 0.2 collective-permute-done.2.taken
  53.4 1.6 project_in_third.1
  55.0 10.7 %collective-permute-start.4 = (bf16[192,2048]{1,0:T(8,128)(2,1)S(1)}, bf16[192,2048]{1,0:T(8,128)(2,1)S(1)}, u32[]{:S(2)}, u32[]{:S(2)}) collective-permute-start(bf16[192,2048]{1,0:T(8,128)(2,1)S(1)} %project_in_third.1), channel_id=1, source_target_pairs={{0,2},{1,15},{2,4},{3,1},{4,6},{5,3},{6,8},{7,5},{8,10},{9,7},{10,... | collective-permute-start | bytes 2359304 | tf_op jit(solution)/shard_map/ppermute | solution.py:363
  65.7 1.3 project_in_opposite.1
  67.0 2.2 %collective-permute-start.5 = (bf16[96,2048]{1,0:T(8,128)(2,1)S(1)}, bf16[96,2048]{1,0:T(8,128)(2,1)S(1)}, u32[]{:S(2)}, u32[]{:S(2)}) collective-permute-start(bf16[96,2048]{1,0:T(8,128)(2,1)S(1)} %project_in_opposite.1), channel_id=1, source_target_pairs={{0,4},{1,13},{2,6},{3,15},{4,8},{5,1},{6,10},{7,3},{8,12},{9,5},{1... | collective-permute-start | bytes 1179656 | tf_op jit(solution)/shard_map/ppermute | solution.py:363
  69.2 2.8 %project_in_near.1 = (bf16[192,2048]{1,0:T(8,128)(2,1)S(1)}, bf16[192,2048]{1,0:T(8,128)(2,1)S(1)}, bf16[96,2048]{1,0:T(8,128)(2,1)S(1)}) custom-call(s32[5]{0:T(128)S(1)} %stack.75.places, bf16[768,896]{1,0:T(8,128)(2,1)S(1)} %after_weights.1.rows, bf16[768,896]{1,0:T(8,128)(2,1)S(1)} %collective-permute-done.2.taken, ...), custom_call_target="tpu_custom_call" | custom-call | flops 1761607680 | bytes 6000000 | tf_op jit(solution)/shard_map/project_in_near/pallas_call | solution.py:346
  72.0 2.2 %collective-permute-start.3 = (bf16[192,2048]{1,0:T(8,128)(2,1)S(1)}, bf16[192,2048]{1,0:T(8,128)(2,1)S(1)}, u32[]{:S(2)}, u32[]{:S(2)}) collective-permute-start(bf16[192,2048]{1,0:T(8,128)(2,1)S(1)} %get-tuple-element.8), channel_id=1, source_target_pairs={{0,2},{1,15},{2,4},{3,1},{4,6},{5,3},{6,8},{7,5},{8,10},{9,7},{10,... | collective-permute-start | bytes 2359304 | tf_op jit(solution)/shard_map/ppermute | solution.py:363
  74.2 8.9 %collective-permute-done.5.half = bf16[96,2048]{1,0:T(8,128)(2,1)S(1)} collective-permute-done((bf16[96,2048]{1,0:T(8,128)(2,1)S(1)}, bf16[96,2048]{1,0:T(8,128)(2,1)S(1)}, u32[]{:S(2)}, u32[]{:S(2)}) %collective-permute-start.5) | collective-permute-done | bytes 393248 | tf_op jit(solution)/shard_map/ppermute | solution.py:363
  83.0 0.0 collective-permute-done.4.second
  83.0 0.3 add_passing.1
  83.4 6.0 %collective-permute-start.6 = (bf16[192,2048]{1,0:T(8,128)(2,1)S(1)}, bf16[192,2048]{1,0:T(8,128)(2,1)S(1)}, u32[]{:S(2)}, u32[]{:S(2)}) collective-permute-start(bf16[192,2048]{1,0:T(8,128)(2,1)S(1)} %add_passing.1), channel_id=1, source_target_pairs={{0,4},{1,13},{2,6},{3,15},{4,8},{5,1},{6,10},{7,3},{8,12},{9,5},{1... | collective-permute-start | bytes 2359304 | tf_op jit(solution)/shard_map/ppermute | solution.py:363
  89.4 10.5 %collective-permute-done.3.first = bf16[192,2048]{1,0:T(8,128)(2,1)S(1)} collective-permute-done((bf16[192,2048]{1,0:T(8,128)(2,1)S(1)}, bf16[192,2048]{1,0:T(8,128)(2,1)S(1)}, u32[]{:S(2)}, u32[]{:S(2)}) %collective-permute-start.3) | collective-permute-done | bytes 786464 | tf_op jit(solution)/shard_map/ppermute | solution.py:363
  99.9 8.4 %collective-permute-done.6.second = bf16[192,2048]{1,0:T(8,128)(2,1)S(1)} collective-permute-done((bf16[192,2048]{1,0:T(8,128)(2,1)S(1)}, bf16[192,2048]{1,0:T(8,128)(2,1)S(1)}, u32[]{:S(2)}, u32[]{:S(2)}) %collective-permute-start.6) | collective-permute-done | bytes 786464 | tf_op jit(solution)/shard_map/ppermute | solution.py:363
  108.3 0.3 add_reached.1.refs_0_
  108.6 1.9 collective-permute-start.7
  110.6 2.3 %collective-permute-done.7.refs_1_ = bf16[192,2048]{1,0:T(8,128)(2,1)S(1)} collective-permute-done((bf16[192,2048]{1,0:T(8,128)(2,1)S(1)}, bf16[192,2048]{1,0:T(8,128)(2,1)S(1)}, u32[]{:S(2)}, u32[]{:S(2)}) %collective-permute-start.7) | collective-permute-done | bytes 786464 | tf_op jit(solution)/shard_map/ppermute | solution.py:381
  112.8 0.4 hidden_units.1.own
  113.2 5.9 %collective-permute-start.8 = (bf16[192,1024]{1,0:T(8,128)(2,1)S(1)}, bf16[192,1024]{1,0:T(8,128)(2,1)S(1)}, u32[]{:S(2)}, u32[]{:S(2)}) collective-permute-start(bf16[192,1024]{1,0:T(8,128)(2,1)S(1)} %hidden_units.1.own), channel_id=1, source_target_pairs={{0,4},{1,13},{2,6},{3,15},{4,8},{5,1},{6,10},{7,3},{8,12},{9,5},{1... | collective-permute-start | bytes 1179656 | tf_op jit(solution)/shard_map/ppermute | solution.py:363
  119.1 2.4 %collective-permute-start.12 = (bf16[192,1024]{1,0:T(8,128)(2,1)S(1)}, bf16[192,1024]{1,0:T(8,128)(2,1)S(1)}, u32[]{:S(2)}, u32[]{:S(2)}) collective-permute-start(bf16[192,1024]{1,0:T(8,128)(2,1)S(1)} %hidden_units.1.own), channel_id=1, source_target_pairs={{0,2},{1,15},{2,4},{3,1},{4,6},{5,3},{6,8},{7,5},{8,10},{9,7},{10,... | collective-permute-start | bytes 1179656 | tf_op jit(solution)/shard_map/ppermute | solution.py:363
  121.5 6.5 %collective-permute-done.8.far = bf16[192,1024]{1,0:T(8,128)(2,1)S(1)} collective-permute-done((bf16[192,1024]{1,0:T(8,128)(2,1)S(1)}, bf16[192,1024]{1,0:T(8,128)(2,1)S(1)}, u32[]{:S(2)}, u32[]{:S(2)}) %collective-permute-start.8) | collective-permute-done | bytes 393248 | tf_op jit(solution)/shard_map/ppermute | solution.py:363
  128.0 3.2 %collective-permute-start.10 = (bf16[192,1024]{1,0:T(8,128)(2,1)S(1)}, bf16[192,1024]{1,0:T(8,128)(2,1)S(1)}, u32[]{:S(2)}, u32[]{:S(2)}) collective-permute-start(bf16[192,1024]{1,0:T(8,128)(2,1)S(1)} %collective-permute-done.8.far), channel_id=1, source_target_pairs={{0,2},{1,15},{2,4},{3,1},{4,6},{5,3},{6,8},{7,5},{8,10},{9,7},{10,... | collective-permute-start | bytes 1179656 | tf_op jit(solution)/shard_map/ppermute | solution.py:363
  131.2 0.0 copy-start
  131.3 4.9 %collective-permute-start.9 = (bf16[96,1024]{1,0:T(8,128)(2,1)S(1)}, bf16[96,1024]{1,0:T(8,128)(2,1)S(1)}, u32[]{:S(2)}, u32[]{:S(2)}) collective-permute-start(bf16[96,1024]{1,0:T(8,128)(2,1)S(1)} %slice_select_fusion), channel_id=1, source_target_pairs={{0,4},{1,13},{2,6},{3,15},{4,8},{5,1},{6,10},{7,3},{8,12},{9,5},{1... | collective-permute-start | bytes 589832 | tf_op jit(solution)/shard_map/ppermute | solution.py:363
  136.2 0.0 collective-permute-done.12.near
  136.2 0.9 pad_maximum_fusion
  137.1 1.9 collective-permute-start.13
  139.0 2.8 %collective-permute-done.9.fourth = bf16[96,1024]{1,0:T(8,128)(2,1)S(1)} collective-permute-done((bf16[96,1024]{1,0:T(8,128)(2,1)S(1)}, bf16[96,1024]{1,0:T(8,128)(2,1)S(1)}, u32[]{:S(2)}, u32[]{:S(2)}) %collective-permute-start.9) | collective-permute-done | bytes 196640 | tf_op jit(solution)/shard_map/ppermute | solution.py:363
  141.8 0.0 collective-permute-done.10.third
  141.8 0.9 pad_maximum_fusion.1
  142.7 3.0 %collective-permute-start.11 = (bf16[288,1024]{1,0:T(8,128)(2,1)}, bf16[288,1024]{1,0:T(8,128)(2,1)}, u32[]{:S(2)}, u32[]{:S(2)}) collective-permute-start(bf16[288,1024]{1,0:T(8,128)(2,1)} %pad_maximum_fusion.1), channel_id=1, source_target_pairs={{0,1},{1,0},{2,3},{3,2},{4,5},{5,4},{6,7},{7,6},{8,9},{9,8},{10,11... | collective-permute-start | bytes 1769480 | tf_op jit(solution)/shard_map/ppermute | solution.py:405
  145.7 0.1 stack.65
  145.8 0.1 add_bitcast_fusion
  145.9 0.0 collective-permute-done.13.swapped_pair
  145.9 0.0 copy-done
  146.0 2.8 %project_out_early.1.filled = bf16[768,896]{1,0:T(8,128)(2,1)} custom-call(s32[2,8]{1,0:T(2,128)S(1)} %pad_add_fusion.places, bf16[192,1024]{1,0:T(8,128)(2,1)S(1)} %hidden_units.1.own, bf16[192,1024]{1,0:T(8,128)(2,1)S(1)} %collective-permute-done.12.near, bf16[192,1024]{1,0:T(8,128)(2,1)S(1)} %collective-permute-done.8.far, ...), custom_call_target="tpu_custom_call" | custom-call | flops 1056964608 | bytes 3000000 | tf_op jit(solution)/shard_map/project_out_early/pallas_call | solution.py:420
  148.8 0.0 collective-permute-done.11.swapped
  148.8 2.5 %project_out_late.1 = bf16[768,896]{1,0:T(8,128)(2,1)} custom-call(s32[2,8]{1,0:T(2,128)S(1)} %pad_add_fusion.places, bf16[96,1024]{1,0:T(8,128)(2,1)S(1)} %collective-permute-done.9.fourth, bf16[288,1024]{1,0:T(8,128)(2,1)} %collective-permute-done.11.swapped, bf16[448,1024]{1,0:T(8,128)(2,1)S(1)} %bitcast.34, ...), custom_call_target="tpu_custom_call", output_to_operand_aliasing={{}: (4, {})} | custom-call | flops 352321536 | bytes 3000000 | tf_op jit(solution)/shard_map/project_out_late/pallas_call | solution.py:420
  151.3 0.0 copy-start.3
  151.3 0.0 copy-start.4
  151.3 0.0 copy-start.5
  151.3 0.0 copy-start.6
  151.3 5.0 %all-to-all-start.1 = ((bf16[32,24,896]{2,1,0:T(8,128)(2,1)}), bf16[32,24,896]{2,1,0:T(8,128)(2,1)S(1)}, u32[]{:S(2)}, u32[]{:S(2)}) async-start(bf16[32,24,896]{2,1,0:T(8,128)(2,1)} %bitcast.28), calls=%async_computation.1 | async-start | bytes 2752512 | tf_op jit(solution)/shard_map/all_to_all | solution.py:436
  156.3 0.0 copy-done.3
  156.3 0.0 copy-done.4
  156.3 0.0 copy-done.5
  156.4 0.0 copy-done.6
  156.4 0.4 weigh_table.1.weigh
  156.8 35.0 %all-to-all-done.1 = bf16[32,24,896]{2,1,0:T(8,128)(2,1)S(1)} async-done(((bf16[32,24,896]{2,1,0:T(8,128)(2,1)}), bf16[32,24,896]{2,1,0:T(8,128)(2,1)S(1)}, u32[]{:S(2)}, u32[]{:S(2)}) %all-to-all-start.1) | async-done | bytes 1376288 | tf_op jit(solution)/shard_map/all_to_all | solution.py:436
  191.8 1.3 mix_rows.1
  (5 shorter events, 0.0 us)
Async XLA Ops:
  2.5 9.8 %copy-start.1 = (bf16[1,448,1024]{2,1,0:T(8,128)(2,1)S(1)}, bf16[1,448,1024]{2,1,0:T(8,128)(2,1)}, u32[]{:S(2)}) copy-start(bf16[1,448,1024]{2,1,0:T(8,128)(2,1)} %param.13) | copy-start | bytes 2752516
  2.5 12.9 %copy-start.2 = (bf16[1,448,1024]{2,1,0:T(8,128)(2,1)S(1)}, bf16[1,448,1024]{2,1,0:T(8,128)(2,1)}, u32[]{:S(2)}) copy-start(bf16[1,448,1024]{2,1,0:T(8,128)(2,1)} %param.14) | copy-start | bytes 2752516
  2.5 44.3 %all-to-all-start = ((bf16[32,24,896]{2,1,0:T(8,128)(2,1)}), bf16[32,24,896]{2,1,0:T(8,128)(2,1)S(1)}, u32[]{:S(2)}, u32[]{:S(2)}) async-start(bf16[32,24,896]{2,1,0:T(8,128)(2,1)} %bitcast.47), calls=%async_computation | async-start | bytes 2752512 | tf_op jit(solution)/shard_map/all_to_all | solution.py:291
  12.2 5.2 %collective-permute-start = (bf16[448,1024]{1,0:T(8,128)(2,1)S(1)}, bf16[448,1024]{1,0:T(8,128)(2,1)S(1)}, u32[]{:S(2)}, u32[]{:S(2)}) collective-permute-start(bf16[448,1024]{1,0:T(8,128)(2,1)S(1)} %bitcast.36), channel_id=1, source_target_pairs={{0,1},{1,0},{2,3},{3,2},{4,5},{5,4},{6,7},{7,6},{8,9},{9,8},{10,11... | collective-permute-start | bytes 2752520 | tf_op jit(solution)/shard_map/ppermute | solution.py:272
  15.4 4.4 %collective-permute-start.1 = (bf16[448,1024]{1,0:T(8,128)(2,1)S(1)}, bf16[448,1024]{1,0:T(8,128)(2,1)S(1)}, u32[]{:S(2)}, u32[]{:S(2)}) collective-permute-start(bf16[448,1024]{1,0:T(8,128)(2,1)S(1)} %bitcast.38), channel_id=1, source_target_pairs={{0,1},{1,0},{2,3},{3,2},{4,5},{5,4},{6,7},{7,6},{8,9},{9,8},{10,11... | collective-permute-start | bytes 2752520 | tf_op jit(solution)/shard_map/ppermute | solution.py:273
  46.8 6.6 %collective-permute-start.2 = (bf16[768,896]{1,0:T(8,128)(2,1)S(1)}, bf16[768,896]{1,0:T(8,128)(2,1)S(1)}, u32[]{:S(2)}, u32[]{:S(2)}) collective-permute-start(bf16[768,896]{1,0:T(8,128)(2,1)S(1)} %after_weights.1.rows), channel_id=1, source_target_pairs={{0,1},{1,0},{2,3},{3,2},{4,5},{5,4},{6,7},{7,6},{8,9},{9,8},{10,11... | collective-permute-start | bytes 4128776 | tf_op jit(solution)/shard_map/ppermute | solution.py:332
  55.0 28.1 %collective-permute-start.4 = (bf16[192,2048]{1,0:T(8,128)(2,1)S(1)}, bf16[192,2048]{1,0:T(8,128)(2,1)S(1)}, u32[]{:S(2)}, u32[]{:S(2)}) collective-permute-start(bf16[192,2048]{1,0:T(8,128)(2,1)S(1)} %project_in_third.1), channel_id=1, source_target_pairs={{0,2},{1,15},{2,4},{3,1},{4,6},{5,3},{6,8},{7,5},{8,10},{9,7},{10,... | collective-permute-start | bytes 2359304 | tf_op jit(solution)/shard_map/ppermute | solution.py:363
  67.0 16.0 %collective-permute-start.5 = (bf16[96,2048]{1,0:T(8,128)(2,1)S(1)}, bf16[96,2048]{1,0:T(8,128)(2,1)S(1)}, u32[]{:S(2)}, u32[]{:S(2)}) collective-permute-start(bf16[96,2048]{1,0:T(8,128)(2,1)S(1)} %project_in_opposite.1), channel_id=1, source_target_pairs={{0,4},{1,13},{2,6},{3,15},{4,8},{5,1},{6,10},{7,3},{8,12},{9,5},{1... | collective-permute-start | bytes 1179656 | tf_op jit(solution)/shard_map/ppermute | solution.py:363
  72.0 27.9 %collective-permute-start.3 = (bf16[192,2048]{1,0:T(8,128)(2,1)S(1)}, bf16[192,2048]{1,0:T(8,128)(2,1)S(1)}, u32[]{:S(2)}, u32[]{:S(2)}) collective-permute-start(bf16[192,2048]{1,0:T(8,128)(2,1)S(1)} %get-tuple-element.8), channel_id=1, source_target_pairs={{0,2},{1,15},{2,4},{3,1},{4,6},{5,3},{6,8},{7,5},{8,10},{9,7},{10,... | collective-permute-start | bytes 2359304 | tf_op jit(solution)/shard_map/ppermute | solution.py:363
  83.4 24.9 %collective-permute-start.6 = (bf16[192,2048]{1,0:T(8,128)(2,1)S(1)}, bf16[192,2048]{1,0:T(8,128)(2,1)S(1)}, u32[]{:S(2)}, u32[]{:S(2)}) collective-permute-start(bf16[192,2048]{1,0:T(8,128)(2,1)S(1)} %add_passing.1), channel_id=1, source_target_pairs={{0,4},{1,13},{2,6},{3,15},{4,8},{5,1},{6,10},{7,3},{8,12},{9,5},{1... | collective-permute-start | bytes 2359304 | tf_op jit(solution)/shard_map/ppermute | solution.py:363
  108.6 4.2 %collective-permute-start.7 = (bf16[192,2048]{1,0:T(8,128)(2,1)S(1)}, bf16[192,2048]{1,0:T(8,128)(2,1)S(1)}, u32[]{:S(2)}, u32[]{:S(2)}) collective-permute-start(bf16[192,2048]{1,0:T(8,128)(2,1)S(1)} %add_reached.1.refs_0_), channel_id=1, source_target_pairs={{0,1},{1,0},{2,3},{3,2},{4,5},{5,4},{6,7},{7,6},{8,9},{9,8},{10,11... | collective-permute-start | bytes 2359304 | tf_op jit(solution)/shard_map/ppermute | solution.py:381
  113.2 14.8 %collective-permute-start.8 = (bf16[192,1024]{1,0:T(8,128)(2,1)S(1)}, bf16[192,1024]{1,0:T(8,128)(2,1)S(1)}, u32[]{:S(2)}, u32[]{:S(2)}) collective-permute-start(bf16[192,1024]{1,0:T(8,128)(2,1)S(1)} %hidden_units.1.own), channel_id=1, source_target_pairs={{0,4},{1,13},{2,6},{3,15},{4,8},{5,1},{6,10},{7,3},{8,12},{9,5},{1... | collective-permute-start | bytes 1179656 | tf_op jit(solution)/shard_map/ppermute | solution.py:363
  119.1 17.0 %collective-permute-start.12 = (bf16[192,1024]{1,0:T(8,128)(2,1)S(1)}, bf16[192,1024]{1,0:T(8,128)(2,1)S(1)}, u32[]{:S(2)}, u32[]{:S(2)}) collective-permute-start(bf16[192,1024]{1,0:T(8,128)(2,1)S(1)} %hidden_units.1.own), channel_id=1, source_target_pairs={{0,2},{1,15},{2,4},{3,1},{4,6},{5,3},{6,8},{7,5},{8,10},{9,7},{10,... | collective-permute-start | bytes 1179656 | tf_op jit(solution)/shard_map/ppermute | solution.py:363
  128.0 13.8 %collective-permute-start.10 = (bf16[192,1024]{1,0:T(8,128)(2,1)S(1)}, bf16[192,1024]{1,0:T(8,128)(2,1)S(1)}, u32[]{:S(2)}, u32[]{:S(2)}) collective-permute-start(bf16[192,1024]{1,0:T(8,128)(2,1)S(1)} %collective-permute-done.8.far), channel_id=1, source_target_pairs={{0,2},{1,15},{2,4},{3,1},{4,6},{5,3},{6,8},{7,5},{8,10},{9,7},{10,... | collective-permute-start | bytes 1179656 | tf_op jit(solution)/shard_map/ppermute | solution.py:363
  131.2 14.7 %copy-start = (bf16[1,1024,448]{1,2,0:T(8,128)(2,1)S(1)}, bf16[1,1024,448]{1,2,0:T(8,128)(2,1)}, u32[]{:S(2)}) copy-start(bf16[1,1024,448]{1,2,0:T(8,128)(2,1)} %param.15) | copy-start | bytes 2752516
  131.3 10.5 %collective-permute-start.9 = (bf16[96,1024]{1,0:T(8,128)(2,1)S(1)}, bf16[96,1024]{1,0:T(8,128)(2,1)S(1)}, u32[]{:S(2)}, u32[]{:S(2)}) collective-permute-start(bf16[96,1024]{1,0:T(8,128)(2,1)S(1)} %slice_select_fusion), channel_id=1, source_target_pairs={{0,4},{1,13},{2,6},{3,15},{4,8},{5,1},{6,10},{7,3},{8,12},{9,5},{1... | collective-permute-start | bytes 589832 | tf_op jit(solution)/shard_map/ppermute | solution.py:363
  137.1 8.8 %collective-permute-start.13 = (bf16[384,1024]{1,0:T(8,128)(2,1)}, bf16[384,1024]{1,0:T(8,128)(2,1)S(1)}, u32[]{:S(2)}, u32[]{:S(2)}) collective-permute-start(bf16[384,1024]{1,0:T(8,128)(2,1)} %pad_maximum_fusion), channel_id=1, source_target_pairs={{0,1},{1,0},{2,3},{3,2},{4,5},{5,4},{6,7},{7,6},{8,9},{9,8},{10,11... | collective-permute-start | bytes 2359304 | tf_op jit(solution)/shard_map/ppermute | solution.py:404
  142.7 6.1 %collective-permute-start.11 = (bf16[288,1024]{1,0:T(8,128)(2,1)}, bf16[288,1024]{1,0:T(8,128)(2,1)}, u32[]{:S(2)}, u32[]{:S(2)}) collective-permute-start(bf16[288,1024]{1,0:T(8,128)(2,1)} %pad_maximum_fusion.1), channel_id=1, source_target_pairs={{0,1},{1,0},{2,3},{3,2},{4,5},{5,4},{6,7},{7,6},{8,9},{9,8},{10,11... | collective-permute-start | bytes 1769480 | tf_op jit(solution)/shard_map/ppermute | solution.py:405
  151.3 5.1 %copy-start.3 = (s32[128,8]{0,1:T(8,128)S(1)}, s32[128,8]{0,1:T(8,128)}, u32[]{:S(2)}) copy-start(s32[128,8]{0,1:T(8,128)} %param.9) | copy-start | bytes 12292
  151.3 5.1 %copy-start.4 = (s32[128,8]{0,1:T(8,128)S(1)}, s32[128,8]{0,1:T(8,128)}, u32[]{:S(2)}) copy-start(s32[128,8]{0,1:T(8,128)} %param.10) | copy-start | bytes 12292
  151.3 5.1 %copy-start.5 = (s32[32]{0:T(128)S(1)}, s32[32]{0:T(128)}, u32[]{:S(2)}) copy-start(s32[32]{0:T(128)} %param.11) | copy-start | bytes 388
  151.3 5.1 %copy-start.6 = (s32[32]{0:T(128)S(1)}, s32[32]{0:T(128)}, u32[]{:S(2)}) copy-start(s32[32]{0:T(128)} %param.12) | copy-start | bytes 388
  151.3 40.5 %all-to-all-start.1 = ((bf16[32,24,896]{2,1,0:T(8,128)(2,1)}), bf16[32,24,896]{2,1,0:T(8,128)(2,1)S(1)}, u32[]{:S(2)}, u32[]{:S(2)}) async-start(bf16[32,24,896]{2,1,0:T(8,128)(2,1)} %bitcast.28), calls=%async_computation.1 | async-start | bytes 2752512 | tf_op jit(solution)/shard_map/all_to_all | solution.py:436

commit v8 on v7

--- a/solution.py
+++ b/solution.py
@@ -375,7 +375,8 @@
 
     (fourth,) = project((4,), "project_in_opposite")
     (third,) = project((3,), "project_in_third")
-    second, first, here = project((2, 1, 0), "project_in_near")
+    (first,) = project((1,), "project_in_first")
+    second, here = project((2, 0), "project_in_second")
     second = add(second, flow(third, 1), flow(fourth, 2), "add_passing")
     reached = add(flow(first, 1), flow(second, 2), here, "add_reached")
     terms = (reached, lax.ppermute(reached, "dp", swap))

time: 194 us -> 194 us (level)
    pallas_call x3 -> x4, Pallas kernels: 5.68 us -> 6.43 us  [project(): pl.pallas_call(functools.partial(project_kernel, chips=chips, part=part),...]
where the time goes in v8:
time: 194 us; the launch traced here: 193 us
  waiting for transfers between devices  101 us (52%)
  starting transfers between devices  67.9 us (35%)
  Pallas kernels  22 us (11%)
    ppermute x8, starting transfers between devices, flow(): return lax.ppermute(rows, 'dp', steps)  37.4 us
    ppermute x8, waiting for transfers between devices, flow(): return lax.ppermute(rows, 'dp', steps)  36.4 us
    all_to_all x1, waiting for transfers between devices, on_device(): values = lax.all_to_all(back, 'ep', split_axis=0, concat_axis=0, tiled=True)  35 us
    all_to_all x1, waiting for transfers between devices, on_device(): lax.all_to_all(send.reshape(groups, HALF, 2 * features), 'ep', split_axis...  24.3 us
    all_to_all x1, starting transfers between devices, on_device(): lax.all_to_all(send.reshape(groups, HALF, 2 * features), 'ep', split_axis...  9.75 us
    pallas_call x4, Pallas kernels, project(): pl.pallas_call(functools.partial(project_kernel, chips=chips, part=part),...  6.43 us
    pallas_call x2, Pallas kernels, project_back(): pl.pallas_call(kernel, out_shape=back_shape, in_specs=[SMEM] + [VMEM] * (...  5.28 us
    all_to_all x1, starting transfers between devices, on_device(): values = lax.all_to_all(back, 'ep', split_axis=0, concat_axis=0, tiled=True)  5.01 us
  transfers between devices with their start and end apart: 16, of which 11 were waited for; matrix products, arithmetic and copies ran while one was open for 1% of the time, Pallas kernels for 7%

profile of v8, /device:TPU:9, one launch (start us, length us, event | category | flops | bytes accessed | tf_op | source)
XLA Modules:
  0.0 193.1 jit_solution(10654334814411663147)
XLA Ops:
  0.0 2.4 %pick_rows.1 = bf16[768,896]{1,0:T(8,128)(2,1)} custom-call(s32[8,128]{1,0:T(8,128)} %bitcast.40, s32[1,32]{1,0:T(1,128)} %bitcast.43, s32[1,32]{1,0:T(1,128)} %bitcast.45, bf16[448,128]{1,0:T(8,128)(2,1)} %bitcast.48), custom_call_target="tpu_custom_call" | custom-call | flops 176160768 | bytes 2000000 | tf_op jit(solution)/shard_map/pick_rows/pallas_call | solution.py:275
  2.5 0.0 copy-start.1
  2.5 0.0 copy-start.2
  2.5 9.8 %all-to-all-start = ((bf16[32,24,896]{2,1,0:T(8,128)(2,1)}), bf16[32,24,896]{2,1,0:T(8,128)(2,1)S(1)}, u32[]{:S(2)}, u32[]{:S(2)}) async-start(bf16[32,24,896]{2,1,0:T(8,128)(2,1)} %bitcast.47), calls=%async_computation | async-start | bytes 2752512 | tf_op jit(solution)/shard_map/all_to_all | solution.py:291
  12.2 0.0 copy-done.1
  12.2 3.1 %collective-permute-start = (bf16[448,1024]{1,0:T(8,128)(2,1)S(1)}, bf16[448,1024]{1,0:T(8,128)(2,1)S(1)}, u32[]{:S(2)}, u32[]{:S(2)}) collective-permute-start(bf16[448,1024]{1,0:T(8,128)(2,1)S(1)} %bitcast.36), channel_id=1, source_target_pairs={{0,1},{1,0},{2,3},{3,2},{4,5},{5,4},{6,7},{7,6},{8,9},{9,8},{10,11... | collective-permute-start | bytes 2752520 | tf_op jit(solution)/shard_map/ppermute | solution.py:272
  15.4 0.0 copy-done.2
  15.4 1.9 collective-permute-start.1
  17.3 0.1 collective-permute-done.gate_other
  17.5 2.3 %collective-permute-done.1.up_other = bf16[448,1024]{1,0:T(8,128)(2,1)S(1)} collective-permute-done((bf16[448,1024]{1,0:T(8,128)(2,1)S(1)}, bf16[448,1024]{1,0:T(8,128)(2,1)S(1)}, u32[]{:S(2)}, u32[]{:S(2)}) %collective-permute-start.1) | collective-permute-done | bytes 917536 | tf_op jit(solution)/shard_map/ppermute | solution.py:273
  19.8 2.7 %gather_weights.1.after.weights = bf16[20,448,1024]{2,1,0:T(8,128)(2,1)} custom-call(bf16[448,1024]{1,0:T(8,128)(2,1)S(1)} %bitcast.37, bf16[448,1024]{1,0:T(8,128)(2,1)S(1)} %collective-permute-done.gate_other, bf16[448,1024]{1,0:T(8,128)(2,1)S(1)} %bitcast.39, bf16[448,1024]{1,0:T(8,128)(2,1)S(1)} %collective-permute-done.1.up_other), custom_call_target="tpu_custom_call" | custom-call | bytes 7400000 | tf_op jit(solution)/shard_map/gather_weights/pallas_call | solution.py:296
  22.5 24.3 %all-to-all-done = bf16[32,24,896]{2,1,0:T(8,128)(2,1)S(1)} async-done(((bf16[32,24,896]{2,1,0:T(8,128)(2,1)}), bf16[32,24,896]{2,1,0:T(8,128)(2,1)S(1)}, u32[]{:S(2)}, u32[]{:S(2)}) %all-to-all-start) | async-done | bytes 1376288 | tf_op jit(solution)/shard_map/all_to_all | solution.py:291
  46.8 3.9 %collective-permute-start.2 = (bf16[768,896]{1,0:T(8,128)(2,1)S(1)}, bf16[768,896]{1,0:T(8,128)(2,1)S(1)}, u32[]{:S(2)}, u32[]{:S(2)}) collective-permute-start(bf16[768,896]{1,0:T(8,128)(2,1)S(1)} %after_weights.1.rows), channel_id=1, source_target_pairs={{0,1},{1,0},{2,3},{3,2},{4,5},{5,4},{6,7},{7,6},{8,9},{9,8},{10,11... | collective-permute-start | bytes 4128776 | tf_op jit(solution)/shard_map/ppermute | solution.py:332
  50.8 0.1 stack.75.places
  50.9 2.3 %load_weights.1.weight = bf16[4,896,512]{2,1,0:T(8,128)(2,1)S(1)} custom-call(bf16[20,448,1024]{2,1,0:T(8,128)(2,1)} %gather_weights.1.after.weights), custom_call_target="tpu_custom_call" | custom-call | bytes 7400000 | tf_op jit(solution)/shard_map/load_weights/pallas_call | solution.py:333
  53.2 0.2 collective-permute-done.2.taken
  53.4 1.6 project_in_third.1
  55.0 10.7 %collective-permute-start.4 = (bf16[192,2048]{1,0:T(8,128)(2,1)S(1)}, bf16[192,2048]{1,0:T(8,128)(2,1)S(1)}, u32[]{:S(2)}, u32[]{:S(2)}) collective-permute-start(bf16[192,2048]{1,0:T(8,128)(2,1)S(1)} %project_in_third.1), channel_id=1, source_target_pairs={{0,2},{1,15},{2,4},{3,1},{4,6},{5,3},{6,8},{7,5},{8,10},{9,7},{10,... | collective-permute-start | bytes 2359304 | tf_op jit(solution)/shard_map/ppermute | solution.py:363
  65.7 1.3 project_in_opposite.1
  67.0 2.2 %collective-permute-start.5 = (bf16[96,2048]{1,0:T(8,128)(2,1)S(1)}, bf16[96,2048]{1,0:T(8,128)(2,1)S(1)}, u32[]{:S(2)}, u32[]{:S(2)}) collective-permute-start(bf16[96,2048]{1,0:T(8,128)(2,1)S(1)} %project_in_opposite.1), channel_id=1, source_target_pairs={{0,4},{1,13},{2,6},{3,15},{4,8},{5,1},{6,10},{7,3},{8,12},{9,5},{1... | collective-permute-start | bytes 1179656 | tf_op jit(solution)/shard_map/ppermute | solution.py:363
  69.2 1.6 project_in_first.1
  70.8 2.2 %collective-permute-start.3 = (bf16[192,2048]{1,0:T(8,128)(2,1)S(1)}, bf16[192,2048]{1,0:T(8,128)(2,1)S(1)}, u32[]{:S(2)}, u32[]{:S(2)}) collective-permute-start(bf16[192,2048]{1,0:T(8,128)(2,1)S(1)} %project_in_first.1), channel_id=1, source_target_pairs={{0,2},{1,15},{2,4},{3,1},{4,6},{5,3},{6,8},{7,5},{8,10},{9,7},{10,... | collective-permute-start | bytes 2359304 | tf_op jit(solution)/shard_map/ppermute | solution.py:363
  72.9 2.0 %project_in_second.1 = (bf16[192,2048]{1,0:T(8,128)(2,1)S(1)}, bf16[96,2048]{1,0:T(8,128)(2,1)S(1)}) custom-call(s32[5]{0:T(128)S(1)} %stack.75.places, bf16[768,896]{1,0:T(8,128)(2,1)S(1)} %after_weights.1.rows, bf16[768,896]{1,0:T(8,128)(2,1)S(1)} %collective-permute-done.2.taken, bf16[4,896,512]{2,1,0:T(8,128)(2,1)S(1)} %load_weights.1.weight), custom_call_target="tpu_custom_call" | custom-call | flops 1056964608 | bytes 6000000 | tf_op jit(solution)/shard_map/project_in_second/pallas_call | solution.py:346
  74.9 8.1 %collective-permute-done.5.half = bf16[96,2048]{1,0:T(8,128)(2,1)S(1)} collective-permute-done((bf16[96,2048]{1,0:T(8,128)(2,1)S(1)}, bf16[96,2048]{1,0:T(8,128)(2,1)S(1)}, u32[]{:S(2)}, u32[]{:S(2)}) %collective-permute-start.5) | collective-permute-done | bytes 393248 | tf_op jit(solution)/shard_map/ppermute | solution.py:363
  83.0 0.0 collective-permute-done.4.second
  83.0 0.3 add_passing.1
  83.4 6.0 %collective-permute-start.6 = (bf16[192,2048]{1,0:T(8,128)(2,1)S(1)}, bf16[192,2048]{1,0:T(8,128)(2,1)S(1)}, u32[]{:S(2)}, u32[]{:S(2)}) collective-permute-start(bf16[192,2048]{1,0:T(8,128)(2,1)S(1)} %add_passing.1), channel_id=1, source_target_pairs={{0,4},{1,13},{2,6},{3,15},{4,8},{5,1},{6,10},{7,3},{8,12},{9,5},{1... | collective-permute-start | bytes 2359304 | tf_op jit(solution)/shard_map/ppermute | solution.py:363
  89.4 10.5 %collective-permute-done.3.first = bf16[192,2048]{1,0:T(8,128)(2,1)S(1)} collective-permute-done((bf16[192,2048]{1,0:T(8,128)(2,1)S(1)}, bf16[192,2048]{1,0:T(8,128)(2,1)S(1)}, u32[]{:S(2)}, u32[]{:S(2)}) %collective-permute-start.3) | collective-permute-done | bytes 786464 | tf_op jit(solution)/shard_map/ppermute | solution.py:363
  99.9 8.4 %collective-permute-done.6.second = bf16[192,2048]{1,0:T(8,128)(2,1)S(1)} collective-permute-done((bf16[192,2048]{1,0:T(8,128)(2,1)S(1)}, bf16[192,2048]{1,0:T(8,128)(2,1)S(1)}, u32[]{:S(2)}, u32[]{:S(2)}) %collective-permute-start.6) | collective-permute-done | bytes 786464 | tf_op jit(solution)/shard_map/ppermute | solution.py:363
  108.3 0.3 add_reached.1.refs_0_
  108.6 1.9 collective-permute-start.7
  110.6 2.3 %collective-permute-done.7.refs_1_ = bf16[192,2048]{1,0:T(8,128)(2,1)S(1)} collective-permute-done((bf16[192,2048]{1,0:T(8,128)(2,1)S(1)}, bf16[192,2048]{1,0:T(8,128)(2,1)S(1)}, u32[]{:S(2)}, u32[]{:S(2)}) %collective-permute-start.7) | collective-permute-done | bytes 786464 | tf_op jit(solution)/shard_map/ppermute | solution.py:382
  112.8 0.4 hidden_units.1.own
  113.2 5.9 %collective-permute-start.8 = (bf16[192,1024]{1,0:T(8,128)(2,1)S(1)}, bf16[192,1024]{1,0:T(8,128)(2,1)S(1)}, u32[]{:S(2)}, u32[]{:S(2)}) collective-permute-start(bf16[192,1024]{1,0:T(8,128)(2,1)S(1)} %hidden_units.1.own), channel_id=1, source_target_pairs={{0,4},{1,13},{2,6},{3,15},{4,8},{5,1},{6,10},{7,3},{8,12},{9,5},{1... | collective-permute-start | bytes 1179656 | tf_op jit(solution)/shard_map/ppermute | solution.py:363
  119.1 2.4 %collective-permute-start.12 = (bf16[192,1024]{1,0:T(8,128)(2,1)S(1)}, bf16[192,1024]{1,0:T(8,128)(2,1)S(1)}, u32[]{:S(2)}, u32[]{:S(2)}) collective-permute-start(bf16[192,1024]{1,0:T(8,128)(2,1)S(1)} %hidden_units.1.own), channel_id=1, source_target_pairs={{0,2},{1,15},{2,4},{3,1},{4,6},{5,3},{6,8},{7,5},{8,10},{9,7},{10,... | collective-permute-start | bytes 1179656 | tf_op jit(solution)/shard_map/ppermute | solution.py:363
  121.5 6.5 %collective-permute-done.8.far = bf16[192,1024]{1,0:T(8,128)(2,1)S(1)} collective-permute-done((bf16[192,1024]{1,0:T(8,128)(2,1)S(1)}, bf16[192,1024]{1,0:T(8,128)(2,1)S(1)}, u32[]{:S(2)}, u32[]{:S(2)}) %collective-permute-start.8) | collective-permute-done | bytes 393248 | tf_op jit(solution)/shard_map/ppermute | solution.py:363
  128.0 3.2 %collective-permute-start.10 = (bf16[192,1024]{1,0:T(8,128)(2,1)S(1)}, bf16[192,1024]{1,0:T(8,128)(2,1)S(1)}, u32[]{:S(2)}, u32[]{:S(2)}) collective-permute-start(bf16[192,1024]{1,0:T(8,128)(2,1)S(1)} %collective-permute-done.8.far), channel_id=1, source_target_pairs={{0,2},{1,15},{2,4},{3,1},{4,6},{5,3},{6,8},{7,5},{8,10},{9,7},{10,... | collective-permute-start | bytes 1179656 | tf_op jit(solution)/shard_map/ppermute | solution.py:363
  131.2 0.0 copy-start
  131.3 4.9 %collective-permute-start.9 = (bf16[96,1024]{1,0:T(8,128)(2,1)S(1)}, bf16[96,1024]{1,0:T(8,128)(2,1)S(1)}, u32[]{:S(2)}, u32[]{:S(2)}) collective-permute-start(bf16[96,1024]{1,0:T(8,128)(2,1)S(1)} %slice_select_fusion), channel_id=1, source_target_pairs={{0,4},{1,13},{2,6},{3,15},{4,8},{5,1},{6,10},{7,3},{8,12},{9,5},{1... | collective-permute-start | bytes 589832 | tf_op jit(solution)/shard_map/ppermute | solution.py:363
  136.2 0.0 collective-permute-done.12.near
  136.2 0.9 pad_maximum_fusion
  137.1 1.9 collective-permute-start.13
  139.0 2.8 %collective-permute-done.9.fourth = bf16[96,1024]{1,0:T(8,128)(2,1)S(1)} collective-permute-done((bf16[96,1024]{1,0:T(8,128)(2,1)S(1)}, bf16[96,1024]{1,0:T(8,128)(2,1)S(1)}, u32[]{:S(2)}, u32[]{:S(2)}) %collective-permute-start.9) | collective-permute-done | bytes 196640 | tf_op jit(solution)/shard_map/ppermute | solution.py:363
  141.8 0.0 collective-permute-done.10.third
  141.8 0.9 pad_maximum_fusion.1
  142.7 3.0 %collective-permute-start.11 = (bf16[288,1024]{1,0:T(8,128)(2,1)}, bf16[288,1024]{1,0:T(8,128)(2,1)}, u32[]{:S(2)}, u32[]{:S(2)}) collective-permute-start(bf16[288,1024]{1,0:T(8,128)(2,1)} %pad_maximum_fusion.1), channel_id=1, source_target_pairs={{0,1},{1,0},{2,3},{3,2},{4,5},{5,4},{6,7},{7,6},{8,9},{9,8},{10,11... | collective-permute-start | bytes 1769480 | tf_op jit(solution)/shard_map/ppermute | solution.py:406
  145.7 0.1 stack.65
  145.8 0.1 add_bitcast_fusion
  145.9 0.0 collective-permute-done.13.swapped_pair
  145.9 0.0 copy-done
  146.0 2.8 %project_out_early.1.filled = bf16[768,896]{1,0:T(8,128)(2,1)} custom-call(s32[2,8]{1,0:T(2,128)S(1)} %pad_add_fusion.places, bf16[192,1024]{1,0:T(8,128)(2,1)S(1)} %hidden_units.1.own, bf16[192,1024]{1,0:T(8,128)(2,1)S(1)} %collective-permute-done.12.near, bf16[192,1024]{1,0:T(8,128)(2,1)S(1)} %collective-permute-done.8.far, ...), custom_call_target="tpu_custom_call" | custom-call | flops 1056964608 | bytes 3000000 | tf_op jit(solution)/shard_map/project_out_early/pallas_call | solution.py:421
  148.8 0.0 collective-permute-done.11.swapped
  148.8 2.5 %project_out_late.1 = bf16[768,896]{1,0:T(8,128)(2,1)} custom-call(s32[2,8]{1,0:T(2,128)S(1)} %pad_add_fusion.places, bf16[96,1024]{1,0:T(8,128)(2,1)S(1)} %collective-permute-done.9.fourth, bf16[288,1024]{1,0:T(8,128)(2,1)} %collective-permute-done.11.swapped, bf16[448,1024]{1,0:T(8,128)(2,1)S(1)} %bitcast.34, ...), custom_call_target="tpu_custom_call", output_to_operand_aliasing={{}: (4, {})} | custom-call | flops 352321536 | bytes 3000000 | tf_op jit(solution)/shard_map/project_out_late/pallas_call | solution.py:421
  151.3 0.0 copy-start.3
  151.3 0.0 copy-start.4
  151.3 0.0 copy-start.5
  151.3 0.0 copy-start.6
  151.3 5.0 %all-to-all-start.1 = ((bf16[32,24,896]{2,1,0:T(8,128)(2,1)}), bf16[32,24,896]{2,1,0:T(8,128)(2,1)S(1)}, u32[]{:S(2)}, u32[]{:S(2)}) async-start(bf16[32,24,896]{2,1,0:T(8,128)(2,1)} %bitcast.28), calls=%async_computation.1 | async-start | bytes 2752512 | tf_op jit(solution)/shard_map/all_to_all | solution.py:437
  156.3 0.0 copy-done.3
  156.3 0.0 copy-done.4
  156.3 0.0 copy-done.5
  156.4 0.4 weigh_table.1.weigh
  156.8 35.0 %all-to-all-done.1 = bf16[32,24,896]{2,1,0:T(8,128)(2,1)S(1)} async-done(((bf16[32,24,896]{2,1,0:T(8,128)(2,1)}), bf16[32,24,896]{2,1,0:T(8,128)(2,1)S(1)}, u32[]{:S(2)}, u32[]{:S(2)}) %all-to-all-start.1) | async-done | bytes 1376288 | tf_op jit(solution)/shard_map/all_to_all | solution.py:437
  191.8 1.3 mix_rows.1
  (6 shorter events, 0.0 us)
Async XLA Ops:
  2.5 9.8 %copy-start.1 = (bf16[1,448,1024]{2,1,0:T(8,128)(2,1)S(1)}, bf16[1,448,1024]{2,1,0:T(8,128)(2,1)}, u32[]{:S(2)}) copy-start(bf16[1,448,1024]{2,1,0:T(8,128)(2,1)} %param.13) | copy-start | bytes 2752516
  2.5 12.9 %copy-start.2 = (bf16[1,448,1024]{2,1,0:T(8,128)(2,1)S(1)}, bf16[1,448,1024]{2,1,0:T(8,128)(2,1)}, u32[]{:S(2)}) copy-start(bf16[1,448,1024]{2,1,0:T(8,128)(2,1)} %param.14) | copy-start | bytes 2752516
  2.5 44.3 %all-to-all-start = ((bf16[32,24,896]{2,1,0:T(8,128)(2,1)}), bf16[32,24,896]{2,1,0:T(8,128)(2,1)S(1)}, u32[]{:S(2)}, u32[]{:S(2)}) async-start(bf16[32,24,896]{2,1,0:T(8,128)(2,1)} %bitcast.47), calls=%async_computation | async-start | bytes 2752512 | tf_op jit(solution)/shard_map/all_to_all | solution.py:291
  12.2 5.2 %collective-permute-start = (bf16[448,1024]{1,0:T(8,128)(2,1)S(1)}, bf16[448,1024]{1,0:T(8,128)(2,1)S(1)}, u32[]{:S(2)}, u32[]{:S(2)}) collective-permute-start(bf16[448,1024]{1,0:T(8,128)(2,1)S(1)} %bitcast.36), channel_id=1, source_target_pairs={{0,1},{1,0},{2,3},{3,2},{4,5},{5,4},{6,7},{7,6},{8,9},{9,8},{10,11... | collective-permute-start | bytes 2752520 | tf_op jit(solution)/shard_map/ppermute | solution.py:272
  15.4 4.4 %collective-permute-start.1 = (bf16[448,1024]{1,0:T(8,128)(2,1)S(1)}, bf16[448,1024]{1,0:T(8,128)(2,1)S(1)}, u32[]{:S(2)}, u32[]{:S(2)}) collective-permute-start(bf16[448,1024]{1,0:T(8,128)(2,1)S(1)} %bitcast.38), channel_id=1, source_target_pairs={{0,1},{1,0},{2,3},{3,2},{4,5},{5,4},{6,7},{7,6},{8,9},{9,8},{10,11... | collective-permute-start | bytes 2752520 | tf_op jit(solution)/shard_map/ppermute | solution.py:273
  46.8 6.6 %collective-permute-start.2 = (bf16[768,896]{1,0:T(8,128)(2,1)S(1)}, bf16[768,896]{1,0:T(8,128)(2,1)S(1)}, u32[]{:S(2)}, u32[]{:S(2)}) collective-permute-start(bf16[768,896]{1,0:T(8,128)(2,1)S(1)} %after_weights.1.rows), channel_id=1, source_target_pairs={{0,1},{1,0},{2,3},{3,2},{4,5},{5,4},{6,7},{7,6},{8,9},{9,8},{10,11... | collective-permute-start | bytes 4128776 | tf_op jit(solution)/shard_map/ppermute | solution.py:332
  55.0 28.1 %collective-permute-start.4 = (bf16[192,2048]{1,0:T(8,128)(2,1)S(1)}, bf16[192,2048]{1,0:T(8,128)(2,1)S(1)}, u32[]{:S(2)}, u32[]{:S(2)}) collective-permute-start(bf16[192,2048]{1,0:T(8,128)(2,1)S(1)} %project_in_third.1), channel_id=1, source_target_pairs={{0,2},{1,15},{2,4},{3,1},{4,6},{5,3},{6,8},{7,5},{8,10},{9,7},{10,... | collective-permute-start | bytes 2359304 | tf_op jit(solution)/shard_map/ppermute | solution.py:363
  67.0 16.0 %collective-permute-start.5 = (bf16[96,2048]{1,0:T(8,128)(2,1)S(1)}, bf16[96,2048]{1,0:T(8,128)(2,1)S(1)}, u32[]{:S(2)}, u32[]{:S(2)}) collective-permute-start(bf16[96,2048]{1,0:T(8,128)(2,1)S(1)} %project_in_opposite.1), channel_id=1, source_target_pairs={{0,4},{1,13},{2,6},{3,15},{4,8},{5,1},{6,10},{7,3},{8,12},{9,5},{1... | collective-permute-start | bytes 1179656 | tf_op jit(solution)/shard_map/ppermute | solution.py:363
  70.8 29.1 %collective-permute-start.3 = (bf16[192,2048]{1,0:T(8,128)(2,1)S(1)}, bf16[192,2048]{1,0:T(8,128)(2,1)S(1)}, u32[]{:S(2)}, u32[]{:S(2)}) collective-permute-start(bf16[192,2048]{1,0:T(8,128)(2,1)S(1)} %project_in_first.1), channel_id=1, source_target_pairs={{0,2},{1,15},{2,4},{3,1},{4,6},{5,3},{6,8},{7,5},{8,10},{9,7},{10,... | collective-permute-start | bytes 2359304 | tf_op jit(solution)/shard_map/ppermute | solution.py:363
  83.4 24.9 %collective-permute-start.6 = (bf16[192,2048]{1,0:T(8,128)(2,1)S(1)}, bf16[192,2048]{1,0:T(8,128)(2,1)S(1)}, u32[]{:S(2)}, u32[]{:S(2)}) collective-permute-start(bf16[192,2048]{1,0:T(8,128)(2,1)S(1)} %add_passing.1), channel_id=1, source_target_pairs={{0,4},{1,13},{2,6},{3,15},{4,8},{5,1},{6,10},{7,3},{8,12},{9,5},{1... | collective-permute-start | bytes 2359304 | tf_op jit(solution)/shard_map/ppermute | solution.py:363
  108.6 4.2 %collective-permute-start.7 = (bf16[192,2048]{1,0:T(8,128)(2,1)S(1)}, bf16[192,2048]{1,0:T(8,128)(2,1)S(1)}, u32[]{:S(2)}, u32[]{:S(2)}) collective-permute-start(bf16[192,2048]{1,0:T(8,128)(2,1)S(1)} %add_reached.1.refs_0_), channel_id=1, source_target_pairs={{0,1},{1,0},{2,3},{3,2},{4,5},{5,4},{6,7},{7,6},{8,9},{9,8},{10,11... | collective-permute-start | bytes 2359304 | tf_op jit(solution)/shard_map/ppermute | solution.py:382
  113.2 14.8 %collective-permute-start.8 = (bf16[192,1024]{1,0:T(8,128)(2,1)S(1)}, bf16[192,1024]{1,0:T(8,128)(2,1)S(1)}, u32[]{:S(2)}, u32[]{:S(2)}) collective-permute-start(bf16[192,1024]{1,0:T(8,128)(2,1)S(1)} %hidden_units.1.own), channel_id=1, source_target_pairs={{0,4},{1,13},{2,6},{3,15},{4,8},{5,1},{6,10},{7,3},{8,12},{9,5},{1... | collective-permute-start | bytes 1179656 | tf_op jit(solution)/shard_map/ppermute | solution.py:363
  119.1 17.0 %collective-permute-start.12 = (bf16[192,1024]{1,0:T(8,128)(2,1)S(1)}, bf16[192,1024]{1,0:T(8,128)(2,1)S(1)}, u32[]{:S(2)}, u32[]{:S(2)}) collective-permute-start(bf16[192,1024]{1,0:T(8,128)(2,1)S(1)} %hidden_units.1.own), channel_id=1, source_target_pairs={{0,2},{1,15},{2,4},{3,1},{4,6},{5,3},{6,8},{7,5},{8,10},{9,7},{10,... | collective-permute-start | bytes 1179656 | tf_op jit(solution)/shard_map/ppermute | solution.py:363
  128.0 13.8 %collective-permute-start.10 = (bf16[192,1024]{1,0:T(8,128)(2,1)S(1)}, bf16[192,1024]{1,0:T(8,128)(2,1)S(1)}, u32[]{:S(2)}, u32[]{:S(2)}) collective-permute-start(bf16[192,1024]{1,0:T(8,128)(2,1)S(1)} %collective-permute-done.8.far), channel_id=1, source_target_pairs={{0,2},{1,15},{2,4},{3,1},{4,6},{5,3},{6,8},{7,5},{8,10},{9,7},{10,... | collective-permute-start | bytes 1179656 | tf_op jit(solution)/shard_map/ppermute | solution.py:363
  131.2 14.7 %copy-start = (bf16[1,1024,448]{1,2,0:T(8,128)(2,1)S(1)}, bf16[1,1024,448]{1,2,0:T(8,128)(2,1)}, u32[]{:S(2)}) copy-start(bf16[1,1024,448]{1,2,0:T(8,128)(2,1)} %param.15) | copy-start | bytes 2752516
  131.3 10.5 %collective-permute-start.9 = (bf16[96,1024]{1,0:T(8,128)(2,1)S(1)}, bf16[96,1024]{1,0:T(8,128)(2,1)S(1)}, u32[]{:S(2)}, u32[]{:S(2)}) collective-permute-start(bf16[96,1024]{1,0:T(8,128)(2,1)S(1)} %slice_select_fusion), channel_id=1, source_target_pairs={{0,4},{1,13},{2,6},{3,15},{4,8},{5,1},{6,10},{7,3},{8,12},{9,5},{1... | collective-permute-start | bytes 589832 | tf_op jit(solution)/shard_map/ppermute | solution.py:363
  137.1 8.8 %collective-permute-start.13 = (bf16[384,1024]{1,0:T(8,128)(2,1)}, bf16[384,1024]{1,0:T(8,128)(2,1)S(1)}, u32[]{:S(2)}, u32[]{:S(2)}) collective-permute-start(bf16[384,1024]{1,0:T(8,128)(2,1)} %pad_maximum_fusion), channel_id=1, source_target_pairs={{0,1},{1,0},{2,3},{3,2},{4,5},{5,4},{6,7},{7,6},{8,9},{9,8},{10,11... | collective-permute-start | bytes 2359304 | tf_op jit(solution)/shard_map/ppermute | solution.py:405
  142.7 6.1 %collective-permute-start.11 = (bf16[288,1024]{1,0:T(8,128)(2,1)}, bf16[288,1024]{1,0:T(8,128)(2,1)}, u32[]{:S(2)}, u32[]{:S(2)}) collective-permute-start(bf16[288,1024]{1,0:T(8,128)(2,1)} %pad_maximum_fusion.1), channel_id=1, source_target_pairs={{0,1},{1,0},{2,3},{3,2},{4,5},{5,4},{6,7},{7,6},{8,9},{9,8},{10,11... | collective-permute-start | bytes 1769480 | tf_op jit(solution)/shard_map/ppermute | solution.py:406
  151.3 5.1 %copy-start.3 = (s32[128,8]{0,1:T(8,128)S(1)}, s32[128,8]{0,1:T(8,128)}, u32[]{:S(2)}) copy-start(s32[128,8]{0,1:T(8,128)} %param.9) | copy-start | bytes 12292
  151.3 5.1 %copy-start.4 = (s32[128,8]{0,1:T(8,128)S(1)}, s32[128,8]{0,1:T(8,128)}, u32[]{:S(2)}) copy-start(s32[128,8]{0,1:T(8,128)} %param.10) | copy-start | bytes 12292
  151.3 5.1 %copy-start.5 = (s32[32]{0:T(128)S(1)}, s32[32]{0:T(128)}, u32[]{:S(2)}) copy-start(s32[32]{0:T(128)} %param.11) | copy-start | bytes 388
  151.3 5.1 %copy-start.6 = (s32[32]{0:T(128)S(1)}, s32[32]{0:T(128)}, u32[]{:S(2)}) copy-start(s32[32]{0:T(128)} %param.12) | copy-start | bytes 388
  151.3 40.5 %all-to-all-start.1 = ((bf16[32,24,896]{2,1,0:T(8,128)(2,1)}), bf16[32,24,896]{2,1,0:T(8,128)(2,1)S(1)}, u32[]{:S(2)}, u32[]{:S(2)}) async-start(bf16[32,24,896]{2,1,0:T(8,128)(2,1)} %bitcast.28), calls=%async_computation.1 | async-start | bytes 2752512 | tf_op jit(solution)/shard_map/all_to_all | solution.py:437
